TPU v7x, 512 devices: a whole 4x8x8 slice. The times are simulated.
512 devices in a mesh: row: 8 (over y_lo, x), col: 8 (over y_hi, core), dep: 8 (over z).
Axes of the slice: x: 4, y: 8 (y_hi: 4, y_lo: 2; y = y_hi * 2 + y_lo), z: 8, core: 2. Of those that a mesh axis runs over, the one named last changes fastest.
Arguments:
- tokens: bfloat16 [512, 12288], P(('col', 'dep'), 'row'), may hold values from -6 to 6
- grad_out: bfloat16 [512, 12288], P(('col', 'dep'), 'row'), may hold values from -6 to 6
- w_in: bfloat16 [12288, 24576], P('row', ('col', 'dep')), may hold values from -0.0546875 to 0.0546875
- w_out: bfloat16 [24576, 12288], P(('col', 'dep'), 'row'), may hold values from -0.0390625 to 0.0390625
Outputs:
- grad_in: bfloat16 [512, 12288], P(('col', 'dep'), 'row')
- grad_w_in: bfloat16 [12288, 24576], P('row', ('col', 'dep'))
- grad_w_out: bfloat16 [24576, 12288], P(('col', 'dep'), 'row')
All inputs are finite; a program needn't handle non-finite values.
Results may differ from a plain program's by a relative error of at most 0.005.
Values may be sent and summed in bfloat16 or wider, within the bound.
No kernel may reach another device: no remote copies, remote signals or barrier semaphores. Data moves between devices by JAX's collectives and lax.ppermute only.
A program may use at most 64 MiB of HBM per device.

v0:
```python
import math

import jax
import jax.numpy as jnp
from jax import lax
from jax.sharding import PartitionSpec as P

coef = 0.7978845608


def gelu_value(h):
    u = coef * (h + 0.044715 * h * h * h)
    return 0.5 * h * (1.0 + jnp.tanh(u))


def gelu_slope(h):
    t = jnp.tanh(coef * (h + 0.044715 * h * h * h))
    return 0.5 * (1.0 + t) + 0.5 * h * (1.0 - t * t) * coef * (1.0 + 0.134145 * h * h)


def hidden_pair(pre, back):
    return (gelu_value(pre).astype(jnp.bfloat16), (back * gelu_slope(pre)).astype(jnp.bfloat16))


def shards(tokens, grad_out, w_in, w_out):
    x_all, dy_all = (
        lax.all_gather(tokens, ("col", "dep"), axis=0, tiled=True),
        lax.all_gather(grad_out, ("col", "dep"), axis=0, tiled=True),
    )
    pre_part = jnp.dot(x_all, w_in, preferred_element_type=jnp.float32)
    back_part = lax.dot_general(
        dy_all, w_out, (((1,), (1,)), ((), ())), preferred_element_type=jnp.float32
    )
    pre, back = lax.psum((pre_part, back_part), "row")
    act, grad_hidden = hidden_pair(pre, back)
    factor = 1.0 / math.sqrt(x_all.shape[0])
    grad_w_out = lax.dot_general(
        act, dy_all, (((0,), (0,)), ((), ())), preferred_element_type=jnp.float32
    )
    grad_w_in = lax.dot_general(
        x_all, grad_hidden, (((0,), (0,)), ((), ())), preferred_element_type=jnp.float32
    )
    input_part = lax.dot_general(
        grad_hidden, w_in, (((1,), (1,)), ((), ())), preferred_element_type=jnp.float32
    )
    grad_in = lax.psum_scatter(input_part, ("col", "dep"), scatter_dimension=0, tiled=True)
    return (
        grad_in.astype(jnp.bfloat16),
        (grad_w_in * factor).astype(jnp.bfloat16),
        (grad_w_out * factor).astype(jnp.bfloat16),
    )


def solution(mesh):
    placed = (
        P(("col", "dep"), "row"),
        P(("col", "dep"), "row"),
        P("row", ("col", "dep")),
        P(("col", "dep"), "row"),
    )
    return jax.shard_map(
        shards,
        mesh=mesh,
        in_specs=placed,
        out_specs=(P(("col", "dep"), "row"), P("row", ("col", "dep")), P(("col", "dep"), "row")),
        check_vma=False,
    )
```

profile of v0, /device:TPU:6, one launch (start us, length us, event | category | flops | bytes accessed | tf_op | source)
XLA Modules:
  0.0 439.8 jit_solution(4565438544735539342)
XLA Ops:
  7.2 0.0 copy-start
  7.2 0.0 all-gather.3.cloned.1.call-start
  7.2 0.7 all-gather.3.cloned.1.call-update
  7.9 0.0 all-gather.5.cloned.1.call-start
  8.0 0.7 all-gather.5.cloned.1.call-update
  8.7 0.0 all-reduce.3.cloned.1.call-start
  8.7 90.9 %all-gather.3.cloned.1.call-done = bf16[512,1536]{1,0:T(8,128)(2,1)} async-done(((bf16[8,1536]{1,0:T(8,128)(2,1)}), bf16[512,1536]{1,0:T(8,128)(2,1)}) %all-gather.3.cloned.1.call-update) | async-done | bytes 1572880 | tf_op jit(solution)/shard_map/all_gather | solution.py:28
  99.6 3.6 fusion.18
  103.2 79.6 %all-gather.5.cloned.1.call-done = bf16[512,1536]{1,0:T(8,128)(2,1)} async-done(((bf16[8,1536]{1,0:T(8,128)(2,1)}), bf16[512,1536]{1,0:T(8,128)(2,1)}) %all-gather.5.cloned.1.call-update) | async-done | bytes 1572880 | tf_op jit(solution)/shard_map/all_gather | solution.py:27
  182.8 0.0 copy-done
  182.8 3.3 fusion.19
  186.1 0.0 all-reduce.3.cloned.1.call-update
  186.1 0.0 reduce-scatter.2.cloned.1.call-start
  186.2 85.3 %all-reduce.3.cloned.1.call-done = (f32[512,384]{1,0:T(8,128)}, f32[512,384]{1,0:T(8,128)}) async-done(((f32[512,384]{1,0:T(8,128)}, f32[512,384]{1,0:T(8,128)}), (f32[512,384]{1,0:T(8,128)}, f32[512,384]{1,0:T(8,128)})) %all-reduce.3.cloned.1.call-update) | async-done | bytes 1572880 | tf_op jit(solution)/shard_map/psum | solution.py:34
  271.4 1.9 fusion.9
  273.3 2.6 fusion.20
  276.0 0.0 reduce-scatter.2.cloned.1.call-update
  276.0 2.2 fusion.2
  278.2 0.0 copy-start.1
  278.2 1.4 copy.7
  279.6 0.0 copy-done.1
  279.6 3.3 fusion.1
  282.9 148.9 %reduce-scatter.2.cloned.1.call-done = f32[8,1536]{1,0:T(8,128)} async-done(((f32[512,1536]{1,0:T(8,128)}), f32[8,1536]{1,0:T(8,128)}) %reduce-scatter.2.cloned.1.call-update) | async-done | bytes 49168 | tf_op jit(solution)/shard_map/reduce_scatter | solution.py:46
  431.8 1.4 convert_element_type.19
Async XLA Ops:
  7.2 175.7 %copy-start = (bf16[1536,384]{1,0:T(8,128)(2,1)S(1)}, bf16[1536,384]{1,0:T(8,128)(2,1)}, u32[]{:S(2)}) copy-start(bf16[1536,384]{1,0:T(8,128)(2,1)} %param.6) | copy-start | bytes 3538948
  7.2 92.5 %all-gather.3.cloned.1.call-start = ((), (), s32[]{:S(2)}) async-start(), calls=%async_computation.1 | async-start | bytes 1597440 | tf_op jit(solution)/shard_map/all_gather | solution.py:28
  7.9 174.9 %all-gather.5.cloned.1.call-start = ((), (), s32[]{:S(2)}) async-start(), calls=%async_computation.2 | async-start | bytes 1597440 | tf_op jit(solution)/shard_map/all_gather | solution.py:27
  8.7 262.8 %all-reduce.3.cloned.1.call-start = ((), (), s32[]{:S(2)}) async-start(), calls=%async_computation.4 | async-start | bytes 3145728 | tf_op jit(solution)/shard_map/psum | solution.py:34
  186.1 245.7 %reduce-scatter.2.cloned.1.call-start = ((), (), s32[]{:S(2)}) async-start(), calls=%async_computation.3 | async-start | bytes 3194880 | tf_op jit(solution)/shard_map/reduce_scatter | solution.py:46
  278.2 1.4 copy-start.1
Sparse Core Ops, SparseCore 0:
  11.3 88.2 all-gather.2
  103.0 79.8 all-gather.4
  186.4 84.9 all-reduce.2
  276.1 155.6 reduce-scatter.1
where the time goes:
time: 440 us
  waiting for transfers between devices  406 us (92%)
  matrix products  15 us (3%)
  between operations  13.8 us (3%)
    reduce_scatter x1, waiting for transfers between devices, shards(): lax.psum_scatter(input_part, ('col', 'dep'), scatter_dimension=0, tiled=T...  149 us
    all_gather x1, waiting for transfers between devices, shards(): lax.all_gather(grad_out, ('col', 'dep'), axis=0, tiled=True)  90.9 us
    psum x1, waiting for transfers between devices, shards(): pre, back = lax.psum((pre_part, back_part), 'row')  85.3 us
    all_gather x1, waiting for transfers between devices, shards(): lax.all_gather(tokens, ('col', 'dep'), axis=0, tiled=True)  79.6 us
  transfers between devices with their start and end apart: 4, of which 4 were waited for; matrix products, arithmetic and copies ran while one was open for 2% of the time, Pallas kernels for 0%

commit v1 on v0

v1 whole, which is shorter than its diff:
```python
import math

import jax
import jax.numpy as jnp
from jax import lax
from jax.sharding import Mesh, PartitionSpec as P

coef = 0.7978845608
ROWS = ("y_lo", "x")
CHIPS = ("y_hi", "dep")


def gelu_value(h):
    u = coef * (h + 0.044715 * h * h * h)
    return 0.5 * h * (1.0 + jnp.tanh(u))


def gelu_slope(h):
    t = jnp.tanh(coef * (h + 0.044715 * h * h * h))
    return 0.5 * (1.0 + t) + 0.5 * h * (1.0 - t * t) * coef * (1.0 + 0.134145 * h * h)


def dot(a, b, dims):
    return lax.dot_general(a, b, ((dims[:1], dims[1:]), ((), ())), preferred_element_type=jnp.float32)


def spread(block, axes):
    n = lax.axis_size(axes)
    return lax.all_to_all(jnp.broadcast_to(block[None], (n,) + block.shape), axes, 0, 0, tiled=True)


def swap(block):
    return lax.ppermute(block, "core", [(0, 1), (1, 0)])


def shards(tokens, grad_out, w_in, w_out):
    bf16, f32 = jnp.bfloat16, jnp.float32
    width, hidden = w_in.shape
    own = spread(jnp.concatenate([tokens, grad_out], axis=1), CHIPS).reshape(-1, 2 * width)
    half = own.shape[0]
    other = swap(own)

    def partials(block):
        pre = dot(block[:, :width], w_in, (1, 0))
        back = dot(block[:, width:], w_out, (1, 1))
        return jnp.concatenate([pre, back], axis=1).astype(bf16)

    part = jnp.concatenate([partials(own), partials(other)], axis=0)
    n = lax.axis_size(ROWS)
    part = lax.all_to_all(part.reshape(n, -1, 2 * hidden), ROWS, 0, 0, tiled=True)
    total = jnp.sum(part.astype(f32), axis=0)
    pre, back = total[:, :hidden], total[:, hidden:]
    pair = jnp.concatenate([gelu_value(pre).astype(bf16), (back * gelu_slope(pre)).astype(bf16)], axis=1)
    pair = spread(pair, ROWS).reshape(2 * half, 2 * hidden)
    act, grad_hidden = pair[:, :hidden], pair[:, hidden:]

    sent = swap(dot(grad_hidden[half:], w_in, (1, 1)).astype(bf16))
    factor = 1.0 / math.sqrt(2 * half)
    x_all = jnp.concatenate([own[:, :width], other[:, :width]], axis=0)
    dy_all = jnp.concatenate([own[:, width:], other[:, width:]], axis=0)
    grad_w_in = dot(x_all, grad_hidden, (0, 0))
    grad_w_out = dot(act, dy_all, (0, 0))
    input_part = (dot(grad_hidden[:half], w_in, (1, 1)) + sent.astype(f32)).astype(bf16)
    n = lax.axis_size(CHIPS)
    input_part = lax.all_to_all(input_part.reshape(n, -1, width), CHIPS, 0, 0, tiled=True)
    grad_in = jnp.sum(input_part.astype(f32), axis=0)
    return (
        grad_in.astype(bf16),
        (grad_w_in * factor).astype(bf16),
        (grad_w_out * factor).astype(bf16),
    )


def solution(mesh):
    rows, cols, deps = mesh.devices.shape
    fine = Mesh(
        mesh.devices.reshape(2, rows // 2, cols // 2, 2, deps), ("y_lo", "x", "y_hi", "core", "dep")
    )
    blocks = ("y_hi", "core", "dep")
    placed = (P(blocks, ROWS), P(blocks, ROWS), P(ROWS, blocks), P(blocks, ROWS))
    return jax.shard_map(
        shards,
        mesh=fine,
        in_specs=placed,
        out_specs=(P(blocks, ROWS), P(ROWS, blocks), P(blocks, ROWS)),
        check_vma=False,
    )
```

time: 440 us -> 142 us (0.32)
  the two profiles are of different devices: /device:TPU:6 before, /device:TPU:64 now
where the time goes in v1:
time: 142 us
  blocking collectives  89.8 us (63%)
  waiting for transfers between devices  24.2 us (17%)
  starting transfers between devices  13.7 us (10%)
  matrix products  8.26 us (6%)
  local copies, waits for them, and re-layouts  3.31 us (2%)
  other arithmetic  1.84 us (1%)
    all_to_all x2, blocking collectives, spread(): lax.all_to_all(jnp.broadcast_to(block[None], (n,) + block.shape), axes, 0...  72.6 us
    all_to_all x1, waiting for transfers between devices, shards(): lax.all_to_all(input_part.reshape(n, -1, width), CHIPS, 0, 0, tiled=True)  19.8 us
    all_to_all x1, blocking collectives, shards(): lax.all_to_all(part.reshape(n, -1, 2 * hidden), ROWS, 0, 0, tiled=True)  17.2 us
    all_to_all x1, starting transfers between devices, shards(): lax.all_to_all(input_part.reshape(n, -1, width), CHIPS, 0, 0, tiled=True)  9.86 us
    dot_general x8, matrix products, dot(): lax.dot_general(a, b, ((dims[:1], dims[1:]), ((), ())), preferred_element...  8.26 us
    ppermute x2, waiting for transfers between devices, swap(): return lax.ppermute(block, 'core', [(0, 1), (1, 0)])  4.44 us
    ppermute x2, starting transfers between devices, swap(): return lax.ppermute(block, 'core', [(0, 1), (1, 0)])  3.83 us
    unnamed x12, local copies, waits for them, and re-layouts  2.89 us
  transfers between devices with their start and end apart: 3, of which 3 were waited for; matrix products, arithmetic and copies ran while one was open for 4% of the time, Pallas kernels for 0%

profile of v1, /device:TPU:64, one launch (start us, length us, event | category | flops | bytes accessed | tf_op | source)
XLA Modules:
  0.0 141.9 jit_solution(5711781744434389397)
XLA Ops:
  0.6 0.0 copy-start
  0.6 0.9 pad_maximum_fusion.1
  1.5 0.2 broadcast_in_dim.4
  1.7 0.0 copy-start.5
  1.7 57.6 %all_to_all.20 = bf16[32,8,3072]{2,1,0:T(8,128)(2,1)S(1)} all-to-all(bf16[32,8,3072]{2,1,0:T(8,128)(2,1)S(1)} %broadcast_in_dim.4), channel_id=1, replica_groups=mesh['y_lo'=2,'x'=4,'y_hi'=4,'core'=2,'dep'=8] {'y_hi','dep'}, dimensions={0} | all-to-all | bytes 3145728 | tf_op jit(solution)/shard_map/all_to_all | solution.py:29
  59.3 1.9 %collective-permute-start = (bf16[256,3072]{1,0:T(8,128)(2,1)S(1)}, bf16[256,3072]{1,0:T(8,128)(2,1)S(1)}, u32[]{:S(2)}, u32[]{:S(2)}) collective-permute-start(bf16[256,3072]{1,0:T(8,128)(2,1)S(1)} %bitcast.11), channel_id=1, source_target_pairs={{0,8},{8,0},{1,9},{9,1},{2,10},{10,2},{3,11},{11,3},{4,12},{12,4},... | collective-permute-start | bytes 4718600 | tf_op jit(solution)/shard_map/ppermute | solution.py:33
  61.2 0.0 copy-done.5
  61.2 0.6 convolution_convert_fusion.3
  61.8 0.0 copy-done
  61.8 0.6 convolution_convert_fusion.4
  62.4 2.2 %collective-permute-done = bf16[256,3072]{1,0:T(8,128)(2,1)S(1)} collective-permute-done((bf16[256,3072]{1,0:T(8,128)(2,1)S(1)}, bf16[256,3072]{1,0:T(8,128)(2,1)S(1)}, u32[]{:S(2)}, u32[]{:S(2)}) %collective-permute-start) | collective-permute-done | bytes 1572896 | tf_op jit(solution)/shard_map/ppermute | solution.py:33
  64.5 0.0 copy-start.3
  64.6 0.6 convolution_convert_fusion.1
  65.1 0.6 copy-done.3
  65.7 0.6 convolution_convert_fusion.2
  66.3 0.1 maximum_maximum_fusion
  66.3 17.2 %all_to_all.21 = bf16[8,64,768]{2,1,0:T(8,128)(2,1)S(1)} all-to-all(bf16[8,64,768]{2,1,0:T(8,128)(2,1)S(1)} %bitcast.15), channel_id=1, replica_groups=mesh['y_lo'=2,'x'=4,'y_hi'=4,'core'=2,'dep'=8] {'y_lo','x'}, dimensions={0} | all-to-all | bytes 1572864 | tf_op jit(solution)/shard_map/all_to_all | solution.py:50
  83.6 0.1 convert_reduce_fusion
  83.7 0.1 multiply_convert_fusion
  83.8 0.1 broadcast_in_dim.5
  83.8 15.0 %all_to_all.22 = bf16[8,64,768]{2,1,0:T(8,128)(2,1)S(1)} all-to-all(bf16[8,64,768]{2,1,0:T(8,128)(2,1)S(1)} %broadcast_in_dim.5), channel_id=1, replica_groups=mesh['y_lo'=2,'x'=4,'y_hi'=4,'core'=2,'dep'=8] {'y_lo','x'}, dimensions={0} | all-to-all | bytes 1572864 | tf_op jit(solution)/shard_map/all_to_all | solution.py:29
  98.8 0.0 copy-start.1
  98.8 0.6 convolution_convert_fusion
  99.5 1.9 %collective-permute-start.1 = (bf16[256,1536]{1,0:T(8,128)(2,1)S(1)}, bf16[256,1536]{1,0:T(8,128)(2,1)S(1)}, u32[]{:S(2)}, u32[]{:S(2)}) collective-permute-start(bf16[256,1536]{1,0:T(8,128)(2,1)S(1)} %convolution_convert_fusion), channel_id=1, source_target_pairs={{0,8},{8,0},{1,9},{9,1},{2,10},{10,2},{3,11},{11,3},{4,12},{12,4},... | collective-permute-start | bytes 2359304 | tf_op jit(solution)/shard_map/ppermute | solution.py:33
  101.4 2.3 %collective-permute-done.1 = bf16[256,1536]{1,0:T(8,128)(2,1)S(1)} collective-permute-done((bf16[256,1536]{1,0:T(8,128)(2,1)S(1)}, bf16[256,1536]{1,0:T(8,128)(2,1)S(1)}, u32[]{:S(2)}, u32[]{:S(2)}) %collective-permute-start.1) | collective-permute-done | bytes 786464 | tf_op jit(solution)/shard_map/ppermute | solution.py:33
  103.6 0.0 copy-done.1
  103.6 1.5 %fusion.8 = bf16[32,8,1536]{2,1,0:T(8,128)(2,1)} fusion(bf16[256,1536]{1,0:T(8,128)(2,1)S(1)} %collective-permute-done.1, bf16[1536,384]{1,0:T(8,128)(2,1)S(1)} %copy-done, bf16[512,768]{1,0:T(8,128)(2,1)S(1)} %bitcast.17), kind=kOutput, calls=%fused_computation.17 | convolution fusion | flops 303169536 | bytes 2949120 | tf_op jit(solution)/shard_map/dot_general | solution.py:24
  105.1 9.9 %all-to-all-start.3 = ((bf16[32,8,1536]{2,1,0:T(8,128)(2,1)}), bf16[32,8,1536]{2,1,0:T(8,128)(2,1)S(1)}, u32[]{:S(2)}, u32[]{:S(2)}) async-start(bf16[32,8,1536]{2,1,0:T(8,128)(2,1)} %fusion.8), calls=%async_computation.3 | async-start | bytes 1572864 | tf_op jit(solution)/shard_map/all_to_all | solution.py:65
  115.0 0.0 copy-start.4
  115.0 0.1 fusion.29
  115.1 1.3 copy-done.4
  116.4 0.0 copy-start.2
  116.4 0.1 fusion.30
  116.5 1.0 copy-done.2
  117.6 1.8 %fusion.1 = bf16[384,1536]{1,0:T(8,128)(2,1)} fusion(bf16[256,1536]{1,0:T(8,128)(2,1)S(1)} %get-tuple-element.5, bf16[256,1536]{1,0:T(8,128)(2,1)S(1)} %get-tuple-element.3, bf16[512,768]{1,0:T(8,128)(2,1)S(1)} %bitcast.18), kind=kOutput, calls=%fused_computation.3 | convolution fusion | flops 608305152 | bytes 3145728 | tf_op jit(solution)/shard_map/dot_general | solution.py:24
  119.4 2.0 %fusion = bf16[1536,384]{1,0:T(8,128)(2,1)} fusion(bf16[256,1536]{1,0:T(8,128)(2,1)S(1)} %get-tuple-element.6, bf16[256,1536]{1,0:T(8,128)(2,1)S(1)} %get-tuple-element.4, bf16[512,768]{1,0:T(8,128)(2,1)S(1)} %bitcast.19), kind=kOutput, calls=%fused_computation.2 | convolution fusion | flops 608305152 | bytes 3145728 | tf_op jit(solution)/shard_map/dot_general | solution.py:24
  121.4 19.8 %all-to-all-done.3 = bf16[32,8,1536]{2,1,0:T(8,128)(2,1)S(1)} async-done(((bf16[32,8,1536]{2,1,0:T(8,128)(2,1)}), bf16[32,8,1536]{2,1,0:T(8,128)(2,1)S(1)}, u32[]{:S(2)}, u32[]{:S(2)}) %all-to-all-start.3) | async-done | bytes 786464 | tf_op jit(solution)/shard_map/all_to_all | solution.py:65
  141.2 0.7 reduce_sum.22
  (1 shorter events, 0.0 us)
Async XLA Ops:
  0.6 61.1 %copy-start = (bf16[1536,384]{1,0:T(8,128)(2,1)S(1)}, bf16[1536,384]{1,0:T(8,128)(2,1)}, u32[]{:S(2)}) copy-start(bf16[1536,384]{1,0:T(8,128)(2,1)} %param.6) | copy-start | bytes 3538948
  1.7 59.5 %copy-start.5 = (bf16[384,1536]{1,0:T(8,128)(2,1)S(1)}, bf16[384,1536]{1,0:T(8,128)(2,1)}, u32[]{:S(2)}) copy-start(bf16[384,1536]{1,0:T(8,128)(2,1)} %param.7) | copy-start | bytes 3538948
  59.3 5.3 %collective-permute-start = (bf16[256,3072]{1,0:T(8,128)(2,1)S(1)}, bf16[256,3072]{1,0:T(8,128)(2,1)S(1)}, u32[]{:S(2)}, u32[]{:S(2)}) collective-permute-start(bf16[256,3072]{1,0:T(8,128)(2,1)S(1)} %bitcast.11), channel_id=1, source_target_pairs={{0,8},{8,0},{1,9},{9,1},{2,10},{10,2},{3,11},{11,3},{4,12},{12,4},... | collective-permute-start | bytes 4718600 | tf_op jit(solution)/shard_map/ppermute | solution.py:33
  64.5 1.1 copy-start.3
  98.8 4.8 %copy-start.1 = (bf16[8,64,768]{2,1,0:T(8,128)(2,1)}, bf16[8,64,768]{2,1,0:T(8,128)(2,1)S(1)}, u32[]{:S(2)}) copy-start(bf16[8,64,768]{2,1,0:T(8,128)(2,1)S(1)} %all_to_all.22) | copy-start | bytes 2359300
  99.5 4.2 %collective-permute-start.1 = (bf16[256,1536]{1,0:T(8,128)(2,1)S(1)}, bf16[256,1536]{1,0:T(8,128)(2,1)S(1)}, u32[]{:S(2)}, u32[]{:S(2)}) collective-permute-start(bf16[256,1536]{1,0:T(8,128)(2,1)S(1)} %convolution_convert_fusion), channel_id=1, source_target_pairs={{0,8},{8,0},{1,9},{9,1},{2,10},{10,2},{3,11},{11,3},{4,12},{12,4},... | collective-permute-start | bytes 2359304 | tf_op jit(solution)/shard_map/ppermute | solution.py:33
  105.1 36.0 %all-to-all-start.3 = ((bf16[32,8,1536]{2,1,0:T(8,128)(2,1)}), bf16[32,8,1536]{2,1,0:T(8,128)(2,1)S(1)}, u32[]{:S(2)}, u32[]{:S(2)}) async-start(bf16[32,8,1536]{2,1,0:T(8,128)(2,1)} %fusion.8), calls=%async_computation.3 | async-start | bytes 1572864 | tf_op jit(solution)/shard_map/all_to_all | solution.py:65
  115.0 1.4 copy-start.4
  116.4 1.1 copy-start.2

commit v2 on v1

v2 whole, which is shorter than its diff:
```python
import math

import jax
import jax.numpy as jnp
from jax import lax
from jax.sharding import Mesh, PartitionSpec as P

coef = 0.7978845608
ROWS = ("y_lo", "x")
EVEN = ("z_hi", "y_hi")
CHIPS = ("z_lo",) + EVEN
RING = ("z_hi", "z_lo")


def gelu_value(h):
    u = coef * (h + 0.044715 * h * h * h)
    return 0.5 * h * (1.0 + jnp.tanh(u))


def gelu_slope(h):
    t = jnp.tanh(coef * (h + 0.044715 * h * h * h))
    return 0.5 * (1.0 + t) + 0.5 * h * (1.0 - t * t) * coef * (1.0 + 0.134145 * h * h)


def dot(a, b, dims):
    return lax.dot_general(a, b, ((dims[:1], dims[1:]), ((), ())), preferred_element_type=jnp.float32)


def exchange(blocks, axes):
    return lax.all_to_all(blocks, axes, 0, 0, tiled=True)


def spread(block, axes):
    n = lax.axis_size(axes)
    return exchange(jnp.broadcast_to(block[None], (n,) + block.shape), axes)


def swap(block):
    return lax.ppermute(block, "core", [(0, 1), (1, 0)])


def fetch(block, by):
    n = lax.axis_size(RING)
    return lax.ppermute(block, RING, [((i + by) % n, i) for i in range(n)])


def gather(block):
    near = spread(block, EVEN).reshape(-1, block.shape[1])
    cut = near.shape[0] // 2
    return near, jnp.concatenate([fetch(near[:cut], 1), fetch(near[cut:], -1)], axis=0)


def shards(tokens, grad_out, w_in, w_out):
    bf16, f32 = jnp.bfloat16, jnp.float32
    width, hidden = w_in.shape
    near, far = gather(jnp.concatenate([tokens, grad_out], axis=1))
    w_in, w_out = [w_in, swap(w_in)], [w_out, swap(w_out)]

    def partials(block):
        pre = [dot(block[:, :width], w, (1, 0)).astype(bf16) for w in w_in]
        back = [dot(block[:, width:], w, (1, 1)).astype(bf16) for w in w_out]
        part = jnp.concatenate(pre + back, axis=1)
        return exchange(part.reshape(lax.axis_size(ROWS), -1, 4 * hidden), ROWS)

    part = jnp.concatenate([partials(near), partials(far)], axis=1)
    total = jnp.sum(part.astype(f32), axis=0)
    pre, back = total[:, : 2 * hidden], total[:, 2 * hidden :]
    pair = jnp.concatenate([gelu_value(pre).astype(bf16), (back * gelu_slope(pre)).astype(bf16)], axis=1)
    pair = spread(pair, ROWS).reshape(lax.axis_size(ROWS), 2, -1, 4 * hidden)
    pair = jnp.swapaxes(pair, 0, 1).reshape(-1, 4 * hidden)
    act, grad_hidden = pair[:, : 2 * hidden], pair[:, 2 * hidden :]

    ordered = jnp.where(lax.axis_index("z_lo") == 0, grad_hidden, jnp.roll(grad_hidden, near.shape[0], axis=0))
    input_part = dot(ordered[:, :hidden], w_in[0], (1, 1)) + dot(ordered[:, hidden:], w_in[1], (1, 1))
    input_part = input_part.astype(bf16)
    input_part = exchange(input_part.reshape(lax.axis_size(CHIPS), -1, width), CHIPS)
    grad_in = jnp.sum(input_part.astype(f32), axis=0)

    own = jnp.concatenate([near, far], axis=0)
    other = swap(own)
    act = jnp.concatenate([act[:, :hidden], swap(act[:, hidden:])], axis=0)
    grad_hidden = jnp.concatenate([grad_hidden[:, :hidden], swap(grad_hidden[:, hidden:])], axis=0)
    x_all = jnp.concatenate([own[:, :width], other[:, :width]], axis=0)
    dy_all = jnp.concatenate([own[:, width:], other[:, width:]], axis=0)
    factor = 1.0 / math.sqrt(x_all.shape[0])
    grad_w_in = dot(x_all, grad_hidden, (0, 0))
    grad_w_out = dot(act, dy_all, (0, 0))
    return (
        grad_in.astype(bf16),
        (grad_w_in * factor).astype(bf16),
        (grad_w_out * factor).astype(bf16),
    )


def solution(mesh):
    rows, cols, deps = mesh.devices.shape
    fine = Mesh(
        mesh.devices.reshape(2, rows // 2, cols // 2, 2, deps // 2, 2),
        ("y_lo", "x", "y_hi", "core", "z_hi", "z_lo"),
    )
    blocks = ("y_hi", "core", "z_hi", "z_lo")
    placed = (P(blocks, ROWS), P(blocks, ROWS), P(ROWS, blocks), P(blocks, ROWS))
    return jax.shard_map(
        shards,
        mesh=fine,
        in_specs=placed,
        out_specs=(P(blocks, ROWS), P(ROWS, blocks), P(blocks, ROWS)),
        check_vma=False,
    )
```

time: 142 us -> 136 us (0.958)
  the two profiles are of different devices: /device:TPU:64 before, /device:TPU:10 now
where the time goes in v2:
time: 136 us; the launch traced here: 135 us
  starting transfers between devices  52.7 us (39%)
  waiting for transfers between devices  40 us (29%)
  matrix products  14.6 us (11%)
  blocking collectives  11.6 us (9%)
  local copies, waits for them, and re-layouts  8.12 us (6%)
  other arithmetic  6.72 us (5%)
    all_to_all x4, waiting for transfers between devices, exchange(): return lax.all_to_all(blocks, axes, 0, 0, tiled=True)  40 us
    all_to_all x4, starting transfers between devices, exchange(): return lax.all_to_all(blocks, axes, 0, 0, tiled=True)  35.1 us
    dot_general x12, matrix products, dot(): lax.dot_general(a, b, ((dims[:1], dims[1:]), ((), ())), preferred_element...  14.6 us
    all_to_all x1, blocking collectives, exchange(): return lax.all_to_all(blocks, axes, 0, 0, tiled=True)  11.6 us
    ppermute x5, starting transfers between devices, swap(): return lax.ppermute(block, 'core', [(0, 1), (1, 0)])  10.6 us
    ppermute x2, starting transfers between devices, fetch(): return lax.ppermute(block, RING, [((i + by) % n, i) for i in range(n)])  7.04 us
    slice x2, local copies, waits for them, and re-layouts, shards(): dy_all = jnp.concatenate([own[:, width:], other[:, width:]], axis=0)  2.95 us
  transfers between devices with their start and end apart: 11, of which 3 were waited for; matrix products, arithmetic and copies ran while one was open for 18% of the time, Pallas kernels for 0%

profile of v2, /device:TPU:10, one launch (start us, length us, event | category | flops | bytes accessed | tf_op | source)
XLA Modules:
  0.0 134.7 jit_solution(3070102650006317845)
XLA Ops:
  0.6 0.0 copy-start
  0.6 0.9 pad_maximum_fusion.4
  1.5 1.0 broadcast_in_dim.4
  2.5 14.8 %all-to-all-start = ((bf16[16,8,3072]{2,1,0:T(8,128)(2,1)}), bf16[16,8,3072]{2,1,0:T(8,128)(2,1)S(1)}, u32[]{:S(2)}, u32[]{:S(2)}) async-start(bf16[16,8,3072]{2,1,0:T(8,128)(2,1)} %broadcast_in_dim.4), calls=%async_computation | async-start | bytes 1572864 | tf_op jit(solution)/shard_map/all_to_all | solution.py:30
  17.2 1.9 %collective-permute-start.1 = (bf16[384,1536]{1,0:T(8,128)(2,1)}, bf16[384,1536]{1,0:T(8,128)(2,1)}, u32[]{:S(2)}, u32[]{:S(2)}) collective-permute-start(bf16[384,1536]{1,0:T(8,128)(2,1)} %param.7), channel_id=1, source_target_pairs={{0,8},{8,0},{1,9},{9,1},{2,10},{10,2},{3,11},{11,3},{4,12},{12,4},... | collective-permute-start | bytes 3538952 | tf_op jit(solution)/shard_map/ppermute | solution.py:39
  19.2 0.0 copy-done
  19.2 2.4 %collective-permute-start = (bf16[1536,384]{1,0:T(8,128)(2,1)S(1)}, bf16[1536,384]{1,0:T(8,128)(2,1)S(1)}, u32[]{:S(2)}, u32[]{:S(2)}) collective-permute-start(bf16[1536,384]{1,0:T(8,128)(2,1)S(1)} %copy-done), channel_id=1, source_target_pairs={{0,8},{8,0},{1,9},{9,1},{2,10},{10,2},{3,11},{11,3},{4,12},{12,4},... | collective-permute-start | bytes 3538952 | tf_op jit(solution)/shard_map/ppermute | solution.py:39
  21.6 20.6 %all-to-all-done = bf16[16,8,3072]{2,1,0:T(8,128)(2,1)S(1)} async-done(((bf16[16,8,3072]{2,1,0:T(8,128)(2,1)}), bf16[16,8,3072]{2,1,0:T(8,128)(2,1)S(1)}, u32[]{:S(2)}, u32[]{:S(2)}) %all-to-all-start) | async-done | bytes 786464 | tf_op jit(solution)/shard_map/all_to_all | solution.py:30
  42.2 0.9 slice_bitcast_fusion
  43.1 3.4 %collective-permute-start.3 = (bf16[64,3072]{1,0:T(8,128)(2,1)}, bf16[64,3072]{1,0:T(8,128)(2,1)S(1)}, u32[]{:S(2)}, u32[]{:S(2)}) collective-permute-start(bf16[64,3072]{1,0:T(8,128)(2,1)} %get-tuple-element.13), channel_id=1, source_target_pairs={{7,0},{0,1},{1,2},{2,3},{3,4},{4,5},{5,6},{6,7},{15,8},{8,9},{9,10... | collective-permute-start | bytes 1179656 | tf_op jit(solution)/shard_map/ppermute | solution.py:44
  46.5 3.7 %collective-permute-start.2 = (bf16[64,3072]{1,0:T(8,128)(2,1)}, bf16[64,3072]{1,0:T(8,128)(2,1)}, u32[]{:S(2)}, u32[]{:S(2)}) collective-permute-start(bf16[64,3072]{1,0:T(8,128)(2,1)} %get-tuple-element.14), channel_id=1, source_target_pairs={{1,0},{2,1},{3,2},{4,3},{5,4},{6,5},{7,6},{0,7},{9,8},{10,9},{11,1... | collective-permute-start | bytes 1179656 | tf_op jit(solution)/shard_map/ppermute | solution.py:44
  50.2 1.8 %convolution_convert_fusion.5 = bf16[128,384]{1,0:T(8,128)(2,1)S(1)} fusion(bf16[384,1536]{1,0:T(8,128)(2,1)} %param.7, bf16[128,3072]{1,0:T(8,128)(2,1)S(1)} %bitcast.23), kind=kOutput, calls=%fused_computation.20 | convolution fusion | flops 151044096 | bytes 1671168 | tf_op jit(solution)/shard_map/dot_general | solution.py:26
  51.9 0.4 convolution_convert_fusion.7
  52.3 0.0 collective-permute-done.1
  52.3 1.8 %convolution_convert_fusion.4 = bf16[128,384]{1,0:T(8,128)(2,1)S(1)} fusion(bf16[384,1536]{1,0:T(8,128)(2,1)} %collective-permute-done.1, bf16[128,3072]{1,0:T(8,128)(2,1)S(1)} %bitcast.25), kind=kOutput, calls=%fused_computation.19 | convolution fusion | flops 151044096 | bytes 1671168 | tf_op jit(solution)/shard_map/dot_general | solution.py:26
  54.1 0.0 collective-permute-done
  54.1 0.4 convolution_convert_fusion.6
  54.5 0.8 pad_maximum_fusion.1
  55.3 6.2 %all-to-all-start.1 = ((bf16[8,16,1536]{2,1,0:T(8,128)(2,1)}), bf16[8,16,1536]{2,1,0:T(8,128)(2,1)}, u32[]{:S(2)}, u32[]{:S(2)}) async-start(bf16[8,16,1536]{2,1,0:T(8,128)(2,1)} %bitcast.31), calls=%async_computation.1 | async-start | bytes 786432 | tf_op jit(solution)/shard_map/all_to_all | solution.py:30
  61.5 0.0 collective-permute-done.2
  61.5 1.0 constant_dynamic-update-slice_fusion.1
  62.5 0.0 collective-permute-done.3
  62.5 1.8 %convolution_convert_fusion.1 = bf16[128,384]{1,0:T(8,128)(2,1)S(1)} fusion(bf16[384,1536]{1,0:T(8,128)(2,1)} %param.7, bf16[128,3072]{1,0:T(8,128)(2,1)S(1)} %constant_dynamic-update-slice_fusion), kind=kOutput, calls=%fused_computation.16 | convolution fusion | flops 151044096 | bytes 1671168 | tf_op jit(solution)/shard_map/dot_general | solution.py:26
  64.3 0.4 convolution_convert_fusion.3
  64.7 1.8 %convolution_convert_fusion = bf16[128,384]{1,0:T(8,128)(2,1)S(1)} fusion(bf16[384,1536]{1,0:T(8,128)(2,1)} %collective-permute-done.1, bf16[128,3072]{1,0:T(8,128)(2,1)S(1)} %constant_dynamic-update-slice_fusion), kind=kOutput, calls=%fused_computation.15 | convolution fusion | flops 151044096 | bytes 1671168 | tf_op jit(solution)/shard_map/dot_general | solution.py:26
  66.5 0.4 convolution_convert_fusion.2
  66.8 0.8 pad_maximum_fusion.2
  67.6 0.0 all-to-all-done.1
  67.6 11.6 %all_to_all.25 = bf16[8,16,1536]{2,1,0:T(8,128)(2,1)S(1)} all-to-all(bf16[8,16,1536]{2,1,0:T(8,128)(2,1)} %bitcast.32), channel_id=1, replica_groups=mesh['y_lo'=2,'x'=4,'y_hi'=4,'core'=2,'z_hi'=4,'z_lo'=2] {'y_lo','x'}, dimensions={0} | all-to-all | bytes 786432 | tf_op jit(solution)/shard_map/all_to_all | solution.py:30
  79.3 1.1 convert_reduce_fusion
  80.4 0.1 multiply_convert_fusion
  80.5 0.9 broadcast_in_dim.5
  81.4 6.2 %all-to-all-start.3 = ((bf16[8,32,1536]{2,1,0:T(8,128)(2,1)}), bf16[8,32,1536]{2,1,0:T(8,128)(2,1)}, u32[]{:S(2)}, u32[]{:S(2)}) async-start(bf16[8,32,1536]{2,1,0:T(8,128)(2,1)} %broadcast_in_dim.5), calls=%async_computation.3 | async-start | bytes 1572864 | tf_op jit(solution)/shard_map/all_to_all | solution.py:30
  87.6 2.3 %pad_maximum_fusion = bf16[256,3072]{1,0:T(8,128)(2,1)} fusion(bf16[64,3072]{1,0:T(8,128)(2,1)S(1)} %collective-permute-done.3, bf16[64,3072]{1,0:T(8,128)(2,1)} %collective-permute-done.2, bf16[128,3072]{1,0:T(8,128)(2,1)S(1)} %bitcast.27), kind=kLoop, calls=%fused_computation.7 | loop fusion | flops 4718592 | bytes 3145728 | tf_op jit(solution)/shard_map/concatenate | solution.py:79
  89.9 1.9 %collective-permute-start.4 = (bf16[256,3072]{1,0:T(8,128)(2,1)}, bf16[256,3072]{1,0:T(8,128)(2,1)}, u32[]{:S(2)}, u32[]{:S(2)}) collective-permute-start(bf16[256,3072]{1,0:T(8,128)(2,1)} %pad_maximum_fusion), channel_id=1, source_target_pairs={{0,8},{8,0},{1,9},{9,1},{2,10},{10,2},{3,11},{11,3},{4,12},{12,4},... | collective-permute-start | bytes 4718600 | tf_op jit(solution)/shard_map/ppermute | solution.py:39
  91.8 3.9 %all-to-all-done.3 = bf16[8,32,1536]{2,1,0:T(8,128)(2,1)} async-done(((bf16[8,32,1536]{2,1,0:T(8,128)(2,1)}), bf16[8,32,1536]{2,1,0:T(8,128)(2,1)}, u32[]{:S(2)}, u32[]{:S(2)}) %all-to-all-start.3) | async-done | bytes 786464 | tf_op jit(solution)/shard_map/all_to_all | solution.py:30
  95.7 1.2 copy.7
  97.0 0.1 slice_select_fusion
  97.1 0.6 fusion.25
  97.7 1.5 %fusion.3 = bf16[32,8,1536]{2,1,0:T(8,128)(2,1)} fusion(f32[256,1536]{1,0:T(8,128)S(1)} %fusion.25, bf16[1536,384]{1,0:T(8,128)(2,1)S(1)} %collective-permute-done, bf16[256,768]{1,0:T(8,128)(2,1)S(1)} %slice_select_fusion), kind=kOutput, calls=%fused_computation.6 | convolution fusion | flops 302776320 | bytes 3735552 | tf_op jit(solution)/shard_map/dot_general | solution.py:26
  99.2 8.0 %all-to-all-start.4 = ((bf16[32,8,1536]{2,1,0:T(8,128)(2,1)}), bf16[32,8,1536]{2,1,0:T(8,128)(2,1)S(1)}, u32[]{:S(2)}, u32[]{:S(2)}) async-start(bf16[32,8,1536]{2,1,0:T(8,128)(2,1)} %fusion.3), calls=%async_computation.4 | async-start | bytes 1572864 | tf_op jit(solution)/shard_map/all_to_all | solution.py:30
  107.2 1.5 %fusion.36 = (bf16[256,1536]{1,0:T(8,128)(2,1)S(1)}, bf16[256,1536]{1,0:T(8,128)(2,1)S(1)}) fusion(bf16[256,3072]{1,0:T(8,128)(2,1)} %pad_maximum_fusion), kind=kLoop, calls=%fused_computation.61 | loop fusion | bytes 3145728 | tf_op jit(solution)/shard_map/slice | solution.py:84
  108.6 0.1 fusion.38
  108.7 1.9 %collective-permute-start.6 = (bf16[256,384]{1,0:T(8,128)(2,1)S(1)}, bf16[256,384]{1,0:T(8,128)(2,1)S(1)}, u32[]{:S(2)}, u32[]{:S(2)}) collective-permute-start(bf16[256,384]{1,0:T(8,128)(2,1)S(1)} %get-tuple-element.8), channel_id=1, source_target_pairs={{0,8},{8,0},{1,9},{9,1},{2,10},{10,2},{3,11},{11,3},{4,12},{12,4},... | collective-permute-start | bytes 589832 | tf_op jit(solution)/shard_map/ppermute | solution.py:39
  110.7 2.4 %collective-permute-start.5 = (bf16[256,384]{1,0:T(8,128)(2,1)S(1)}, bf16[256,384]{1,0:T(8,128)(2,1)S(1)}, u32[]{:S(2)}, u32[]{:S(2)}) collective-permute-start(bf16[256,384]{1,0:T(8,128)(2,1)S(1)} %get-tuple-element.9), channel_id=1, source_target_pairs={{0,8},{8,0},{1,9},{9,1},{2,10},{10,2},{3,11},{11,3},{4,12},{12,4},... | collective-permute-start | bytes 589832 | tf_op jit(solution)/shard_map/ppermute | solution.py:39
  113.1 0.0 collective-permute-done.4
  113.1 1.5 %fusion.37 = (bf16[256,1536]{1,0:T(8,128)(2,1)S(1)}, bf16[256,1536]{1,0:T(8,128)(2,1)S(1)}) fusion(bf16[256,3072]{1,0:T(8,128)(2,1)} %collective-permute-done.4), kind=kLoop, calls=%fused_computation.62 | loop fusion | bytes 3145728 | tf_op jit(solution)/shard_map/slice | solution.py:84
  114.6 0.0 collective-permute-done.6
  114.6 1.8 %fusion.1 = bf16[384,1536]{1,0:T(8,128)(2,1)} fusion(bf16[256,1536]{1,0:T(8,128)(2,1)S(1)} %get-tuple-element.5, bf16[256,1536]{1,0:T(8,128)(2,1)S(1)} %get-tuple-element.3, bf16[256,384]{1,0:T(8,128)(2,1)S(1)} %collective-permute-done.6, bf16[256,384]{1,0:T(8,128)(2,1)S(1)} %get-tuple-element.7), kind=kOutput, calls=%fused_computation.3 | convolution fusion | flops 609091584 | bytes 3145728 | tf_op jit(solution)/shard_map/dot_general | solution.py:26
  116.4 0.0 collective-permute-done.5
  116.4 2.0 %fusion = bf16[1536,384]{1,0:T(8,128)(2,1)} fusion(bf16[256,1536]{1,0:T(8,128)(2,1)S(1)} %get-tuple-element.6, bf16[256,1536]{1,0:T(8,128)(2,1)S(1)} %get-tuple-element.4, bf16[256,384]{1,0:T(8,128)(2,1)S(1)} %collective-permute-done.5, bf16[256,384]{1,0:T(8,128)(2,1)S(1)} %get-tuple-element.10), kind=kOutput, calls=%fused_computation.2 | convolution fusion | flops 609091584 | bytes 3145728 | tf_op jit(solution)/shard_map/dot_general | solution.py:26
  118.4 15.5 %all-to-all-done.4 = bf16[32,8,1536]{2,1,0:T(8,128)(2,1)S(1)} async-done(((bf16[32,8,1536]{2,1,0:T(8,128)(2,1)}), bf16[32,8,1536]{2,1,0:T(8,128)(2,1)S(1)}, u32[]{:S(2)}, u32[]{:S(2)}) %all-to-all-start.4) | async-done | bytes 786464 | tf_op jit(solution)/shard_map/all_to_all | solution.py:30
  134.0 0.7 reduce_sum.22
  (3 shorter events, 0.1 us)
Async XLA Ops:
  0.6 18.5 %copy-start = (bf16[1536,384]{1,0:T(8,128)(2,1)S(1)}, bf16[1536,384]{1,0:T(8,128)(2,1)}, u32[]{:S(2)}) copy-start(bf16[1536,384]{1,0:T(8,128)(2,1)} %param.6) | copy-start | bytes 3538948
  2.5 39.7 %all-to-all-start = ((bf16[16,8,3072]{2,1,0:T(8,128)(2,1)}), bf16[16,8,3072]{2,1,0:T(8,128)(2,1)S(1)}, u32[]{:S(2)}, u32[]{:S(2)}) async-start(bf16[16,8,3072]{2,1,0:T(8,128)(2,1)} %broadcast_in_dim.4), calls=%async_computation | async-start | bytes 1572864 | tf_op jit(solution)/shard_map/all_to_all | solution.py:30
  17.2 35.1 %collective-permute-start.1 = (bf16[384,1536]{1,0:T(8,128)(2,1)}, bf16[384,1536]{1,0:T(8,128)(2,1)}, u32[]{:S(2)}, u32[]{:S(2)}) collective-permute-start(bf16[384,1536]{1,0:T(8,128)(2,1)} %param.7), channel_id=1, source_target_pairs={{0,8},{8,0},{1,9},{9,1},{2,10},{10,2},{3,11},{11,3},{4,12},{12,4},... | collective-permute-start | bytes 3538952 | tf_op jit(solution)/shard_map/ppermute | solution.py:39
  19.2 34.9 %collective-permute-start = (bf16[1536,384]{1,0:T(8,128)(2,1)S(1)}, bf16[1536,384]{1,0:T(8,128)(2,1)S(1)}, u32[]{:S(2)}, u32[]{:S(2)}) collective-permute-start(bf16[1536,384]{1,0:T(8,128)(2,1)S(1)} %copy-done), channel_id=1, source_target_pairs={{0,8},{8,0},{1,9},{9,1},{2,10},{10,2},{3,11},{11,3},{4,12},{12,4},... | collective-permute-start | bytes 3538952 | tf_op jit(solution)/shard_map/ppermute | solution.py:39
  43.1 19.4 %collective-permute-start.3 = (bf16[64,3072]{1,0:T(8,128)(2,1)}, bf16[64,3072]{1,0:T(8,128)(2,1)S(1)}, u32[]{:S(2)}, u32[]{:S(2)}) collective-permute-start(bf16[64,3072]{1,0:T(8,128)(2,1)} %get-tuple-element.13), channel_id=1, source_target_pairs={{7,0},{0,1},{1,2},{2,3},{3,4},{4,5},{5,6},{6,7},{15,8},{8,9},{9,10... | collective-permute-start | bytes 1179656 | tf_op jit(solution)/shard_map/ppermute | solution.py:44
  46.5 15.0 %collective-permute-start.2 = (bf16[64,3072]{1,0:T(8,128)(2,1)}, bf16[64,3072]{1,0:T(8,128)(2,1)}, u32[]{:S(2)}, u32[]{:S(2)}) collective-permute-start(bf16[64,3072]{1,0:T(8,128)(2,1)} %get-tuple-element.14), channel_id=1, source_target_pairs={{1,0},{2,1},{3,2},{4,3},{5,4},{6,5},{7,6},{0,7},{9,8},{10,9},{11,1... | collective-permute-start | bytes 1179656 | tf_op jit(solution)/shard_map/ppermute | solution.py:44
  55.3 12.4 %all-to-all-start.1 = ((bf16[8,16,1536]{2,1,0:T(8,128)(2,1)}), bf16[8,16,1536]{2,1,0:T(8,128)(2,1)}, u32[]{:S(2)}, u32[]{:S(2)}) async-start(bf16[8,16,1536]{2,1,0:T(8,128)(2,1)} %bitcast.31), calls=%async_computation.1 | async-start | bytes 786432 | tf_op jit(solution)/shard_map/all_to_all | solution.py:30
  81.4 14.3 %all-to-all-start.3 = ((bf16[8,32,1536]{2,1,0:T(8,128)(2,1)}), bf16[8,32,1536]{2,1,0:T(8,128)(2,1)}, u32[]{:S(2)}, u32[]{:S(2)}) async-start(bf16[8,32,1536]{2,1,0:T(8,128)(2,1)} %broadcast_in_dim.5), calls=%async_computation.3 | async-start | bytes 1572864 | tf_op jit(solution)/shard_map/all_to_all | solution.py:30
  89.9 23.2 %collective-permute-start.4 = (bf16[256,3072]{1,0:T(8,128)(2,1)}, bf16[256,3072]{1,0:T(8,128)(2,1)}, u32[]{:S(2)}, u32[]{:S(2)}) collective-permute-start(bf16[256,3072]{1,0:T(8,128)(2,1)} %pad_maximum_fusion), channel_id=1, source_target_pairs={{0,8},{8,0},{1,9},{9,1},{2,10},{10,2},{3,11},{11,3},{4,12},{12,4},... | collective-permute-start | bytes 4718600 | tf_op jit(solution)/shard_map/ppermute | solution.py:39
  99.2 34.8 %all-to-all-start.4 = ((bf16[32,8,1536]{2,1,0:T(8,128)(2,1)}), bf16[32,8,1536]{2,1,0:T(8,128)(2,1)S(1)}, u32[]{:S(2)}, u32[]{:S(2)}) async-start(bf16[32,8,1536]{2,1,0:T(8,128)(2,1)} %fusion.3), calls=%async_computation.4 | async-start | bytes 1572864 | tf_op jit(solution)/shard_map/all_to_all | solution.py:30
  108.7 5.8 %collective-permute-start.6 = (bf16[256,384]{1,0:T(8,128)(2,1)S(1)}, bf16[256,384]{1,0:T(8,128)(2,1)S(1)}, u32[]{:S(2)}, u32[]{:S(2)}) collective-permute-start(bf16[256,384]{1,0:T(8,128)(2,1)S(1)} %get-tuple-element.8), channel_id=1, source_target_pairs={{0,8},{8,0},{1,9},{9,1},{2,10},{10,2},{3,11},{11,3},{4,12},{12,4},... | collective-permute-start | bytes 589832 | tf_op jit(solution)/shard_map/ppermute | solution.py:39
  110.7 5.7 %collective-permute-start.5 = (bf16[256,384]{1,0:T(8,128)(2,1)S(1)}, bf16[256,384]{1,0:T(8,128)(2,1)S(1)}, u32[]{:S(2)}, u32[]{:S(2)}) collective-permute-start(bf16[256,384]{1,0:T(8,128)(2,1)S(1)} %get-tuple-element.9), channel_id=1, source_target_pairs={{0,8},{8,0},{1,9},{9,1},{2,10},{10,2},{3,11},{11,3},{4,12},{12,4},... | collective-permute-start | bytes 589832 | tf_op jit(solution)/shard_map/ppermute | solution.py:39

commit v3 on v2

v3 whole, which is shorter than its diff:
```python
import functools
import math

import jax
import jax.numpy as jnp
from jax import lax
from jax.experimental import pallas as pl
from jax.experimental.pallas import tpu as pltpu
from jax.sharding import Mesh, PartitionSpec as P

coef = 0.7978845608
ROWS = ("y_lo", "x")
EVEN = ("z_hi", "y_far", "y_near")
CHIPS = ("z_hi", "y_far", "z_lo", "y_near")
RING = ("z_hi", "z_lo")


def gelu_value(h):
    u = coef * (h + 0.044715 * h * h * h)
    return 0.5 * h * (1.0 + jnp.tanh(u))


def gelu_slope(h):
    t = jnp.tanh(coef * (h + 0.044715 * h * h * h))
    return 0.5 * (1.0 + t) + 0.5 * h * (1.0 - t * t) * coef * (1.0 + 0.134145 * h * h)


def dot(a, b, dims):
    return lax.dot_general(a, b, ((dims[:1], dims[1:]), ((), ())), preferred_element_type=jnp.float32)


def exchange(blocks, axes):
    return lax.all_to_all(blocks, axes, 0, 0, tiled=True)


def spread(block, axes):
    n = lax.axis_size(axes)
    return exchange(jnp.broadcast_to(block[None], (n,) + block.shape), axes)


def swap(block):
    return lax.ppermute(block, "core", [(0, 1), (1, 0)])


def fetch(block, by):
    n = lax.axis_size(RING)
    return lax.ppermute(block, RING, [((i + by) % n, i) for i in range(n)])


def gather(block):
    near = spread(block, EVEN).reshape(-1, block.shape[1])
    cut = near.shape[0] // 2
    return near, [fetch(near[:cut], 1), fetch(near[cut:], -1)]


def load(weights, held, arrived):
    copies = [pltpu.make_async_copy(w, h, arrived.at[i]) for i, (w, h) in enumerate(zip(weights, held))]
    for copy in copies:
        copy.start()
    return copies


def with_weights(kernel, out_shape, blocks, weights, cost):
    vmem = pl.BlockSpec(memory_space=pltpu.VMEM)
    cut = len(weights) // 2
    others = [pltpu.with_memory_space_constraint(w, pltpu.HBM) for w in weights[cut:]]
    return pl.pallas_call(
        kernel,
        out_shape=out_shape,
        in_specs=[vmem] * len(blocks)
        + [pl.BlockSpec(memory_space=pl.ANY)] * cut
        + [pl.BlockSpec(memory_space=pltpu.HBM)] * len(others),
        out_specs=vmem,
        scratch_shapes=[pltpu.VMEM(w.shape, w.dtype) for w in weights]
        + [pltpu.SemaphoreType.DMA((len(weights),))],
        compiler_params=pltpu.CompilerParams(vmem_limit_bytes=16 * 2**20),
        cost_estimate=cost,
    )(*blocks, *weights[:cut], *others)


def products_kernel(count, *refs):
    blocks, weights, out = refs[:count], refs[count : count + 4], refs[count + 4]
    held, arrived = refs[count + 5 : count + 9], refs[count + 9]
    copies = load(weights, held, arrived)
    block = jnp.concatenate([b[...] for b in blocks], axis=0)
    width, hidden = held[0].shape
    for i, place in enumerate((0, 2, 1, 3)):
        copies[i].wait()
        if place < 2:
            part = dot(block[:, :width], held[i][...], (1, 0))
        else:
            part = dot(block[:, width:], held[i][...], (1, 1))
        out[:, place * hidden : (place + 1) * hidden] = part.astype(out.dtype)


def products(blocks, w_in, w_out, weight):
    rows, (width, hidden) = sum(b.shape[0] for b in blocks), w_in[0].shape
    return with_weights(
        functools.partial(products_kernel, len(blocks)),
        jax.ShapeDtypeStruct((rows, 4 * hidden), jnp.bfloat16),
        blocks,
        [w_in[0], w_out[0], w_in[1], w_out[1]],
        pl.CostEstimate(
            flops=8 * weight * rows * width * hidden, bytes_accessed=8 * width * hidden, transcendentals=0
        ),
    )


def input_kernel(pair, w_mine, w_other, out, mine, other, arrived):
    copies = load((w_mine, w_other), (mine, other), arrived)
    hidden = mine.shape[1]
    copies[0].wait()
    total = dot(pair[:, 2 * hidden : 3 * hidden], mine[...], (1, 1))
    copies[1].wait()
    out[...] = (total + dot(pair[:, 3 * hidden :], other[...], (1, 1))).astype(out.dtype)


def input_products(pair, w_in):
    rows, (width, hidden) = pair.shape[0], w_in[0].shape
    return with_weights(
        input_kernel,
        jax.ShapeDtypeStruct((rows, width), jnp.bfloat16),
        [pair],
        w_in,
        pl.CostEstimate(
            flops=4 * rows * width * hidden, bytes_accessed=6 * width * hidden, transcendentals=0
        ),
    )


def shards(tokens, grad_out, w_in, w_out):
    bf16, f32 = jnp.bfloat16, jnp.float32
    width, hidden = w_in.shape
    rows = lax.axis_size(ROWS)
    low = lax.axis_index("z_lo") == 0

    def by_z(near, far):
        both = jnp.where(low, near, far), jnp.where(low, far, near)
        return jnp.concatenate(both, axis=-2)

    near, far = gather(jnp.concatenate([tokens, grad_out], axis=1))
    w_in, w_out = [w_in, swap(w_in)], [w_out, swap(w_out)]
    parts = products([near], w_in, w_out, 1), products(far, w_in, w_out, 25)
    parts = [exchange(part.reshape(rows, -1, 4 * hidden), ROWS) for part in parts]
    total = by_z(*[jnp.sum(part.astype(f32), axis=0) for part in parts])
    pre, back = total[:, : 2 * hidden], total[:, 2 * hidden :]
    pair = jnp.concatenate([gelu_value(pre).astype(bf16), (back * gelu_slope(pre)).astype(bf16)], axis=1)
    pair = spread(pair, ROWS).reshape(-1, 4 * hidden)
    act, grad_hidden = pair[:, : 2 * hidden], pair[:, 2 * hidden :]

    input_part = exchange(input_products(pair, w_in).reshape(lax.axis_size(CHIPS), -1, width), CHIPS)
    grad_in = jnp.sum(input_part.astype(f32), axis=0)

    far = jnp.concatenate(far, axis=0)
    own = by_z(*[block.reshape(rows, -1, 2 * width) for block in (near, far)]).reshape(-1, 2 * width)
    other = swap(own)
    act = jnp.concatenate([act[:, :hidden], swap(act[:, hidden:])], axis=0)
    grad_hidden = jnp.concatenate([grad_hidden[:, :hidden], swap(grad_hidden[:, hidden:])], axis=0)
    x_all = jnp.concatenate([own[:, :width], other[:, :width]], axis=0)
    dy_all = jnp.concatenate([own[:, width:], other[:, width:]], axis=0)
    factor = 1.0 / math.sqrt(x_all.shape[0])
    grad_w_in = dot(x_all, grad_hidden, (0, 0))
    grad_w_out = dot(act, dy_all, (0, 0))
    return (
        grad_in.astype(bf16),
        (grad_w_in * factor).astype(bf16),
        (grad_w_out * factor).astype(bf16),
    )


def solution(mesh):
    rows, cols, deps = mesh.devices.shape
    fine = Mesh(
        mesh.devices.reshape(2, rows // 2, cols // 4, 2, 2, deps // 2, 2),
        ("y_lo", "x", "y_far", "y_near", "core", "z_hi", "z_lo"),
    )
    blocks = ("y_far", "y_near", "core", "z_hi", "z_lo")
    placed = (P(blocks, ROWS), P(blocks, ROWS), P(ROWS, blocks), P(blocks, ROWS))
    return jax.shard_map(
        shards,
        mesh=fine,
        in_specs=placed,
        out_specs=(P(blocks, ROWS), P(ROWS, blocks), P(blocks, ROWS)),
        check_vma=False,
    )
```

time: 136 us -> 129 us (0.949)
  the two profiles are of different devices: /device:TPU:10 before, /device:TPU:6 now
where the time goes in v3:
time: 129 us; the launch traced here: 127 us
  starting transfers between devices  58.4 us (45%)
  waiting for transfers between devices  40.3 us (31%)
  Pallas kernels  11.6 us (9%)
  other arithmetic  6.15 us (5%)
  local copies, waits for them, and re-layouts  5.88 us (5%)
  matrix products  3.86 us (3%)
    all_to_all x5, starting transfers between devices, exchange(): return lax.all_to_all(blocks, axes, 0, 0, tiled=True)  41.5 us
    all_to_all x5, waiting for transfers between devices, exchange(): return lax.all_to_all(blocks, axes, 0, 0, tiled=True)  39.3 us
    pallas_call x3, Pallas kernels, with_weights(): pl.pallas_call(kernel, out_shape=out_shape, in_specs=[vmem] * len(blocks)...  11.6 us
    ppermute x5, starting transfers between devices, swap(): return lax.ppermute(block, 'core', [(0, 1), (1, 0)])  10.6 us
    ppermute x2, starting transfers between devices, fetch(): return lax.ppermute(block, RING, [((i + by) % n, i) for i in range(n)])  6.26 us
    dot_general x2, matrix products, dot(): lax.dot_general(a, b, ((dims[:1], dims[1:]), ((), ())), preferred_element...  3.86 us
    slice x2, local copies, waits for them, and re-layouts, shards(): dy_all = jnp.concatenate([own[:, width:], other[:, width:]], axis=0)  2.95 us
  transfers between devices with their start and end apart: 12, of which 5 were waited for; matrix products, arithmetic and copies ran while one was open for 10% of the time, Pallas kernels for 9%

profile of v3, /device:TPU:6, one launch (start us, length us, event | category | flops | bytes accessed | tf_op | source)
XLA Modules:
  0.0 127.0 jit_solution(16480923022936519702)
XLA Ops:
  0.6 0.0 copy-start
  0.6 0.0 copy-start.1
  0.7 0.9 pad_maximum_fusion.4
  1.6 1.0 broadcast_in_dim.4
  2.5 15.7 %all-to-all-start = ((bf16[16,8,3072]{2,1,0:T(8,128)(2,1)}), bf16[16,8,3072]{2,1,0:T(8,128)(2,1)S(1)}, u32[]{:S(2)}, u32[]{:S(2)}) async-start(bf16[16,8,3072]{2,1,0:T(8,128)(2,1)} %broadcast_in_dim.4), calls=%async_computation | async-start | bytes 1572864 | tf_op jit(solution)/shard_map/all_to_all | solution.py:33
  18.2 0.0 copy-done
  18.2 1.9 %collective-permute-start = (bf16[1536,384]{1,0:T(8,128)(2,1)S(1)}, bf16[1536,384]{1,0:T(8,128)(2,1)}, u32[]{:S(2)}, u32[]{:S(2)}) collective-permute-start(bf16[1536,384]{1,0:T(8,128)(2,1)S(1)} %copy-done), channel_id=1, source_target_pairs={{0,8},{8,0},{1,9},{9,1},{2,10},{10,2},{3,11},{11,3},{4,12},{12,4},... | collective-permute-start | bytes 3538952 | tf_op jit(solution)/shard_map/ppermute | solution.py:42
  20.1 0.0 copy-done.1
  20.1 2.4 %collective-permute-start.1 = (bf16[384,1536]{1,0:T(8,128)(2,1)S(1)}, bf16[384,1536]{1,0:T(8,128)(2,1)}, u32[]{:S(2)}, u32[]{:S(2)}) collective-permute-start(bf16[384,1536]{1,0:T(8,128)(2,1)S(1)} %copy-done.1), channel_id=1, source_target_pairs={{0,8},{8,0},{1,9},{9,1},{2,10},{10,2},{3,11},{11,3},{4,12},{12,4},... | collective-permute-start | bytes 3538952 | tf_op jit(solution)/shard_map/ppermute | solution.py:42
  22.6 21.1 %all-to-all-done = bf16[16,8,3072]{2,1,0:T(8,128)(2,1)S(1)} async-done(((bf16[16,8,3072]{2,1,0:T(8,128)(2,1)}), bf16[16,8,3072]{2,1,0:T(8,128)(2,1)S(1)}, u32[]{:S(2)}, u32[]{:S(2)}) %all-to-all-start) | async-done | bytes 786464 | tf_op jit(solution)/shard_map/all_to_all | solution.py:33
  43.7 0.9 slice_bitcast_fusion
  44.6 4.3 %collective-permute-start.2 = (bf16[64,3072]{1,0:T(8,128)(2,1)}, bf16[64,3072]{1,0:T(8,128)(2,1)S(1)}, u32[]{:S(2)}, u32[]{:S(2)}) collective-permute-start(bf16[64,3072]{1,0:T(8,128)(2,1)} %get-tuple-element.14), channel_id=1, source_target_pairs={{1,0},{2,1},{3,2},{4,3},{5,4},{6,5},{7,6},{0,7},{9,8},{10,9},{11,1... | collective-permute-start | bytes 1179656 | tf_op jit(solution)/shard_map/ppermute | solution.py:47
  49.0 1.9 %collective-permute-start.3 = (bf16[64,3072]{1,0:T(8,128)(2,1)}, bf16[64,3072]{1,0:T(8,128)(2,1)}, u32[]{:S(2)}, u32[]{:S(2)}) collective-permute-start(bf16[64,3072]{1,0:T(8,128)(2,1)} %get-tuple-element.13), channel_id=1, source_target_pairs={{7,0},{0,1},{1,2},{2,3},{3,4},{4,5},{5,6},{6,7},{15,8},{8,9},{9,10... | collective-permute-start | bytes 1179656 | tf_op jit(solution)/shard_map/ppermute | solution.py:47
  50.9 0.0 collective-permute-done.refs_3_.refs_4_.w_other
  50.9 0.0 collective-permute-done.1.refs_4_.refs_5_
  50.9 3.6 %shard_map.67 = bf16[128,1536]{1,0:T(8,128)(2,1)} custom-call(bf16[128,3072]{1,0:T(8,128)(2,1)S(1)} %bitcast.15, bf16[1536,384]{1,0:T(8,128)(2,1)S(1)} %copy-done, bf16[384,1536]{1,0:T(8,128)(2,1)S(1)} %copy-done.1, bf16[1536,384]{1,0:T(8,128)(2,1)} %collective-permute-done.refs_3_.refs_4_.w_other, bf16[384,1536]{1,0:T(8,128)(2,1)} %collective-permute-done.1.refs_4_.refs_5_), custom_call_target="tpu_custom_call" | custom-call | flops 603979776 | bytes 4718592 | tf_op jit(solution)/shard_map/pallas_call | solution.py:67
  54.5 4.8 %all-to-all-start.1 = ((bf16[8,16,1536]{2,1,0:T(8,128)(2,1)}), bf16[8,16,1536]{2,1,0:T(8,128)(2,1)}, u32[]{:S(2)}, u32[]{:S(2)}) async-start(bf16[8,16,1536]{2,1,0:T(8,128)(2,1)} %bitcast.1), calls=%async_computation.1 | async-start | bytes 786432 | tf_op jit(solution)/shard_map/all_to_all | solution.py:33
  59.3 0.0 collective-permute-done.2.refs_0_
  59.3 1.0 collective-permute-done.3.refs_1_
  60.3 4.6 %shard_map.68 = bf16[128,1536]{1,0:T(8,128)(2,1)} custom-call(bf16[64,3072]{1,0:T(8,128)(2,1)S(1)} %collective-permute-done.2.refs_0_, bf16[64,3072]{1,0:T(8,128)(2,1)} %collective-permute-done.3.refs_1_, bf16[1536,384]{1,0:T(8,128)(2,1)S(1)} %copy-done, bf16[384,1536]{1,0:T(8,128)(2,1)S(1)} %copy-done.1, ...), custom_call_target="tpu_custom_call" | custom-call | flops 15099494400 | bytes 4718592 | tf_op jit(solution)/shard_map/pallas_call | solution.py:67
  64.9 0.0 all-to-all-done.1
  64.9 5.6 %all-to-all-start.2 = ((bf16[8,16,1536]{2,1,0:T(8,128)(2,1)}), bf16[8,16,1536]{2,1,0:T(8,128)(2,1)S(1)}, u32[]{:S(2)}, u32[]{:S(2)}) async-start(bf16[8,16,1536]{2,1,0:T(8,128)(2,1)} %bitcast.4), calls=%async_computation.2 | async-start | bytes 786432 | tf_op jit(solution)/shard_map/all_to_all | solution.py:33
  70.5 1.9 %pad_maximum_fusion.1 = bf16[128,3072]{1,0:T(8,128)(2,1)} fusion(bf16[64,3072]{1,0:T(8,128)(2,1)} %collective-permute-done.3.refs_1_, bf16[64,3072]{1,0:T(8,128)(2,1)S(1)} %collective-permute-done.2.refs_0_), kind=kLoop, calls=%fused_computation.11 | loop fusion | flops 1572864 | bytes 1572864 | tf_op jit(solution)/shard_map/concatenate | solution.py:154
  72.4 1.1 convert_reduce_fusion.1
  73.5 2.4 %all-to-all-done.2 = bf16[8,16,1536]{2,1,0:T(8,128)(2,1)S(1)} async-done(((bf16[8,16,1536]{2,1,0:T(8,128)(2,1)}), bf16[8,16,1536]{2,1,0:T(8,128)(2,1)S(1)}, u32[]{:S(2)}, u32[]{:S(2)}) %all-to-all-start.2) | async-done | bytes 393248 | tf_op jit(solution)/shard_map/all_to_all | solution.py:33
  75.9 0.1 convert_reduce_fusion
  76.0 0.0 copy-start.2
  76.0 0.1 multiply_convert_fusion
  76.1 0.9 broadcast_in_dim.5
  77.0 5.9 %all-to-all-start.3 = ((bf16[8,32,1536]{2,1,0:T(8,128)(2,1)}), bf16[8,32,1536]{2,1,0:T(8,128)(2,1)S(1)}, u32[]{:S(2)}, u32[]{:S(2)}) async-start(bf16[8,32,1536]{2,1,0:T(8,128)(2,1)} %broadcast_in_dim.5), calls=%async_computation.3 | async-start | bytes 1572864 | tf_op jit(solution)/shard_map/all_to_all | solution.py:33
  82.9 0.0 copy-done.2
  82.9 0.1 bitcast_select_fusion.1
  83.0 1.3 %pad_maximum_fusion = bf16[8,32,3072]{2,1,0:T(8,128)(2,1)} fusion(bf16[8,16,3072]{2,1,0:T(8,128)(2,1)S(1)} %get-tuple-element.8, bf16[8,16,3072]{2,1,0:T(8,128)(2,1)S(1)} %get-tuple-element.7), kind=kLoop, calls=%fused_computation.4 | loop fusion | flops 3145728 | bytes 3145728 | tf_op jit(solution)/shard_map/concatenate | solution.py:139
  84.3 1.9 %collective-permute-start.4 = (bf16[256,3072]{1,0:T(8,128)(2,1)}, bf16[256,3072]{1,0:T(8,128)(2,1)}, u32[]{:S(2)}, u32[]{:S(2)}) collective-permute-start(bf16[256,3072]{1,0:T(8,128)(2,1)} %bitcast.9), channel_id=1, source_target_pairs={{0,8},{8,0},{1,9},{9,1},{2,10},{10,2},{3,11},{11,3},{4,12},{12,4},... | collective-permute-start | bytes 4718600 | tf_op jit(solution)/shard_map/ppermute | solution.py:42
  86.2 4.3 %all-to-all-done.3 = bf16[8,32,1536]{2,1,0:T(8,128)(2,1)S(1)} async-done(((bf16[8,32,1536]{2,1,0:T(8,128)(2,1)}), bf16[8,32,1536]{2,1,0:T(8,128)(2,1)S(1)}, u32[]{:S(2)}, u32[]{:S(2)}) %all-to-all-start.3) | async-done | bytes 786464 | tf_op jit(solution)/shard_map/all_to_all | solution.py:33
  90.5 3.4 %shard_map.69 = bf16[256,1536]{1,0:T(8,128)(2,1)} custom-call(bf16[256,1536]{1,0:T(8,128)(2,1)S(1)} %bitcast.17, bf16[1536,384]{1,0:T(8,128)(2,1)S(1)} %copy-done, bf16[1536,384]{1,0:T(8,128)(2,1)} %collective-permute-done.refs_3_.refs_4_.w_other), custom_call_target="tpu_custom_call" | custom-call | flops 603979776 | bytes 3538944 | tf_op jit(solution)/shard_map/pallas_call | solution.py:67
  93.9 9.6 %all-to-all-start.4 = ((bf16[32,8,1536]{2,1,0:T(8,128)(2,1)}), bf16[32,8,1536]{2,1,0:T(8,128)(2,1)S(1)}, u32[]{:S(2)}, u32[]{:S(2)}) async-start(bf16[32,8,1536]{2,1,0:T(8,128)(2,1)} %bitcast.6), calls=%async_computation.4 | async-start | bytes 1572864 | tf_op jit(solution)/shard_map/all_to_all | solution.py:33
  103.5 1.5 %fusion.24 = (bf16[256,1536]{1,0:T(8,128)(2,1)S(1)}, bf16[256,1536]{1,0:T(8,128)(2,1)S(1)}) fusion(bf16[256,3072]{1,0:T(8,128)(2,1)} %bitcast.9), kind=kLoop, calls=%fused_computation.44 | loop fusion | bytes 3145728 | tf_op jit(solution)/shard_map/slice | solution.py:160
  105.0 0.1 fusion.26
  105.1 1.9 %collective-permute-start.5 = (bf16[256,384]{1,0:T(8,128)(2,1)S(1)}, bf16[256,384]{1,0:T(8,128)(2,1)S(1)}, u32[]{:S(2)}, u32[]{:S(2)}) collective-permute-start(bf16[256,384]{1,0:T(8,128)(2,1)S(1)} %get-tuple-element.11), channel_id=1, source_target_pairs={{0,8},{8,0},{1,9},{9,1},{2,10},{10,2},{3,11},{11,3},{4,12},{12,4},... | collective-permute-start | bytes 589832 | tf_op jit(solution)/shard_map/ppermute | solution.py:42
  107.0 2.4 %collective-permute-start.6 = (bf16[256,384]{1,0:T(8,128)(2,1)S(1)}, bf16[256,384]{1,0:T(8,128)(2,1)S(1)}, u32[]{:S(2)}, u32[]{:S(2)}) collective-permute-start(bf16[256,384]{1,0:T(8,128)(2,1)S(1)} %get-tuple-element.10), channel_id=1, source_target_pairs={{0,8},{8,0},{1,9},{9,1},{2,10},{10,2},{3,11},{11,3},{4,12},{12,4},... | collective-permute-start | bytes 589832 | tf_op jit(solution)/shard_map/ppermute | solution.py:42
  109.4 0.0 collective-permute-done.4
  109.4 1.5 %fusion.25 = (bf16[256,1536]{1,0:T(8,128)(2,1)S(1)}, bf16[256,1536]{1,0:T(8,128)(2,1)S(1)}) fusion(bf16[256,3072]{1,0:T(8,128)(2,1)} %collective-permute-done.4), kind=kLoop, calls=%fused_computation.45 | loop fusion | bytes 3145728 | tf_op jit(solution)/shard_map/slice | solution.py:160
  110.9 0.0 collective-permute-done.6
  110.9 1.8 %fusion.1 = bf16[384,1536]{1,0:T(8,128)(2,1)} fusion(bf16[256,1536]{1,0:T(8,128)(2,1)S(1)} %get-tuple-element.5, bf16[256,1536]{1,0:T(8,128)(2,1)S(1)} %get-tuple-element.3, bf16[256,384]{1,0:T(8,128)(2,1)S(1)} %collective-permute-done.6, bf16[256,384]{1,0:T(8,128)(2,1)S(1)} %get-tuple-element.9), kind=kOutput, calls=%fused_computation.3 | convolution fusion | flops 609091584 | bytes 3145728 | tf_op jit(solution)/shard_map/dot_general | solution.py:29
  112.7 0.0 collective-permute-done.5
  112.7 2.0 %fusion = bf16[1536,384]{1,0:T(8,128)(2,1)} fusion(bf16[256,1536]{1,0:T(8,128)(2,1)S(1)} %get-tuple-element.6, bf16[256,1536]{1,0:T(8,128)(2,1)S(1)} %get-tuple-element.4, bf16[256,384]{1,0:T(8,128)(2,1)S(1)} %collective-permute-done.5, bf16[256,384]{1,0:T(8,128)(2,1)S(1)} %get-tuple-element.12), kind=kOutput, calls=%fused_computation.2 | convolution fusion | flops 609091584 | bytes 3145728 | tf_op jit(solution)/shard_map/dot_general | solution.py:29
  114.8 11.5 %all-to-all-done.4 = bf16[32,8,1536]{2,1,0:T(8,128)(2,1)S(1)} async-done(((bf16[32,8,1536]{2,1,0:T(8,128)(2,1)}), bf16[32,8,1536]{2,1,0:T(8,128)(2,1)S(1)}, u32[]{:S(2)}, u32[]{:S(2)}) %all-to-all-start.4) | async-done | bytes 786464 | tf_op jit(solution)/shard_map/all_to_all | solution.py:33
  126.3 0.7 reduce_sum.32
  (2 shorter events, 0.0 us)
Async XLA Ops:
  0.6 17.6 %copy-start = (bf16[1536,384]{1,0:T(8,128)(2,1)S(1)}, bf16[1536,384]{1,0:T(8,128)(2,1)}, u32[]{:S(2)}) copy-start(bf16[1536,384]{1,0:T(8,128)(2,1)} %w_mine.1) | copy-start | bytes 3538948
  0.6 19.5 %copy-start.1 = (bf16[384,1536]{1,0:T(8,128)(2,1)S(1)}, bf16[384,1536]{1,0:T(8,128)(2,1)}, u32[]{:S(2)}) copy-start(bf16[384,1536]{1,0:T(8,128)(2,1)} %refs_3_.1) | copy-start | bytes 3538948
  2.5 41.2 %all-to-all-start = ((bf16[16,8,3072]{2,1,0:T(8,128)(2,1)}), bf16[16,8,3072]{2,1,0:T(8,128)(2,1)S(1)}, u32[]{:S(2)}, u32[]{:S(2)}) async-start(bf16[16,8,3072]{2,1,0:T(8,128)(2,1)} %broadcast_in_dim.4), calls=%async_computation | async-start | bytes 1572864 | tf_op jit(solution)/shard_map/all_to_all | solution.py:33
  18.2 32.7 %collective-permute-start = (bf16[1536,384]{1,0:T(8,128)(2,1)S(1)}, bf16[1536,384]{1,0:T(8,128)(2,1)}, u32[]{:S(2)}, u32[]{:S(2)}) collective-permute-start(bf16[1536,384]{1,0:T(8,128)(2,1)S(1)} %copy-done), channel_id=1, source_target_pairs={{0,8},{8,0},{1,9},{9,1},{2,10},{10,2},{3,11},{11,3},{4,12},{12,4},... | collective-permute-start | bytes 3538952 | tf_op jit(solution)/shard_map/ppermute | solution.py:42
  20.1 30.8 %collective-permute-start.1 = (bf16[384,1536]{1,0:T(8,128)(2,1)S(1)}, bf16[384,1536]{1,0:T(8,128)(2,1)}, u32[]{:S(2)}, u32[]{:S(2)}) collective-permute-start(bf16[384,1536]{1,0:T(8,128)(2,1)S(1)} %copy-done.1), channel_id=1, source_target_pairs={{0,8},{8,0},{1,9},{9,1},{2,10},{10,2},{3,11},{11,3},{4,12},{12,4},... | collective-permute-start | bytes 3538952 | tf_op jit(solution)/shard_map/ppermute | solution.py:42
  44.6 14.7 %collective-permute-start.2 = (bf16[64,3072]{1,0:T(8,128)(2,1)}, bf16[64,3072]{1,0:T(8,128)(2,1)S(1)}, u32[]{:S(2)}, u32[]{:S(2)}) collective-permute-start(bf16[64,3072]{1,0:T(8,128)(2,1)} %get-tuple-element.14), channel_id=1, source_target_pairs={{1,0},{2,1},{3,2},{4,3},{5,4},{6,5},{7,6},{0,7},{9,8},{10,9},{11,1... | collective-permute-start | bytes 1179656 | tf_op jit(solution)/shard_map/ppermute | solution.py:47
  49.0 11.3 %collective-permute-start.3 = (bf16[64,3072]{1,0:T(8,128)(2,1)}, bf16[64,3072]{1,0:T(8,128)(2,1)}, u32[]{:S(2)}, u32[]{:S(2)}) collective-permute-start(bf16[64,3072]{1,0:T(8,128)(2,1)} %get-tuple-element.13), channel_id=1, source_target_pairs={{7,0},{0,1},{1,2},{2,3},{3,4},{4,5},{5,6},{6,7},{15,8},{8,9},{9,10... | collective-permute-start | bytes 1179656 | tf_op jit(solution)/shard_map/ppermute | solution.py:47
  54.5 10.4 %all-to-all-start.1 = ((bf16[8,16,1536]{2,1,0:T(8,128)(2,1)}), bf16[8,16,1536]{2,1,0:T(8,128)(2,1)}, u32[]{:S(2)}, u32[]{:S(2)}) async-start(bf16[8,16,1536]{2,1,0:T(8,128)(2,1)} %bitcast.1), calls=%async_computation.1 | async-start | bytes 786432 | tf_op jit(solution)/shard_map/all_to_all | solution.py:33
  64.9 11.0 %all-to-all-start.2 = ((bf16[8,16,1536]{2,1,0:T(8,128)(2,1)}), bf16[8,16,1536]{2,1,0:T(8,128)(2,1)S(1)}, u32[]{:S(2)}, u32[]{:S(2)}) async-start(bf16[8,16,1536]{2,1,0:T(8,128)(2,1)} %bitcast.4), calls=%async_computation.2 | async-start | bytes 786432 | tf_op jit(solution)/shard_map/all_to_all | solution.py:33
  76.0 6.9 %copy-start.2 = (bf16[128,3072]{1,0:T(8,128)(2,1)S(1)}, bf16[128,3072]{1,0:T(8,128)(2,1)}, u32[]{:S(2)}) copy-start(bf16[128,3072]{1,0:T(8,128)(2,1)} %pad_maximum_fusion.1) | copy-start | bytes 2359300
  77.0 13.4 %all-to-all-start.3 = ((bf16[8,32,1536]{2,1,0:T(8,128)(2,1)}), bf16[8,32,1536]{2,1,0:T(8,128)(2,1)S(1)}, u32[]{:S(2)}, u32[]{:S(2)}) async-start(bf16[8,32,1536]{2,1,0:T(8,128)(2,1)} %broadcast_in_dim.5), calls=%async_computation.3 | async-start | bytes 1572864 | tf_op jit(solution)/shard_map/all_to_all | solution.py:33
  84.3 25.1 %collective-permute-start.4 = (bf16[256,3072]{1,0:T(8,128)(2,1)}, bf16[256,3072]{1,0:T(8,128)(2,1)}, u32[]{:S(2)}, u32[]{:S(2)}) collective-permute-start(bf16[256,3072]{1,0:T(8,128)(2,1)} %bitcast.9), channel_id=1, source_target_pairs={{0,8},{8,0},{1,9},{9,1},{2,10},{10,2},{3,11},{11,3},{4,12},{12,4},... | collective-permute-start | bytes 4718600 | tf_op jit(solution)/shard_map/ppermute | solution.py:42
  93.9 32.4 %all-to-all-start.4 = ((bf16[32,8,1536]{2,1,0:T(8,128)(2,1)}), bf16[32,8,1536]{2,1,0:T(8,128)(2,1)S(1)}, u32[]{:S(2)}, u32[]{:S(2)}) async-start(bf16[32,8,1536]{2,1,0:T(8,128)(2,1)} %bitcast.6), calls=%async_computation.4 | async-start | bytes 1572864 | tf_op jit(solution)/shard_map/all_to_all | solution.py:33
  105.1 7.7 %collective-permute-start.5 = (bf16[256,384]{1,0:T(8,128)(2,1)S(1)}, bf16[256,384]{1,0:T(8,128)(2,1)S(1)}, u32[]{:S(2)}, u32[]{:S(2)}) collective-permute-start(bf16[256,384]{1,0:T(8,128)(2,1)S(1)} %get-tuple-element.11), channel_id=1, source_target_pairs={{0,8},{8,0},{1,9},{9,1},{2,10},{10,2},{3,11},{11,3},{4,12},{12,4},... | collective-permute-start | bytes 589832 | tf_op jit(solution)/shard_map/ppermute | solution.py:42
  107.0 3.9 %collective-permute-start.6 = (bf16[256,384]{1,0:T(8,128)(2,1)S(1)}, bf16[256,384]{1,0:T(8,128)(2,1)S(1)}, u32[]{:S(2)}, u32[]{:S(2)}) collective-permute-start(bf16[256,384]{1,0:T(8,128)(2,1)S(1)} %get-tuple-element.10), channel_id=1, source_target_pairs={{0,8},{8,0},{1,9},{9,1},{2,10},{10,2},{3,11},{11,3},{4,12},{12,4},... | collective-permute-start | bytes 589832 | tf_op jit(solution)/shard_map/ppermute | solution.py:42

commit v4 on v2

v4 whole, which is shorter than its diff:
```python
import functools
import math

import jax
import jax.numpy as jnp
from jax import lax
from jax.experimental import pallas as pl
from jax.experimental.pallas import tpu as pltpu
from jax.sharding import Mesh, PartitionSpec as P

coef = 0.7978845608
ROWS = ("y_lo", "x")
EVEN = ("y_near", "y_far", "z_hi", "z_mid")
CHIPS = ("y_near", "y_far", "z_hi", "z_lo", "z_mid")
RING = ("z_hi", "z_mid", "z_lo")


def gelu_value(h):
    u = coef * (h + 0.044715 * h * h * h)
    return 0.5 * h * (1.0 + jnp.tanh(u))


def gelu_slope(h):
    t = jnp.tanh(coef * (h + 0.044715 * h * h * h))
    return 0.5 * (1.0 + t) + 0.5 * h * (1.0 - t * t) * coef * (1.0 + 0.134145 * h * h)


def dot(a, b, dims):
    return lax.dot_general(a, b, ((dims[:1], dims[1:]), ((), ())), preferred_element_type=jnp.float32)


def exchange(blocks, axes):
    return lax.all_to_all(blocks, axes, 0, 0, tiled=True)


def spread(block, axes):
    n = lax.axis_size(axes)
    return exchange(jnp.broadcast_to(block[None], (n,) + block.shape), axes)


def swap(block):
    return lax.ppermute(block, "core", [(0, 1), (1, 0)])


def fetch(block, by):
    n = lax.axis_size(RING)
    return lax.ppermute(block, RING, [((i + by) % n, i) for i in range(n)])


def gather(block):
    near = spread(block, EVEN).reshape(-1, block.shape[1])
    cut = near.shape[0] // 2
    return near, [fetch(near[:cut], 1), fetch(near[cut:], -1)]


VMEM = pl.BlockSpec(memory_space=pltpu.VMEM)
HBM = pl.BlockSpec(memory_space=pltpu.HBM)
PARAMS = pltpu.CompilerParams(vmem_limit_bytes=16 * 2**20)


def in_hbm(*arrays):
    return [pltpu.with_memory_space_constraint(a, pltpu.HBM) for a in arrays]


def start_all(places, arrived):
    copies = [pltpu.make_async_copy(a, b, arrived.at[i]) for i, (a, b) in enumerate(places)]
    for copy in copies:
        copy.start()
    return copies


def hold_kernel(w_in, w_out, held_in, held_out, arrived):
    for copy in start_all([(w_in, held_in), (w_out, held_out)], arrived):
        copy.wait()


def hold(w_in, w_out):
    return pl.pallas_call(
        hold_kernel,
        out_shape=(pltpu.VMEM(w_in.shape, w_in.dtype), pltpu.VMEM(w_out.shape, w_out.dtype)),
        in_specs=[HBM, HBM],
        out_specs=(VMEM, VMEM),
        scratch_shapes=[pltpu.SemaphoreType.DMA((2,))],
        compiler_params=PARAMS,
        cost_estimate=pl.CostEstimate(flops=0, bytes_accessed=8 * w_in.size, transcendentals=0),
    )(*in_hbm(w_in, w_out))


def products_kernel(count, *refs):
    blocks = refs[:count]
    w_in, w_out, w_in_other, w_out_other, part, block, in_held, out_held, total, arrived, sent = refs[count:]
    width, hidden = w_in.shape
    rows = blocks[0].shape[0]
    copies = start_all(
        [(b, block.at[pl.ds(i * rows, rows)]) for i, b in enumerate(blocks)]
        + [(w_in_other, in_held), (w_out_other, out_held)],
        arrived,
    )
    for copy in copies[:count]:
        copy.wait()
    results = []
    for i, weight in enumerate((w_in, w_out, in_held, out_held)):
        if i >= 2:
            copies[count + i - 2].wait()
        if i % 2 == 0:
            value = dot(block[:, :width], weight[...], (1, 0))
        else:
            value = dot(block[:, width:], weight[...], (1, 1))
        place = pl.ds((i // 2 + 2 * (i % 2)) * hidden, hidden)
        total[:, place] = value.astype(total.dtype)
        results.append(pltpu.make_async_copy(total.at[:, place], part.at[:, place], sent.at[i]))
        results[i].start()
    for result in results:
        result.wait()


def products(blocks, held, others, weight):
    rows, (width, hidden) = sum(b.shape[0] for b in blocks), held[0].shape
    dtype, count = blocks[0].dtype, len(blocks)
    return pl.pallas_call(
        functools.partial(products_kernel, count),
        out_shape=jax.ShapeDtypeStruct((rows, 4 * hidden), dtype),
        in_specs=[pl.BlockSpec(memory_space=pl.ANY)] * count + [VMEM] * 2 + [HBM] * 2,
        out_specs=HBM,
        scratch_shapes=[
            pltpu.VMEM((rows, 2 * width), dtype),
            pltpu.VMEM((width, hidden), dtype),
            pltpu.VMEM((hidden, width), dtype),
            pltpu.VMEM((rows, 4 * hidden), dtype),
            pltpu.SemaphoreType.DMA((count + 2,)),
            pltpu.SemaphoreType.DMA((4,)),
        ],
        compiler_params=PARAMS,
        cost_estimate=pl.CostEstimate(
            flops=8 * weight * rows * width * hidden, bytes_accessed=8 * width * hidden, transcendentals=0
        ),
    )(*blocks, *held, *in_hbm(*others))


def input_kernel(pair, w_mine, w_other, out, grad_hidden, mine, other, total, arrived, sent):
    width, hidden = mine.shape
    cut = width // 3
    pieces = [pl.ds(i * cut, cut) for i in range(3)]
    places = [(pair.at[:, 2 * hidden :], grad_hidden)]
    for piece in pieces:
        places += [(w_mine.at[piece], mine.at[piece]), (w_other.at[piece], other.at[piece])]
    copies = start_all(places, arrived)
    copies[0].wait()
    results = []
    for i, piece in enumerate(pieces):
        copies[1 + 2 * i].wait()
        value = dot(grad_hidden[:, :hidden], mine[piece, :], (1, 1))
        copies[2 + 2 * i].wait()
        value = value + dot(grad_hidden[:, hidden:], other[piece, :], (1, 1))
        total[:, piece] = value.astype(total.dtype)
        results.append(pltpu.make_async_copy(total.at[:, piece], out.at[:, piece], sent.at[i]))
        results[i].start()
    for result in results:
        result.wait()


def input_products(pair, w_in):
    rows, (width, hidden) = pair.shape[0], w_in[0].shape
    return pl.pallas_call(
        input_kernel,
        out_shape=jax.ShapeDtypeStruct((rows, width), pair.dtype),
        in_specs=[pl.BlockSpec(memory_space=pl.ANY)] + [HBM] * 2,
        out_specs=HBM,
        scratch_shapes=[
            pltpu.VMEM((rows, 2 * hidden), pair.dtype),
            pltpu.VMEM((width, hidden), pair.dtype),
            pltpu.VMEM((width, hidden), pair.dtype),
            pltpu.VMEM((rows, width), pair.dtype),
            pltpu.SemaphoreType.DMA((7,)),
            pltpu.SemaphoreType.DMA((3,)),
        ],
        compiler_params=PARAMS,
        cost_estimate=pl.CostEstimate(
            flops=4 * rows * width * hidden, bytes_accessed=6 * width * hidden, transcendentals=0
        ),
    )(pair, *in_hbm(*w_in))


def shards(tokens, grad_out, w_in, w_out):
    bf16, f32 = jnp.bfloat16, jnp.float32
    width, hidden = w_in.shape
    rows = lax.axis_size(ROWS)

    low = lax.axis_index("z_lo") == 0

    def by_z(near, far):
        return jnp.concatenate([jnp.where(low, near, far), jnp.where(low, far, near)], axis=-2)

    near, far = gather(jnp.concatenate([tokens, grad_out], axis=1))
    held, others = hold(w_in, w_out), [swap(w_in), swap(w_out)]
    parts = products([near], held, others, 25), products(far, held, others, 25)
    parts = [exchange(part.reshape(rows, -1, 4 * hidden), ROWS) for part in parts]
    total = by_z(*[jnp.sum(part.astype(f32), axis=0) for part in parts])
    pre, back = total[:, : 2 * hidden], total[:, 2 * hidden :]
    pair = jnp.concatenate([gelu_value(pre).astype(bf16), (back * gelu_slope(pre)).astype(bf16)], axis=1)
    pair = spread(pair, ROWS).reshape(-1, 4 * hidden)
    input_part = exchange(input_products(pair, [w_in, others[0]]).reshape(lax.axis_size(CHIPS), -1, width), CHIPS)
    grad_in = jnp.sum(input_part.astype(f32), axis=0)

    act, grad_hidden = pair[:, : 2 * hidden], pair[:, 2 * hidden :]
    far = jnp.concatenate(far, axis=0)
    own = by_z(*[b.reshape(rows, -1, 2 * width) for b in (near, far)]).reshape(-1, 2 * width)
    other = swap(own)
    act = jnp.concatenate([act[:, :hidden], swap(act[:, hidden:])], axis=0)
    grad_hidden = jnp.concatenate([grad_hidden[:, :hidden], swap(grad_hidden[:, hidden:])], axis=0)
    x_all = jnp.concatenate([own[:, :width], other[:, :width]], axis=0)
    dy_all = jnp.concatenate([own[:, width:], other[:, width:]], axis=0)
    factor = 1.0 / math.sqrt(x_all.shape[0])
    grad_w_in = dot(x_all, grad_hidden, (0, 0))
    grad_w_out = dot(act, dy_all, (0, 0))
    return (
        grad_in.astype(bf16),
        (grad_w_in * factor).astype(bf16),
        (grad_w_out * factor).astype(bf16),
    )


def solution(mesh):
    rows, cols, deps = mesh.devices.shape
    fine = Mesh(
        mesh.devices.reshape(2, rows // 2, cols // 4, 2, 2, 2, deps // 4, 2),
        ("y_lo", "x", "y_far", "y_near", "core", "z_hi", "z_mid", "z_lo"),
    )
    blocks = ("y_far", "y_near", "core", "z_hi", "z_mid", "z_lo")
    placed = (P(blocks, ROWS), P(blocks, ROWS), P(ROWS, blocks), P(blocks, ROWS))
    return jax.shard_map(
        shards,
        mesh=fine,
        in_specs=placed,
        out_specs=(P(blocks, ROWS), P(ROWS, blocks), P(blocks, ROWS)),
        check_vma=False,
    )
```

time: 136 us -> 128 us (0.941)
  the two profiles are of different devices: /device:TPU:10 before, /device:TPU:6 now
where the time goes in v4:
time: 128 us; the launch traced here: 125 us
  starting transfers between devices  53.7 us (42%)
  waiting for transfers between devices  46.7 us (36%)
  Pallas kernels  11.6 us (9%)
  local copies, waits for them, and re-layouts  6.64 us (5%)
  matrix products  3.85 us (3%)
  other arithmetic  1.96 us (2%)
    all_to_all x5, waiting for transfers between devices, exchange(): return lax.all_to_all(blocks, axes, 0, 0, tiled=True)  44.6 us
    all_to_all x5, starting transfers between devices, exchange(): return lax.all_to_all(blocks, axes, 0, 0, tiled=True)  37.3 us
    ppermute x5, starting transfers between devices, swap(): return lax.ppermute(block, 'core', [(0, 1), (1, 0)])  10.6 us
    pallas_call x2, Pallas kernels, products(): pl.pallas_call(functools.partial(products_kernel, count), out_shape=jax.S...  6.46 us
    ppermute x2, starting transfers between devices, fetch(): return lax.ppermute(block, RING, [((i + by) % n, i) for i in range(n)])  5.83 us
    dot_general x2, matrix products, dot(): lax.dot_general(a, b, ((dims[:1], dims[1:]), ((), ())), preferred_element...  3.85 us
    pallas_call x1, Pallas kernels, input_products(): pl.pallas_call(input_kernel, out_shape=jax.ShapeDtypeStruct((rows, width)...  3.47 us
  transfers between devices with their start and end apart: 12, of which 5 were waited for; matrix products, arithmetic and copies ran while one was open for 5% of the time, Pallas kernels for 9%

profile of v4, /device:TPU:6, one launch (start us, length us, event | category | flops | bytes accessed | tf_op | source)
XLA Modules:
  0.0 125.3 jit_solution(16207959730683822422)
XLA Ops:
  0.6 0.8 pad_maximum_fusion.4
  1.4 1.0 broadcast_in_dim.4
  2.3 15.7 %all-to-all-start = ((bf16[16,8,3072]{2,1,0:T(8,128)(2,1)}), bf16[16,8,3072]{2,1,0:T(8,128)(2,1)S(1)}, u32[]{:S(2)}, u32[]{:S(2)}) async-start(bf16[16,8,3072]{2,1,0:T(8,128)(2,1)} %broadcast_in_dim.4), calls=%async_computation | async-start | bytes 1572864 | tf_op jit(solution)/shard_map/all_to_all | solution.py:33
  18.0 1.9 %collective-permute-start = (bf16[1536,384]{1,0:T(8,128)(2,1)}, bf16[1536,384]{1,0:T(8,128)(2,1)}, u32[]{:S(2)}, u32[]{:S(2)}) collective-permute-start(bf16[1536,384]{1,0:T(8,128)(2,1)} %w_mine.1), channel_id=1, source_target_pairs={{0,8},{8,0},{1,9},{9,1},{2,10},{10,2},{3,11},{11,3},{4,12},{12,4},... | collective-permute-start | bytes 3538952 | tf_op jit(solution)/shard_map/ppermute | solution.py:42
  20.0 2.4 %collective-permute-start.1 = (bf16[384,1536]{1,0:T(8,128)(2,1)}, bf16[384,1536]{1,0:T(8,128)(2,1)}, u32[]{:S(2)}, u32[]{:S(2)}) collective-permute-start(bf16[384,1536]{1,0:T(8,128)(2,1)} %w_out.1), channel_id=1, source_target_pairs={{0,8},{8,0},{1,9},{9,1},{2,10},{10,2},{3,11},{11,3},{4,12},{12,4},... | collective-permute-start | bytes 3538952 | tf_op jit(solution)/shard_map/ppermute | solution.py:42
  22.4 1.6 %shard_map.67 = (bf16[1536,384]{1,0:T(8,128)(2,1)S(1)}, bf16[384,1536]{1,0:T(8,128)(2,1)S(1)}) custom-call(bf16[1536,384]{1,0:T(8,128)(2,1)} %w_mine.1, bf16[384,1536]{1,0:T(8,128)(2,1)} %w_out.1), custom_call_target="tpu_custom_call" | custom-call | bytes 4718592 | tf_op jit(solution)/shard_map/pallas_call | solution.py:78
  24.0 0.0 copy-start
  24.0 1.0 copy-done
  25.0 21.3 %all-to-all-done = bf16[16,8,3072]{2,1,0:T(8,128)(2,1)S(1)} async-done(((bf16[16,8,3072]{2,1,0:T(8,128)(2,1)}), bf16[16,8,3072]{2,1,0:T(8,128)(2,1)S(1)}, u32[]{:S(2)}, u32[]{:S(2)}) %all-to-all-start) | async-done | bytes 786464 | tf_op jit(solution)/shard_map/all_to_all | solution.py:33
  46.4 0.0 copy-start.1
  46.4 0.8 slice_bitcast_fusion
  47.2 3.3 %collective-permute-start.2 = (bf16[64,3072]{1,0:T(8,128)(2,1)}, bf16[64,3072]{1,0:T(8,128)(2,1)S(1)}, u32[]{:S(2)}, u32[]{:S(2)}) collective-permute-start(bf16[64,3072]{1,0:T(8,128)(2,1)} %get-tuple-element.18), channel_id=1, source_target_pairs={{1,0},{2,1},{3,2},{4,3},{5,4},{6,5},{7,6},{0,7},{9,8},{10,9},{11,1... | collective-permute-start | bytes 1179656 | tf_op jit(solution)/shard_map/ppermute | solution.py:47
  50.5 2.5 %collective-permute-start.3 = (bf16[64,3072]{1,0:T(8,128)(2,1)S(1)}, bf16[64,3072]{1,0:T(8,128)(2,1)S(1)}, u32[]{:S(2)}, u32[]{:S(2)}) collective-permute-start(bf16[64,3072]{1,0:T(8,128)(2,1)S(1)} %get-tuple-element.17), channel_id=1, source_target_pairs={{7,0},{0,1},{1,2},{2,3},{3,4},{4,5},{5,6},{6,7},{15,8},{8,9},{9,10... | collective-permute-start | bytes 1179656 | tf_op jit(solution)/shard_map/ppermute | solution.py:47
  53.0 0.0 collective-permute-done.refs_3_.refs_4_.w_other
  53.0 0.0 collective-permute-done.1.refs_4_.refs_5_
  53.0 0.0 copy-done.1
  53.0 3.1 %shard_map.68 = bf16[128,1536]{1,0:T(8,128)(2,1)} custom-call(bf16[128,3072]{1,0:T(8,128)(2,1)S(1)} %bitcast.15, bf16[1536,384]{1,0:T(8,128)(2,1)S(1)} %get-tuple-element.5.refs_1_.refs_2_, bf16[384,1536]{1,0:T(8,128)(2,1)S(1)} %copy-done.1, bf16[1536,384]{1,0:T(8,128)(2,1)} %collective-permute-done.refs_3_.refs_4_.w_other, ...), custom_call_target="tpu_custom_call" | custom-call | flops 15099494400 | bytes 4718592 | tf_op jit(solution)/shard_map/pallas_call | solution.py:120
  56.1 4.8 %all-to-all-start.1 = ((bf16[8,16,1536]{2,1,0:T(8,128)(2,1)}), bf16[8,16,1536]{2,1,0:T(8,128)(2,1)S(1)}, u32[]{:S(2)}, u32[]{:S(2)}) async-start(bf16[8,16,1536]{2,1,0:T(8,128)(2,1)} %bitcast.1), calls=%async_computation.1 | async-start | bytes 786432 | tf_op jit(solution)/shard_map/all_to_all | solution.py:33
  60.9 0.0 collective-permute-done.2.refs_0_
  60.9 2.1 %collective-permute-done.3.refs_1_ = bf16[64,3072]{1,0:T(8,128)(2,1)S(1)} collective-permute-done((bf16[64,3072]{1,0:T(8,128)(2,1)S(1)}, bf16[64,3072]{1,0:T(8,128)(2,1)S(1)}, u32[]{:S(2)}, u32[]{:S(2)}) %collective-permute-start.3) | collective-permute-done | bytes 393248 | tf_op jit(solution)/shard_map/ppermute | solution.py:47
  63.0 0.0 copy-start.2
  63.0 1.3 %copy-done.2 = bf16[384,1536]{1,0:T(8,128)(2,1)S(1)} copy-done((bf16[384,1536]{1,0:T(8,128)(2,1)S(1)}, bf16[384,1536]{1,0:T(8,128)(2,1)}, u32[]{:S(2)}) %copy-start.2) | copy-done | bytes 1179672
  64.3 3.4 %shard_map.69 = bf16[128,1536]{1,0:T(8,128)(2,1)} custom-call(bf16[64,3072]{1,0:T(8,128)(2,1)S(1)} %collective-permute-done.2.refs_0_, bf16[64,3072]{1,0:T(8,128)(2,1)S(1)} %collective-permute-done.3.refs_1_, bf16[1536,384]{1,0:T(8,128)(2,1)S(1)} %get-tuple-element.5.refs_1_.refs_2_, bf16[384,1536]{1,0:T(8,128)(2,1)S(1)} %copy-done.2, ...), custom_call_target="tpu_custom_call" | custom-call | flops 15099494400 | bytes 4718592 | tf_op jit(solution)/shard_map/pallas_call | solution.py:120
  67.7 0.0 all-to-all-done.1
  67.7 4.8 %all-to-all-start.2 = ((bf16[8,16,1536]{2,1,0:T(8,128)(2,1)}), bf16[8,16,1536]{2,1,0:T(8,128)(2,1)S(1)}, u32[]{:S(2)}, u32[]{:S(2)}) async-start(bf16[8,16,1536]{2,1,0:T(8,128)(2,1)} %bitcast.4), calls=%async_computation.2 | async-start | bytes 786432 | tf_op jit(solution)/shard_map/all_to_all | solution.py:33
  72.5 0.1 pad_maximum_fusion.1
  72.5 0.1 convert_reduce_fusion.1
  72.6 5.2 %all-to-all-done.2 = bf16[8,16,1536]{2,1,0:T(8,128)(2,1)S(1)} async-done(((bf16[8,16,1536]{2,1,0:T(8,128)(2,1)}), bf16[8,16,1536]{2,1,0:T(8,128)(2,1)S(1)}, u32[]{:S(2)}, u32[]{:S(2)}) %all-to-all-start.2) | async-done | bytes 393248 | tf_op jit(solution)/shard_map/all_to_all | solution.py:33
  77.8 0.1 convert_reduce_fusion
  77.9 0.1 multiply_convert_fusion
  78.0 0.9 broadcast_in_dim.5
  79.0 5.9 %all-to-all-start.3 = ((bf16[8,32,1536]{2,1,0:T(8,128)(2,1)}), bf16[8,32,1536]{2,1,0:T(8,128)(2,1)S(1)}, u32[]{:S(2)}, u32[]{:S(2)}) async-start(bf16[8,32,1536]{2,1,0:T(8,128)(2,1)} %broadcast_in_dim.5), calls=%async_computation.3 | async-start | bytes 1572864 | tf_op jit(solution)/shard_map/all_to_all | solution.py:33
  84.8 0.1 bitcast_select_fusion.1
  84.9 0.1 pad_maximum_fusion
  85.0 1.9 %collective-permute-start.4 = (bf16[256,3072]{1,0:T(8,128)(2,1)S(1)}, bf16[256,3072]{1,0:T(8,128)(2,1)}, u32[]{:S(2)}, u32[]{:S(2)}) collective-permute-start(bf16[256,3072]{1,0:T(8,128)(2,1)S(1)} %bitcast.19), channel_id=1, source_target_pairs={{0,8},{8,0},{1,9},{9,1},{2,10},{10,2},{3,11},{11,3},{4,12},{12,4},... | collective-permute-start | bytes 4718600 | tf_op jit(solution)/shard_map/ppermute | solution.py:42
  87.0 5.4 %all-to-all-done.3 = bf16[8,32,1536]{2,1,0:T(8,128)(2,1)S(1)} async-done(((bf16[8,32,1536]{2,1,0:T(8,128)(2,1)}), bf16[8,32,1536]{2,1,0:T(8,128)(2,1)S(1)}, u32[]{:S(2)}, u32[]{:S(2)}) %all-to-all-start.3) | async-done | bytes 786464 | tf_op jit(solution)/shard_map/all_to_all | solution.py:33
  92.4 3.5 %shard_map.70 = bf16[256,1536]{1,0:T(8,128)(2,1)} custom-call(bf16[256,1536]{1,0:T(8,128)(2,1)S(1)} %bitcast.17, bf16[1536,384]{1,0:T(8,128)(2,1)} %w_mine.1, bf16[1536,384]{1,0:T(8,128)(2,1)} %collective-permute-done.refs_3_.refs_4_.w_other), custom_call_target="tpu_custom_call" | custom-call | flops 603979776 | bytes 3538944 | tf_op jit(solution)/shard_map/pallas_call | solution.py:164
  95.9 6.2 %all-to-all-start.4 = ((bf16[32,8,1536]{2,1,0:T(8,128)(2,1)}), bf16[32,8,1536]{2,1,0:T(8,128)(2,1)S(1)}, u32[]{:S(2)}, u32[]{:S(2)}) async-start(bf16[32,8,1536]{2,1,0:T(8,128)(2,1)} %bitcast.6), calls=%async_computation.4 | async-start | bytes 1572864 | tf_op jit(solution)/shard_map/all_to_all | solution.py:33
  102.1 0.1 fusion.24
  102.2 0.1 fusion.26
  102.3 1.9 %collective-permute-start.5 = (bf16[256,384]{1,0:T(8,128)(2,1)S(1)}, bf16[256,384]{1,0:T(8,128)(2,1)S(1)}, u32[]{:S(2)}, u32[]{:S(2)}) collective-permute-start(bf16[256,384]{1,0:T(8,128)(2,1)S(1)} %get-tuple-element.15), channel_id=1, source_target_pairs={{0,8},{8,0},{1,9},{9,1},{2,10},{10,2},{3,11},{11,3},{4,12},{12,4},... | collective-permute-start | bytes 589832 | tf_op jit(solution)/shard_map/ppermute | solution.py:42
  104.3 2.4 %collective-permute-start.6 = (bf16[256,384]{1,0:T(8,128)(2,1)S(1)}, bf16[256,384]{1,0:T(8,128)(2,1)S(1)}, u32[]{:S(2)}, u32[]{:S(2)}) collective-permute-start(bf16[256,384]{1,0:T(8,128)(2,1)S(1)} %get-tuple-element.14), channel_id=1, source_target_pairs={{0,8},{8,0},{1,9},{9,1},{2,10},{10,2},{3,11},{11,3},{4,12},{12,4},... | collective-permute-start | bytes 589832 | tf_op jit(solution)/shard_map/ppermute | solution.py:42
  106.7 0.0 collective-permute-done.4
  106.7 1.5 %fusion.25 = (bf16[256,1536]{1,0:T(8,128)(2,1)S(1)}, bf16[256,1536]{1,0:T(8,128)(2,1)S(1)}) fusion(bf16[256,3072]{1,0:T(8,128)(2,1)} %collective-permute-done.4), kind=kLoop, calls=%fused_computation.45 | loop fusion | bytes 3145728 | tf_op jit(solution)/shard_map/slice | solution.py:212
  108.2 0.0 collective-permute-done.6
  108.2 1.8 %fusion.1 = bf16[384,1536]{1,0:T(8,128)(2,1)} fusion(bf16[256,1536]{1,0:T(8,128)(2,1)S(1)} %get-tuple-element.9, bf16[256,1536]{1,0:T(8,128)(2,1)S(1)} %get-tuple-element.7, bf16[256,384]{1,0:T(8,128)(2,1)S(1)} %collective-permute-done.6, bf16[256,384]{1,0:T(8,128)(2,1)S(1)} %get-tuple-element.13), kind=kOutput, calls=%fused_computation.3 | convolution fusion | flops 609091584 | bytes 3145728 | tf_op jit(solution)/shard_map/dot_general | solution.py:29
  110.0 0.0 collective-permute-done.5
  110.0 2.0 %fusion = bf16[1536,384]{1,0:T(8,128)(2,1)} fusion(bf16[256,1536]{1,0:T(8,128)(2,1)S(1)} %get-tuple-element.10, bf16[256,1536]{1,0:T(8,128)(2,1)S(1)} %get-tuple-element.8, bf16[256,384]{1,0:T(8,128)(2,1)S(1)} %collective-permute-done.5, bf16[256,384]{1,0:T(8,128)(2,1)S(1)} %get-tuple-element.16), kind=kOutput, calls=%fused_computation.2 | convolution fusion | flops 609091584 | bytes 3145728 | tf_op jit(solution)/shard_map/dot_general | solution.py:29
  112.0 12.6 %all-to-all-done.4 = bf16[32,8,1536]{2,1,0:T(8,128)(2,1)S(1)} async-done(((bf16[32,8,1536]{2,1,0:T(8,128)(2,1)}), bf16[32,8,1536]{2,1,0:T(8,128)(2,1)S(1)}, u32[]{:S(2)}, u32[]{:S(2)}) %all-to-all-start.4) | async-done | bytes 786464 | tf_op jit(solution)/shard_map/all_to_all | solution.py:33
  124.6 0.7 reduce_sum.32
  (2 shorter events, 0.0 us)
Async XLA Ops:
  2.3 44.0 %all-to-all-start = ((bf16[16,8,3072]{2,1,0:T(8,128)(2,1)}), bf16[16,8,3072]{2,1,0:T(8,128)(2,1)S(1)}, u32[]{:S(2)}, u32[]{:S(2)}) async-start(bf16[16,8,3072]{2,1,0:T(8,128)(2,1)} %broadcast_in_dim.4), calls=%async_computation | async-start | bytes 1572864 | tf_op jit(solution)/shard_map/all_to_all | solution.py:33
  18.0 35.0 %collective-permute-start = (bf16[1536,384]{1,0:T(8,128)(2,1)}, bf16[1536,384]{1,0:T(8,128)(2,1)}, u32[]{:S(2)}, u32[]{:S(2)}) collective-permute-start(bf16[1536,384]{1,0:T(8,128)(2,1)} %w_mine.1), channel_id=1, source_target_pairs={{0,8},{8,0},{1,9},{9,1},{2,10},{10,2},{3,11},{11,3},{4,12},{12,4},... | collective-permute-start | bytes 3538952 | tf_op jit(solution)/shard_map/ppermute | solution.py:42
  20.0 33.1 %collective-permute-start.1 = (bf16[384,1536]{1,0:T(8,128)(2,1)}, bf16[384,1536]{1,0:T(8,128)(2,1)}, u32[]{:S(2)}, u32[]{:S(2)}) collective-permute-start(bf16[384,1536]{1,0:T(8,128)(2,1)} %w_out.1), channel_id=1, source_target_pairs={{0,8},{8,0},{1,9},{9,1},{2,10},{10,2},{3,11},{11,3},{4,12},{12,4},... | collective-permute-start | bytes 3538952 | tf_op jit(solution)/shard_map/ppermute | solution.py:42
  24.0 1.0 copy-start
  46.4 6.7 %copy-start.1 = (bf16[384,1536]{1,0:T(8,128)(2,1)S(1)}, bf16[384,1536]{1,0:T(8,128)(2,1)}, u32[]{:S(2)}) copy-start(bf16[384,1536]{1,0:T(8,128)(2,1)} %copy-done) | copy-start | bytes 3538948
  47.2 13.7 %collective-permute-start.2 = (bf16[64,3072]{1,0:T(8,128)(2,1)}, bf16[64,3072]{1,0:T(8,128)(2,1)S(1)}, u32[]{:S(2)}, u32[]{:S(2)}) collective-permute-start(bf16[64,3072]{1,0:T(8,128)(2,1)} %get-tuple-element.18), channel_id=1, source_target_pairs={{1,0},{2,1},{3,2},{4,3},{5,4},{6,5},{7,6},{0,7},{9,8},{10,9},{11,1... | collective-permute-start | bytes 1179656 | tf_op jit(solution)/shard_map/ppermute | solution.py:47
  50.5 12.6 %collective-permute-start.3 = (bf16[64,3072]{1,0:T(8,128)(2,1)S(1)}, bf16[64,3072]{1,0:T(8,128)(2,1)S(1)}, u32[]{:S(2)}, u32[]{:S(2)}) collective-permute-start(bf16[64,3072]{1,0:T(8,128)(2,1)S(1)} %get-tuple-element.17), channel_id=1, source_target_pairs={{7,0},{0,1},{1,2},{2,3},{3,4},{4,5},{5,6},{6,7},{15,8},{8,9},{9,10... | collective-permute-start | bytes 1179656 | tf_op jit(solution)/shard_map/ppermute | solution.py:47
  56.1 11.6 %all-to-all-start.1 = ((bf16[8,16,1536]{2,1,0:T(8,128)(2,1)}), bf16[8,16,1536]{2,1,0:T(8,128)(2,1)S(1)}, u32[]{:S(2)}, u32[]{:S(2)}) async-start(bf16[8,16,1536]{2,1,0:T(8,128)(2,1)} %bitcast.1), calls=%async_computation.1 | async-start | bytes 786432 | tf_op jit(solution)/shard_map/all_to_all | solution.py:33
  63.0 1.3 %copy-start.2 = (bf16[384,1536]{1,0:T(8,128)(2,1)S(1)}, bf16[384,1536]{1,0:T(8,128)(2,1)}, u32[]{:S(2)}) copy-start(bf16[384,1536]{1,0:T(8,128)(2,1)} %copy-done) | copy-start | bytes 3538948
  67.7 10.2 %all-to-all-start.2 = ((bf16[8,16,1536]{2,1,0:T(8,128)(2,1)}), bf16[8,16,1536]{2,1,0:T(8,128)(2,1)S(1)}, u32[]{:S(2)}, u32[]{:S(2)}) async-start(bf16[8,16,1536]{2,1,0:T(8,128)(2,1)} %bitcast.4), calls=%async_computation.2 | async-start | bytes 786432 | tf_op jit(solution)/shard_map/all_to_all | solution.py:33
  79.0 13.4 %all-to-all-start.3 = ((bf16[8,32,1536]{2,1,0:T(8,128)(2,1)}), bf16[8,32,1536]{2,1,0:T(8,128)(2,1)S(1)}, u32[]{:S(2)}, u32[]{:S(2)}) async-start(bf16[8,32,1536]{2,1,0:T(8,128)(2,1)} %broadcast_in_dim.5), calls=%async_computation.3 | async-start | bytes 1572864 | tf_op jit(solution)/shard_map/all_to_all | solution.py:33
  85.0 21.6 %collective-permute-start.4 = (bf16[256,3072]{1,0:T(8,128)(2,1)S(1)}, bf16[256,3072]{1,0:T(8,128)(2,1)}, u32[]{:S(2)}, u32[]{:S(2)}) collective-permute-start(bf16[256,3072]{1,0:T(8,128)(2,1)S(1)} %bitcast.19), channel_id=1, source_target_pairs={{0,8},{8,0},{1,9},{9,1},{2,10},{10,2},{3,11},{11,3},{4,12},{12,4},... | collective-permute-start | bytes 4718600 | tf_op jit(solution)/shard_map/ppermute | solution.py:42
  95.9 28.7 %all-to-all-start.4 = ((bf16[32,8,1536]{2,1,0:T(8,128)(2,1)}), bf16[32,8,1536]{2,1,0:T(8,128)(2,1)S(1)}, u32[]{:S(2)}, u32[]{:S(2)}) async-start(bf16[32,8,1536]{2,1,0:T(8,128)(2,1)} %bitcast.6), calls=%async_computation.4 | async-start | bytes 1572864 | tf_op jit(solution)/shard_map/all_to_all | solution.py:33
  102.3 7.7 %collective-permute-start.5 = (bf16[256,384]{1,0:T(8,128)(2,1)S(1)}, bf16[256,384]{1,0:T(8,128)(2,1)S(1)}, u32[]{:S(2)}, u32[]{:S(2)}) collective-permute-start(bf16[256,384]{1,0:T(8,128)(2,1)S(1)} %get-tuple-element.15), channel_id=1, source_target_pairs={{0,8},{8,0},{1,9},{9,1},{2,10},{10,2},{3,11},{11,3},{4,12},{12,4},... | collective-permute-start | bytes 589832 | tf_op jit(solution)/shard_map/ppermute | solution.py:42
  104.3 3.9 %collective-permute-start.6 = (bf16[256,384]{1,0:T(8,128)(2,1)S(1)}, bf16[256,384]{1,0:T(8,128)(2,1)S(1)}, u32[]{:S(2)}, u32[]{:S(2)}) collective-permute-start(bf16[256,384]{1,0:T(8,128)(2,1)S(1)} %get-tuple-element.14), channel_id=1, source_target_pairs={{0,8},{8,0},{1,9},{9,1},{2,10},{10,2},{3,11},{11,3},{4,12},{12,4},... | collective-permute-start | bytes 589832 | tf_op jit(solution)/shard_map/ppermute | solution.py:42

commit v5 on v4

--- a/solution.py
+++ b/solution.py
@@ -10,8 +10,8 @@
 
 coef = 0.7978845608
 ROWS = ("y_lo", "x")
-EVEN = ("y_near", "y_far", "z_hi", "z_mid")
-CHIPS = ("y_near", "y_far", "z_hi", "z_lo", "z_mid")
+EVEN = ("y_far", "y_near", "z_hi", "z_mid")
+CHIPS = ("y_far", "y_near", "z_hi", "z_lo", "z_mid")
 RING = ("z_hi", "z_mid", "z_lo")
 
 

time: 128 us -> 126 us (0.984)
  waiting for transfers between devices: 46.7 us -> 43.7 us
  starting transfers between devices: 53.7 us -> 55.6 us
    all_to_all x5, waiting for transfers between devices: 44.6 us -> 42.7 us  [exchange(): return lax.all_to_all(blocks, axes, 0, 0, tiled=True)]
    all_to_all x5, starting transfers between devices: 37.3 us -> 39.2 us  [exchange(): return lax.all_to_all(blocks, axes, 0, 0, tiled=True)]
where the time goes in v5:
time: 126 us; the launch traced here: 124 us
  starting transfers between devices  55.6 us (44%)
  waiting for transfers between devices  43.7 us (35%)
  Pallas kernels  11.6 us (9%)
  local copies, waits for them, and re-layouts  6.64 us (5%)
  matrix products  3.84 us (3%)
  other arithmetic  1.96 us (2%)
    all_to_all x5, waiting for transfers between devices, exchange(): return lax.all_to_all(blocks, axes, 0, 0, tiled=True)  42.7 us
    all_to_all x5, starting transfers between devices, exchange(): return lax.all_to_all(blocks, axes, 0, 0, tiled=True)  39.2 us
    ppermute x5, starting transfers between devices, swap(): return lax.ppermute(block, 'core', [(0, 1), (1, 0)])  10.6 us
    pallas_call x2, Pallas kernels, products(): pl.pallas_call(functools.partial(products_kernel, count), out_shape=jax.S...  6.46 us
    ppermute x2, starting transfers between devices, fetch(): return lax.ppermute(block, RING, [((i + by) % n, i) for i in range(n)])  5.83 us
    dot_general x2, matrix products, dot(): lax.dot_general(a, b, ((dims[:1], dims[1:]), ((), ())), preferred_element...  3.84 us
    pallas_call x1, Pallas kernels, input_products(): pl.pallas_call(input_kernel, out_shape=jax.ShapeDtypeStruct((rows, width)...  3.47 us
  transfers between devices with their start and end apart: 12, of which 5 were waited for; matrix products, arithmetic and copies ran while one was open for 5% of the time, Pallas kernels for 9%

profile of v5, /device:TPU:6, one launch (start us, length us, event | category | flops | bytes accessed | tf_op | source)
XLA Modules:
  0.0 124.2 jit_solution(14564878492771829651)
XLA Ops:
  0.6 0.8 pad_maximum_fusion.4
  1.4 1.0 broadcast_in_dim.4
  2.3 15.7 %all-to-all-start = ((bf16[16,8,3072]{2,1,0:T(8,128)(2,1)}), bf16[16,8,3072]{2,1,0:T(8,128)(2,1)S(1)}, u32[]{:S(2)}, u32[]{:S(2)}) async-start(bf16[16,8,3072]{2,1,0:T(8,128)(2,1)} %broadcast_in_dim.4), calls=%async_computation | async-start | bytes 1572864 | tf_op jit(solution)/shard_map/all_to_all | solution.py:33
  18.0 1.9 %collective-permute-start = (bf16[1536,384]{1,0:T(8,128)(2,1)}, bf16[1536,384]{1,0:T(8,128)(2,1)}, u32[]{:S(2)}, u32[]{:S(2)}) collective-permute-start(bf16[1536,384]{1,0:T(8,128)(2,1)} %w_mine.1), channel_id=1, source_target_pairs={{0,8},{8,0},{1,9},{9,1},{2,10},{10,2},{3,11},{11,3},{4,12},{12,4},... | collective-permute-start | bytes 3538952 | tf_op jit(solution)/shard_map/ppermute | solution.py:42
  20.0 2.4 %collective-permute-start.1 = (bf16[384,1536]{1,0:T(8,128)(2,1)}, bf16[384,1536]{1,0:T(8,128)(2,1)}, u32[]{:S(2)}, u32[]{:S(2)}) collective-permute-start(bf16[384,1536]{1,0:T(8,128)(2,1)} %w_out.1), channel_id=1, source_target_pairs={{0,8},{8,0},{1,9},{9,1},{2,10},{10,2},{3,11},{11,3},{4,12},{12,4},... | collective-permute-start | bytes 3538952 | tf_op jit(solution)/shard_map/ppermute | solution.py:42
  22.4 1.6 %shard_map.67 = (bf16[1536,384]{1,0:T(8,128)(2,1)S(1)}, bf16[384,1536]{1,0:T(8,128)(2,1)S(1)}) custom-call(bf16[1536,384]{1,0:T(8,128)(2,1)} %w_mine.1, bf16[384,1536]{1,0:T(8,128)(2,1)} %w_out.1), custom_call_target="tpu_custom_call" | custom-call | bytes 4718592 | tf_op jit(solution)/shard_map/pallas_call | solution.py:78
  24.0 0.0 copy-start
  24.0 1.0 copy-done
  25.0 20.7 %all-to-all-done = bf16[16,8,3072]{2,1,0:T(8,128)(2,1)S(1)} async-done(((bf16[16,8,3072]{2,1,0:T(8,128)(2,1)}), bf16[16,8,3072]{2,1,0:T(8,128)(2,1)S(1)}, u32[]{:S(2)}, u32[]{:S(2)}) %all-to-all-start) | async-done | bytes 786464 | tf_op jit(solution)/shard_map/all_to_all | solution.py:33
  45.7 0.0 copy-start.1
  45.7 0.8 slice_bitcast_fusion
  46.5 2.7 %collective-permute-start.2 = (bf16[64,3072]{1,0:T(8,128)(2,1)}, bf16[64,3072]{1,0:T(8,128)(2,1)S(1)}, u32[]{:S(2)}, u32[]{:S(2)}) collective-permute-start(bf16[64,3072]{1,0:T(8,128)(2,1)} %get-tuple-element.18), channel_id=1, source_target_pairs={{1,0},{2,1},{3,2},{4,3},{5,4},{6,5},{7,6},{0,7},{9,8},{10,9},{11,1... | collective-permute-start | bytes 1179656 | tf_op jit(solution)/shard_map/ppermute | solution.py:47
  49.2 3.1 %collective-permute-start.3 = (bf16[64,3072]{1,0:T(8,128)(2,1)S(1)}, bf16[64,3072]{1,0:T(8,128)(2,1)S(1)}, u32[]{:S(2)}, u32[]{:S(2)}) collective-permute-start(bf16[64,3072]{1,0:T(8,128)(2,1)S(1)} %get-tuple-element.17), channel_id=1, source_target_pairs={{7,0},{0,1},{1,2},{2,3},{3,4},{4,5},{5,6},{6,7},{15,8},{8,9},{9,10... | collective-permute-start | bytes 1179656 | tf_op jit(solution)/shard_map/ppermute | solution.py:47
  52.4 0.0 collective-permute-done.refs_3_.refs_4_.w_other
  52.4 0.0 collective-permute-done.1.refs_4_.refs_5_
  52.4 0.0 copy-done.1
  52.4 3.1 %shard_map.68 = bf16[128,1536]{1,0:T(8,128)(2,1)} custom-call(bf16[128,3072]{1,0:T(8,128)(2,1)S(1)} %bitcast.15, bf16[1536,384]{1,0:T(8,128)(2,1)S(1)} %get-tuple-element.5.refs_1_.refs_2_, bf16[384,1536]{1,0:T(8,128)(2,1)S(1)} %copy-done.1, bf16[1536,384]{1,0:T(8,128)(2,1)} %collective-permute-done.refs_3_.refs_4_.w_other, ...), custom_call_target="tpu_custom_call" | custom-call | flops 15099494400 | bytes 4718592 | tf_op jit(solution)/shard_map/pallas_call | solution.py:120
  55.5 4.8 %all-to-all-start.1 = ((bf16[8,16,1536]{2,1,0:T(8,128)(2,1)}), bf16[8,16,1536]{2,1,0:T(8,128)(2,1)S(1)}, u32[]{:S(2)}, u32[]{:S(2)}) async-start(bf16[8,16,1536]{2,1,0:T(8,128)(2,1)} %bitcast.1), calls=%async_computation.1 | async-start | bytes 786432 | tf_op jit(solution)/shard_map/all_to_all | solution.py:33
  60.3 0.0 collective-permute-done.2.refs_0_
  60.3 0.9 collective-permute-done.3.refs_1_
  61.2 0.0 copy-start.2
  61.2 1.3 %copy-done.2 = bf16[384,1536]{1,0:T(8,128)(2,1)S(1)} copy-done((bf16[384,1536]{1,0:T(8,128)(2,1)S(1)}, bf16[384,1536]{1,0:T(8,128)(2,1)}, u32[]{:S(2)}) %copy-start.2) | copy-done | bytes 1179672
  62.5 3.4 %shard_map.69 = bf16[128,1536]{1,0:T(8,128)(2,1)} custom-call(bf16[64,3072]{1,0:T(8,128)(2,1)S(1)} %collective-permute-done.2.refs_0_, bf16[64,3072]{1,0:T(8,128)(2,1)S(1)} %collective-permute-done.3.refs_1_, bf16[1536,384]{1,0:T(8,128)(2,1)S(1)} %get-tuple-element.5.refs_1_.refs_2_, bf16[384,1536]{1,0:T(8,128)(2,1)S(1)} %copy-done.2, ...), custom_call_target="tpu_custom_call" | custom-call | flops 15099494400 | bytes 4718592 | tf_op jit(solution)/shard_map/pallas_call | solution.py:120
  65.9 0.0 all-to-all-done.1
  65.9 5.5 %all-to-all-start.2 = ((bf16[8,16,1536]{2,1,0:T(8,128)(2,1)}), bf16[8,16,1536]{2,1,0:T(8,128)(2,1)S(1)}, u32[]{:S(2)}, u32[]{:S(2)}) async-start(bf16[8,16,1536]{2,1,0:T(8,128)(2,1)} %bitcast.4), calls=%async_computation.2 | async-start | bytes 786432 | tf_op jit(solution)/shard_map/all_to_all | solution.py:33
  71.4 0.1 pad_maximum_fusion.1
  71.4 0.1 convert_reduce_fusion.1
  71.5 5.3 %all-to-all-done.2 = bf16[8,16,1536]{2,1,0:T(8,128)(2,1)S(1)} async-done(((bf16[8,16,1536]{2,1,0:T(8,128)(2,1)}), bf16[8,16,1536]{2,1,0:T(8,128)(2,1)S(1)}, u32[]{:S(2)}, u32[]{:S(2)}) %all-to-all-start.2) | async-done | bytes 393248 | tf_op jit(solution)/shard_map/all_to_all | solution.py:33
  76.8 0.1 convert_reduce_fusion
  76.9 0.1 multiply_convert_fusion
  77.0 0.9 broadcast_in_dim.5
  77.9 5.9 %all-to-all-start.3 = ((bf16[8,32,1536]{2,1,0:T(8,128)(2,1)}), bf16[8,32,1536]{2,1,0:T(8,128)(2,1)S(1)}, u32[]{:S(2)}, u32[]{:S(2)}) async-start(bf16[8,32,1536]{2,1,0:T(8,128)(2,1)} %broadcast_in_dim.5), calls=%async_computation.3 | async-start | bytes 1572864 | tf_op jit(solution)/shard_map/all_to_all | solution.py:33
  83.7 0.1 bitcast_select_fusion.1
  83.9 0.1 pad_maximum_fusion
  84.0 1.9 %collective-permute-start.4 = (bf16[256,3072]{1,0:T(8,128)(2,1)S(1)}, bf16[256,3072]{1,0:T(8,128)(2,1)}, u32[]{:S(2)}, u32[]{:S(2)}) collective-permute-start(bf16[256,3072]{1,0:T(8,128)(2,1)S(1)} %bitcast.19), channel_id=1, source_target_pairs={{0,8},{8,0},{1,9},{9,1},{2,10},{10,2},{3,11},{11,3},{4,12},{12,4},... | collective-permute-start | bytes 4718600 | tf_op jit(solution)/shard_map/ppermute | solution.py:42
  85.9 5.4 %all-to-all-done.3 = bf16[8,32,1536]{2,1,0:T(8,128)(2,1)S(1)} async-done(((bf16[8,32,1536]{2,1,0:T(8,128)(2,1)}), bf16[8,32,1536]{2,1,0:T(8,128)(2,1)S(1)}, u32[]{:S(2)}, u32[]{:S(2)}) %all-to-all-start.3) | async-done | bytes 786464 | tf_op jit(solution)/shard_map/all_to_all | solution.py:33
  91.3 3.5 %shard_map.70 = bf16[256,1536]{1,0:T(8,128)(2,1)} custom-call(bf16[256,1536]{1,0:T(8,128)(2,1)S(1)} %bitcast.17, bf16[1536,384]{1,0:T(8,128)(2,1)} %w_mine.1, bf16[1536,384]{1,0:T(8,128)(2,1)} %collective-permute-done.refs_3_.refs_4_.w_other), custom_call_target="tpu_custom_call" | custom-call | flops 603979776 | bytes 3538944 | tf_op jit(solution)/shard_map/pallas_call | solution.py:164
  94.8 7.4 %all-to-all-start.4 = ((bf16[32,8,1536]{2,1,0:T(8,128)(2,1)}), bf16[32,8,1536]{2,1,0:T(8,128)(2,1)S(1)}, u32[]{:S(2)}, u32[]{:S(2)}) async-start(bf16[32,8,1536]{2,1,0:T(8,128)(2,1)} %bitcast.6), calls=%async_computation.4 | async-start | bytes 1572864 | tf_op jit(solution)/shard_map/all_to_all | solution.py:33
  102.2 0.1 fusion.24
  102.3 0.1 fusion.26
  102.4 1.9 %collective-permute-start.5 = (bf16[256,384]{1,0:T(8,128)(2,1)S(1)}, bf16[256,384]{1,0:T(8,128)(2,1)S(1)}, u32[]{:S(2)}, u32[]{:S(2)}) collective-permute-start(bf16[256,384]{1,0:T(8,128)(2,1)S(1)} %get-tuple-element.15), channel_id=1, source_target_pairs={{0,8},{8,0},{1,9},{9,1},{2,10},{10,2},{3,11},{11,3},{4,12},{12,4},... | collective-permute-start | bytes 589832 | tf_op jit(solution)/shard_map/ppermute | solution.py:42
  104.3 2.4 %collective-permute-start.6 = (bf16[256,384]{1,0:T(8,128)(2,1)S(1)}, bf16[256,384]{1,0:T(8,128)(2,1)S(1)}, u32[]{:S(2)}, u32[]{:S(2)}) collective-permute-start(bf16[256,384]{1,0:T(8,128)(2,1)S(1)} %get-tuple-element.14), channel_id=1, source_target_pairs={{0,8},{8,0},{1,9},{9,1},{2,10},{10,2},{3,11},{11,3},{4,12},{12,4},... | collective-permute-start | bytes 589832 | tf_op jit(solution)/shard_map/ppermute | solution.py:42
  106.7 0.0 collective-permute-done.4
  106.7 1.5 %fusion.25 = (bf16[256,1536]{1,0:T(8,128)(2,1)S(1)}, bf16[256,1536]{1,0:T(8,128)(2,1)S(1)}) fusion(bf16[256,3072]{1,0:T(8,128)(2,1)} %collective-permute-done.4), kind=kLoop, calls=%fused_computation.45 | loop fusion | bytes 3145728 | tf_op jit(solution)/shard_map/slice | solution.py:212
  108.2 0.0 collective-permute-done.6
  108.2 1.8 %fusion.1 = bf16[384,1536]{1,0:T(8,128)(2,1)} fusion(bf16[256,1536]{1,0:T(8,128)(2,1)S(1)} %get-tuple-element.9, bf16[256,1536]{1,0:T(8,128)(2,1)S(1)} %get-tuple-element.7, bf16[256,384]{1,0:T(8,128)(2,1)S(1)} %collective-permute-done.6, bf16[256,384]{1,0:T(8,128)(2,1)S(1)} %get-tuple-element.13), kind=kOutput, calls=%fused_computation.3 | convolution fusion | flops 609091584 | bytes 3145728 | tf_op jit(solution)/shard_map/dot_general | solution.py:29
  110.0 0.0 collective-permute-done.5
  110.0 2.0 %fusion = bf16[1536,384]{1,0:T(8,128)(2,1)} fusion(bf16[256,1536]{1,0:T(8,128)(2,1)S(1)} %get-tuple-element.10, bf16[256,1536]{1,0:T(8,128)(2,1)S(1)} %get-tuple-element.8, bf16[256,384]{1,0:T(8,128)(2,1)S(1)} %collective-permute-done.5, bf16[256,384]{1,0:T(8,128)(2,1)S(1)} %get-tuple-element.16), kind=kOutput, calls=%fused_computation.2 | convolution fusion | flops 609091584 | bytes 3145728 | tf_op jit(solution)/shard_map/dot_general | solution.py:29
  112.1 11.4 %all-to-all-done.4 = bf16[32,8,1536]{2,1,0:T(8,128)(2,1)S(1)} async-done(((bf16[32,8,1536]{2,1,0:T(8,128)(2,1)}), bf16[32,8,1536]{2,1,0:T(8,128)(2,1)S(1)}, u32[]{:S(2)}, u32[]{:S(2)}) %all-to-all-start.4) | async-done | bytes 786464 | tf_op jit(solution)/shard_map/all_to_all | solution.py:33
  123.4 0.7 reduce_sum.32
  (2 shorter events, 0.0 us)
Async XLA Ops:
  2.3 43.4 %all-to-all-start = ((bf16[16,8,3072]{2,1,0:T(8,128)(2,1)}), bf16[16,8,3072]{2,1,0:T(8,128)(2,1)S(1)}, u32[]{:S(2)}, u32[]{:S(2)}) async-start(bf16[16,8,3072]{2,1,0:T(8,128)(2,1)} %broadcast_in_dim.4), calls=%async_computation | async-start | bytes 1572864 | tf_op jit(solution)/shard_map/all_to_all | solution.py:33
  18.0 34.3 %collective-permute-start = (bf16[1536,384]{1,0:T(8,128)(2,1)}, bf16[1536,384]{1,0:T(8,128)(2,1)}, u32[]{:S(2)}, u32[]{:S(2)}) collective-permute-start(bf16[1536,384]{1,0:T(8,128)(2,1)} %w_mine.1), channel_id=1, source_target_pairs={{0,8},{8,0},{1,9},{9,1},{2,10},{10,2},{3,11},{11,3},{4,12},{12,4},... | collective-permute-start | bytes 3538952 | tf_op jit(solution)/shard_map/ppermute | solution.py:42
  20.0 32.4 %collective-permute-start.1 = (bf16[384,1536]{1,0:T(8,128)(2,1)}, bf16[384,1536]{1,0:T(8,128)(2,1)}, u32[]{:S(2)}, u32[]{:S(2)}) collective-permute-start(bf16[384,1536]{1,0:T(8,128)(2,1)} %w_out.1), channel_id=1, source_target_pairs={{0,8},{8,0},{1,9},{9,1},{2,10},{10,2},{3,11},{11,3},{4,12},{12,4},... | collective-permute-start | bytes 3538952 | tf_op jit(solution)/shard_map/ppermute | solution.py:42
  24.0 1.0 copy-start
  45.7 6.7 %copy-start.1 = (bf16[384,1536]{1,0:T(8,128)(2,1)S(1)}, bf16[384,1536]{1,0:T(8,128)(2,1)}, u32[]{:S(2)}) copy-start(bf16[384,1536]{1,0:T(8,128)(2,1)} %copy-done) | copy-start | bytes 3538948
  46.5 13.7 %collective-permute-start.2 = (bf16[64,3072]{1,0:T(8,128)(2,1)}, bf16[64,3072]{1,0:T(8,128)(2,1)S(1)}, u32[]{:S(2)}, u32[]{:S(2)}) collective-permute-start(bf16[64,3072]{1,0:T(8,128)(2,1)} %get-tuple-element.18), channel_id=1, source_target_pairs={{1,0},{2,1},{3,2},{4,3},{5,4},{6,5},{7,6},{0,7},{9,8},{10,9},{11,1... | collective-permute-start | bytes 1179656 | tf_op jit(solution)/shard_map/ppermute | solution.py:47
  49.2 12.0 %collective-permute-start.3 = (bf16[64,3072]{1,0:T(8,128)(2,1)S(1)}, bf16[64,3072]{1,0:T(8,128)(2,1)S(1)}, u32[]{:S(2)}, u32[]{:S(2)}) collective-permute-start(bf16[64,3072]{1,0:T(8,128)(2,1)S(1)} %get-tuple-element.17), channel_id=1, source_target_pairs={{7,0},{0,1},{1,2},{2,3},{3,4},{4,5},{5,6},{6,7},{15,8},{8,9},{9,10... | collective-permute-start | bytes 1179656 | tf_op jit(solution)/shard_map/ppermute | solution.py:47
  55.5 10.4 %all-to-all-start.1 = ((bf16[8,16,1536]{2,1,0:T(8,128)(2,1)}), bf16[8,16,1536]{2,1,0:T(8,128)(2,1)S(1)}, u32[]{:S(2)}, u32[]{:S(2)}) async-start(bf16[8,16,1536]{2,1,0:T(8,128)(2,1)} %bitcast.1), calls=%async_computation.1 | async-start | bytes 786432 | tf_op jit(solution)/shard_map/all_to_all | solution.py:33
  61.2 1.3 %copy-start.2 = (bf16[384,1536]{1,0:T(8,128)(2,1)S(1)}, bf16[384,1536]{1,0:T(8,128)(2,1)}, u32[]{:S(2)}) copy-start(bf16[384,1536]{1,0:T(8,128)(2,1)} %copy-done) | copy-start | bytes 3538948
  65.9 10.9 %all-to-all-start.2 = ((bf16[8,16,1536]{2,1,0:T(8,128)(2,1)}), bf16[8,16,1536]{2,1,0:T(8,128)(2,1)S(1)}, u32[]{:S(2)}, u32[]{:S(2)}) async-start(bf16[8,16,1536]{2,1,0:T(8,128)(2,1)} %bitcast.4), calls=%async_computation.2 | async-start | bytes 786432 | tf_op jit(solution)/shard_map/all_to_all | solution.py:33
  77.9 13.4 %all-to-all-start.3 = ((bf16[8,32,1536]{2,1,0:T(8,128)(2,1)}), bf16[8,32,1536]{2,1,0:T(8,128)(2,1)S(1)}, u32[]{:S(2)}, u32[]{:S(2)}) async-start(bf16[8,32,1536]{2,1,0:T(8,128)(2,1)} %broadcast_in_dim.5), calls=%async_computation.3 | async-start | bytes 1572864 | tf_op jit(solution)/shard_map/all_to_all | solution.py:33
  84.0 22.8 %collective-permute-start.4 = (bf16[256,3072]{1,0:T(8,128)(2,1)S(1)}, bf16[256,3072]{1,0:T(8,128)(2,1)}, u32[]{:S(2)}, u32[]{:S(2)}) collective-permute-start(bf16[256,3072]{1,0:T(8,128)(2,1)S(1)} %bitcast.19), channel_id=1, source_target_pairs={{0,8},{8,0},{1,9},{9,1},{2,10},{10,2},{3,11},{11,3},{4,12},{12,4},... | collective-permute-start | bytes 4718600 | tf_op jit(solution)/shard_map/ppermute | solution.py:42
  94.8 28.6 %all-to-all-start.4 = ((bf16[32,8,1536]{2,1,0:T(8,128)(2,1)}), bf16[32,8,1536]{2,1,0:T(8,128)(2,1)S(1)}, u32[]{:S(2)}, u32[]{:S(2)}) async-start(bf16[32,8,1536]{2,1,0:T(8,128)(2,1)} %bitcast.6), calls=%async_computation.4 | async-start | bytes 1572864 | tf_op jit(solution)/shard_map/all_to_all | solution.py:33
  102.4 7.7 %collective-permute-start.5 = (bf16[256,384]{1,0:T(8,128)(2,1)S(1)}, bf16[256,384]{1,0:T(8,128)(2,1)S(1)}, u32[]{:S(2)}, u32[]{:S(2)}) collective-permute-start(bf16[256,384]{1,0:T(8,128)(2,1)S(1)} %get-tuple-element.15), channel_id=1, source_target_pairs={{0,8},{8,0},{1,9},{9,1},{2,10},{10,2},{3,11},{11,3},{4,12},{12,4},... | collective-permute-start | bytes 589832 | tf_op jit(solution)/shard_map/ppermute | solution.py:42
  104.3 3.9 %collective-permute-start.6 = (bf16[256,384]{1,0:T(8,128)(2,1)S(1)}, bf16[256,384]{1,0:T(8,128)(2,1)S(1)}, u32[]{:S(2)}, u32[]{:S(2)}) collective-permute-start(bf16[256,384]{1,0:T(8,128)(2,1)S(1)} %get-tuple-element.14), channel_id=1, source_target_pairs={{0,8},{8,0},{1,9},{9,1},{2,10},{10,2},{3,11},{11,3},{4,12},{12,4},... | collective-permute-start | bytes 589832 | tf_op jit(solution)/shard_map/ppermute | solution.py:42

commit v6 on v5

--- a/solution.py
+++ b/solution.py
@@ -120,7 +120,7 @@
     return pl.pallas_call(
         functools.partial(products_kernel, count),
         out_shape=jax.ShapeDtypeStruct((rows, 4 * hidden), dtype),
-        in_specs=[pl.BlockSpec(memory_space=pl.ANY)] * count + [VMEM] * 2 + [HBM] * 2,
+        in_specs=[HBM] * count + [VMEM] * 2 + [HBM] * 2,
         out_specs=HBM,
         scratch_shapes=[
             pltpu.VMEM((rows, 2 * width), dtype),
@@ -134,7 +134,7 @@
         cost_estimate=pl.CostEstimate(
             flops=8 * weight * rows * width * hidden, bytes_accessed=8 * width * hidden, transcendentals=0
         ),
-    )(*blocks, *held, *in_hbm(*others))
+    )(*in_hbm(*blocks), *held, *in_hbm(*others))
 
 
 def input_kernel(pair, w_mine, w_other, out, grad_hidden, mine, other, total, arrived, sent):

time: 126 us -> 125 us (level)
  local copies, waits for them, and re-layouts: 6.64 us -> 4.59 us
    unnamed x6, local copies, waits for them, and re-layouts: 2.28 us -> 0.01 us
  transfers between devices with their start and end apart: 12 -> 12, of which waited for: 5 -> 6; matrix products, arithmetic and copies ran while one was open for 5% -> 6% of each run, Pallas kernels for 9% -> 10%
where the time goes in v6:
time: 125 us; the launch traced here: 124 us
  starting transfers between devices  55 us (44%)
  waiting for transfers between devices  44.1 us (35%)
  Pallas kernels  12.3 us (10%)
  local copies, waits for them, and re-layouts  4.59 us (4%)
  matrix products  3.84 us (3%)
  other arithmetic  3.07 us (2%)
    all_to_all x5, waiting for transfers between devices, exchange(): return lax.all_to_all(blocks, axes, 0, 0, tiled=True)  43.4 us
    all_to_all x5, starting transfers between devices, exchange(): return lax.all_to_all(blocks, axes, 0, 0, tiled=True)  38.6 us
    ppermute x5, starting transfers between devices, swap(): return lax.ppermute(block, 'core', [(0, 1), (1, 0)])  10.6 us
    pallas_call x2, Pallas kernels, products(): pl.pallas_call(functools.partial(products_kernel, count), out_shape=jax.S...  7.15 us
    ppermute x2, starting transfers between devices, fetch(): return lax.ppermute(block, RING, [((i + by) % n, i) for i in range(n)])  5.83 us
    dot_general x2, matrix products, dot(): lax.dot_general(a, b, ((dims[:1], dims[1:]), ((), ())), preferred_element...  3.84 us
    pallas_call x1, Pallas kernels, input_products(): pl.pallas_call(input_kernel, out_shape=jax.ShapeDtypeStruct((rows, width)...  3.47 us
  transfers between devices with their start and end apart: 12, of which 6 were waited for; matrix products, arithmetic and copies ran while one was open for 6% of the time, Pallas kernels for 10%

profile of v6, /device:TPU:6, one launch (start us, length us, event | category | flops | bytes accessed | tf_op | source)
XLA Modules:
  0.0 123.8 jit_solution(9850243025964315648)
XLA Ops:
  0.6 0.8 pad_maximum_fusion.4
  1.4 1.0 broadcast_in_dim.4
  2.3 15.7 %all-to-all-start = ((bf16[16,8,3072]{2,1,0:T(8,128)(2,1)}), bf16[16,8,3072]{2,1,0:T(8,128)(2,1)S(1)}, u32[]{:S(2)}, u32[]{:S(2)}) async-start(bf16[16,8,3072]{2,1,0:T(8,128)(2,1)} %broadcast_in_dim.4), calls=%async_computation | async-start | bytes 1572864 | tf_op jit(solution)/shard_map/all_to_all | solution.py:33
  18.0 1.9 %collective-permute-start = (bf16[1536,384]{1,0:T(8,128)(2,1)}, bf16[1536,384]{1,0:T(8,128)(2,1)}, u32[]{:S(2)}, u32[]{:S(2)}) collective-permute-start(bf16[1536,384]{1,0:T(8,128)(2,1)} %w_mine.1), channel_id=1, source_target_pairs={{0,8},{8,0},{1,9},{9,1},{2,10},{10,2},{3,11},{11,3},{4,12},{12,4},... | collective-permute-start | bytes 3538952 | tf_op jit(solution)/shard_map/ppermute | solution.py:42
  20.0 2.4 %collective-permute-start.1 = (bf16[384,1536]{1,0:T(8,128)(2,1)}, bf16[384,1536]{1,0:T(8,128)(2,1)}, u32[]{:S(2)}, u32[]{:S(2)}) collective-permute-start(bf16[384,1536]{1,0:T(8,128)(2,1)} %w_out.1), channel_id=1, source_target_pairs={{0,8},{8,0},{1,9},{9,1},{2,10},{10,2},{3,11},{11,3},{4,12},{12,4},... | collective-permute-start | bytes 3538952 | tf_op jit(solution)/shard_map/ppermute | solution.py:42
  22.4 1.6 %shard_map.67 = (bf16[1536,384]{1,0:T(8,128)(2,1)S(1)}, bf16[384,1536]{1,0:T(8,128)(2,1)S(1)}) custom-call(bf16[1536,384]{1,0:T(8,128)(2,1)} %w_mine.1, bf16[384,1536]{1,0:T(8,128)(2,1)} %w_out.1), custom_call_target="tpu_custom_call" | custom-call | bytes 4718592 | tf_op jit(solution)/shard_map/pallas_call | solution.py:78
  24.0 21.7 %all-to-all-done = bf16[16,8,3072]{2,1,0:T(8,128)(2,1)S(1)} async-done(((bf16[16,8,3072]{2,1,0:T(8,128)(2,1)}), bf16[16,8,3072]{2,1,0:T(8,128)(2,1)S(1)}, u32[]{:S(2)}, u32[]{:S(2)}) %all-to-all-start) | async-done | bytes 786464 | tf_op jit(solution)/shard_map/all_to_all | solution.py:33
  45.7 0.0 copy-start
  45.7 1.0 slice_bitcast_fusion
  46.7 2.7 %collective-permute-start.2 = (bf16[64,3072]{1,0:T(8,128)(2,1)}, bf16[64,3072]{1,0:T(8,128)(2,1)S(1)}, u32[]{:S(2)}, u32[]{:S(2)}) collective-permute-start(bf16[64,3072]{1,0:T(8,128)(2,1)} %get-tuple-element.18), channel_id=1, source_target_pairs={{1,0},{2,1},{3,2},{4,3},{5,4},{6,5},{7,6},{0,7},{9,8},{10,9},{11,1... | collective-permute-start | bytes 1179656 | tf_op jit(solution)/shard_map/ppermute | solution.py:47
  49.4 3.1 %collective-permute-start.3 = (bf16[64,3072]{1,0:T(8,128)(2,1)}, bf16[64,3072]{1,0:T(8,128)(2,1)}, u32[]{:S(2)}, u32[]{:S(2)}) collective-permute-start(bf16[64,3072]{1,0:T(8,128)(2,1)} %get-tuple-element.17), channel_id=1, source_target_pairs={{7,0},{0,1},{1,2},{2,3},{3,4},{4,5},{5,6},{6,7},{15,8},{8,9},{9,10... | collective-permute-start | bytes 1179656 | tf_op jit(solution)/shard_map/ppermute | solution.py:47
  52.6 0.0 collective-permute-done.refs_3_.refs_4_.w_other
  52.6 0.0 collective-permute-done.1.refs_4_.refs_5_
  52.6 0.0 copy-done
  52.6 3.6 %shard_map.68 = bf16[128,1536]{1,0:T(8,128)(2,1)} custom-call(bf16[128,3072]{1,0:T(8,128)(2,1)} %bitcast.17, bf16[1536,384]{1,0:T(8,128)(2,1)S(1)} %get-tuple-element.5.refs_1_.refs_2_, bf16[384,1536]{1,0:T(8,128)(2,1)S(1)} %get-tuple-element.6.refs_2_.refs_3_, bf16[1536,384]{1,0:T(8,128)(2,1)} %collective-permute-done.refs_3_.refs_4_.w_other, ...), custom_call_target="tpu_custom_call" | custom-call | flops 15099494400 | bytes 4718592 | tf_op jit(solution)/shard_map/pallas_call | solution.py:120
  56.2 4.8 %all-to-all-start.1 = ((bf16[8,16,1536]{2,1,0:T(8,128)(2,1)}), bf16[8,16,1536]{2,1,0:T(8,128)(2,1)S(1)}, u32[]{:S(2)}, u32[]{:S(2)}) async-start(bf16[8,16,1536]{2,1,0:T(8,128)(2,1)} %bitcast.1), calls=%async_computation.1 | async-start | bytes 786432 | tf_op jit(solution)/shard_map/all_to_all | solution.py:33
  61.0 0.0 collective-permute-done.2.refs_0_
  61.0 0.0 copy-start.2
  61.0 0.7 collective-permute-done.3.refs_1_
  61.7 0.0 copy-done.2
  61.7 3.6 %shard_map.69 = bf16[128,1536]{1,0:T(8,128)(2,1)} custom-call(bf16[64,3072]{1,0:T(8,128)(2,1)} %copy-done.2, bf16[64,3072]{1,0:T(8,128)(2,1)} %collective-permute-done.3.refs_1_, bf16[1536,384]{1,0:T(8,128)(2,1)S(1)} %get-tuple-element.5.refs_1_.refs_2_, bf16[384,1536]{1,0:T(8,128)(2,1)S(1)} %get-tuple-element.6.refs_2_.refs_3_, ...), custom_call_target="tpu_custom_call" | custom-call | flops 15099494400 | bytes 4718592 | tf_op jit(solution)/shard_map/pallas_call | solution.py:120
  65.3 1.0 all-to-all-done.1
  66.4 5.8 %all-to-all-start.2 = ((bf16[8,16,1536]{2,1,0:T(8,128)(2,1)}), bf16[8,16,1536]{2,1,0:T(8,128)(2,1)S(1)}, u32[]{:S(2)}, u32[]{:S(2)}) async-start(bf16[8,16,1536]{2,1,0:T(8,128)(2,1)} %bitcast.4), calls=%async_computation.2 | async-start | bytes 786432 | tf_op jit(solution)/shard_map/all_to_all | solution.py:33
  72.1 1.2 pad_maximum_fusion.1
  73.3 0.1 convert_reduce_fusion.1
  73.3 4.2 %all-to-all-done.2 = bf16[8,16,1536]{2,1,0:T(8,128)(2,1)S(1)} async-done(((bf16[8,16,1536]{2,1,0:T(8,128)(2,1)}), bf16[8,16,1536]{2,1,0:T(8,128)(2,1)S(1)}, u32[]{:S(2)}, u32[]{:S(2)}) %all-to-all-start.2) | async-done | bytes 393248 | tf_op jit(solution)/shard_map/all_to_all | solution.py:33
  77.5 0.1 convert_reduce_fusion
  77.6 0.0 copy-start.1
  77.6 0.1 multiply_convert_fusion
  77.7 0.9 broadcast_in_dim.5
  78.6 5.9 %all-to-all-start.3 = ((bf16[8,32,1536]{2,1,0:T(8,128)(2,1)}), bf16[8,32,1536]{2,1,0:T(8,128)(2,1)S(1)}, u32[]{:S(2)}, u32[]{:S(2)}) async-start(bf16[8,32,1536]{2,1,0:T(8,128)(2,1)} %broadcast_in_dim.5), calls=%async_computation.3 | async-start | bytes 1572864 | tf_op jit(solution)/shard_map/all_to_all | solution.py:33
  84.5 0.0 copy-done.1
  84.5 0.1 bitcast_select_fusion.1
  84.6 0.1 pad_maximum_fusion
  84.7 1.9 %collective-permute-start.4 = (bf16[256,3072]{1,0:T(8,128)(2,1)S(1)}, bf16[256,3072]{1,0:T(8,128)(2,1)}, u32[]{:S(2)}, u32[]{:S(2)}) collective-permute-start(bf16[256,3072]{1,0:T(8,128)(2,1)S(1)} %bitcast.19), channel_id=1, source_target_pairs={{0,8},{8,0},{1,9},{9,1},{2,10},{10,2},{3,11},{11,3},{4,12},{12,4},... | collective-permute-start | bytes 4718600 | tf_op jit(solution)/shard_map/ppermute | solution.py:42
  86.6 5.4 %all-to-all-done.3 = bf16[8,32,1536]{2,1,0:T(8,128)(2,1)S(1)} async-done(((bf16[8,32,1536]{2,1,0:T(8,128)(2,1)}), bf16[8,32,1536]{2,1,0:T(8,128)(2,1)S(1)}, u32[]{:S(2)}, u32[]{:S(2)}) %all-to-all-start.3) | async-done | bytes 786464 | tf_op jit(solution)/shard_map/all_to_all | solution.py:33
  92.1 3.5 %shard_map.70 = bf16[256,1536]{1,0:T(8,128)(2,1)} custom-call(bf16[256,1536]{1,0:T(8,128)(2,1)S(1)} %bitcast.15, bf16[1536,384]{1,0:T(8,128)(2,1)} %w_mine.1, bf16[1536,384]{1,0:T(8,128)(2,1)} %collective-permute-done.refs_3_.refs_4_.w_other), custom_call_target="tpu_custom_call" | custom-call | flops 603979776 | bytes 3538944 | tf_op jit(solution)/shard_map/pallas_call | solution.py:164
  95.5 6.5 %all-to-all-start.4 = ((bf16[32,8,1536]{2,1,0:T(8,128)(2,1)}), bf16[32,8,1536]{2,1,0:T(8,128)(2,1)S(1)}, u32[]{:S(2)}, u32[]{:S(2)}) async-start(bf16[32,8,1536]{2,1,0:T(8,128)(2,1)} %bitcast.6), calls=%async_computation.4 | async-start | bytes 1572864 | tf_op jit(solution)/shard_map/all_to_all | solution.py:33
  102.1 0.1 fusion.24
  102.2 0.1 fusion.26
  102.3 1.9 %collective-permute-start.5 = (bf16[256,384]{1,0:T(8,128)(2,1)S(1)}, bf16[256,384]{1,0:T(8,128)(2,1)S(1)}, u32[]{:S(2)}, u32[]{:S(2)}) collective-permute-start(bf16[256,384]{1,0:T(8,128)(2,1)S(1)} %get-tuple-element.15), channel_id=1, source_target_pairs={{0,8},{8,0},{1,9},{9,1},{2,10},{10,2},{3,11},{11,3},{4,12},{12,4},... | collective-permute-start | bytes 589832 | tf_op jit(solution)/shard_map/ppermute | solution.py:42
  104.2 2.4 %collective-permute-start.6 = (bf16[256,384]{1,0:T(8,128)(2,1)S(1)}, bf16[256,384]{1,0:T(8,128)(2,1)S(1)}, u32[]{:S(2)}, u32[]{:S(2)}) collective-permute-start(bf16[256,384]{1,0:T(8,128)(2,1)S(1)} %get-tuple-element.14), channel_id=1, source_target_pairs={{0,8},{8,0},{1,9},{9,1},{2,10},{10,2},{3,11},{11,3},{4,12},{12,4},... | collective-permute-start | bytes 589832 | tf_op jit(solution)/shard_map/ppermute | solution.py:42
  106.6 0.0 collective-permute-done.4
  106.6 1.5 %fusion.25 = (bf16[256,1536]{1,0:T(8,128)(2,1)S(1)}, bf16[256,1536]{1,0:T(8,128)(2,1)S(1)}) fusion(bf16[256,3072]{1,0:T(8,128)(2,1)} %collective-permute-done.4), kind=kLoop, calls=%fused_computation.45 | loop fusion | bytes 3145728 | tf_op jit(solution)/shard_map/slice | solution.py:212
  108.1 0.0 collective-permute-done.6
  108.1 1.8 %fusion.1 = bf16[384,1536]{1,0:T(8,128)(2,1)} fusion(bf16[256,1536]{1,0:T(8,128)(2,1)S(1)} %get-tuple-element.9, bf16[256,1536]{1,0:T(8,128)(2,1)S(1)} %get-tuple-element.7, bf16[256,384]{1,0:T(8,128)(2,1)S(1)} %collective-permute-done.6, bf16[256,384]{1,0:T(8,128)(2,1)S(1)} %get-tuple-element.13), kind=kOutput, calls=%fused_computation.3 | convolution fusion | flops 609091584 | bytes 3145728 | tf_op jit(solution)/shard_map/dot_general | solution.py:29
  109.9 0.0 collective-permute-done.5
  109.9 2.0 %fusion = bf16[1536,384]{1,0:T(8,128)(2,1)} fusion(bf16[256,1536]{1,0:T(8,128)(2,1)S(1)} %get-tuple-element.10, bf16[256,1536]{1,0:T(8,128)(2,1)S(1)} %get-tuple-element.8, bf16[256,384]{1,0:T(8,128)(2,1)S(1)} %collective-permute-done.5, bf16[256,384]{1,0:T(8,128)(2,1)S(1)} %get-tuple-element.16), kind=kOutput, calls=%fused_computation.2 | convolution fusion | flops 609091584 | bytes 3145728 | tf_op jit(solution)/shard_map/dot_general | solution.py:29
  112.0 11.1 %all-to-all-done.4 = bf16[32,8,1536]{2,1,0:T(8,128)(2,1)S(1)} async-done(((bf16[32,8,1536]{2,1,0:T(8,128)(2,1)}), bf16[32,8,1536]{2,1,0:T(8,128)(2,1)S(1)}, u32[]{:S(2)}, u32[]{:S(2)}) %all-to-all-start.4) | async-done | bytes 786464 | tf_op jit(solution)/shard_map/all_to_all | solution.py:33
  123.0 0.7 reduce_sum.32
  (2 shorter events, 0.0 us)
Async XLA Ops:
  2.3 43.4 %all-to-all-start = ((bf16[16,8,3072]{2,1,0:T(8,128)(2,1)}), bf16[16,8,3072]{2,1,0:T(8,128)(2,1)S(1)}, u32[]{:S(2)}, u32[]{:S(2)}) async-start(bf16[16,8,3072]{2,1,0:T(8,128)(2,1)} %broadcast_in_dim.4), calls=%async_computation | async-start | bytes 1572864 | tf_op jit(solution)/shard_map/all_to_all | solution.py:33
  18.0 34.6 %collective-permute-start = (bf16[1536,384]{1,0:T(8,128)(2,1)}, bf16[1536,384]{1,0:T(8,128)(2,1)}, u32[]{:S(2)}, u32[]{:S(2)}) collective-permute-start(bf16[1536,384]{1,0:T(8,128)(2,1)} %w_mine.1), channel_id=1, source_target_pairs={{0,8},{8,0},{1,9},{9,1},{2,10},{10,2},{3,11},{11,3},{4,12},{12,4},... | collective-permute-start | bytes 3538952 | tf_op jit(solution)/shard_map/ppermute | solution.py:42
  20.0 32.6 %collective-permute-start.1 = (bf16[384,1536]{1,0:T(8,128)(2,1)}, bf16[384,1536]{1,0:T(8,128)(2,1)}, u32[]{:S(2)}, u32[]{:S(2)}) collective-permute-start(bf16[384,1536]{1,0:T(8,128)(2,1)} %w_out.1), channel_id=1, source_target_pairs={{0,8},{8,0},{1,9},{9,1},{2,10},{10,2},{3,11},{11,3},{4,12},{12,4},... | collective-permute-start | bytes 3538952 | tf_op jit(solution)/shard_map/ppermute | solution.py:42
  45.7 6.9 %copy-start = (bf16[16,8,3072]{2,1,0:T(8,128)(2,1)}, bf16[16,8,3072]{2,1,0:T(8,128)(2,1)S(1)}, u32[]{:S(2)}) copy-start(bf16[16,8,3072]{2,1,0:T(8,128)(2,1)S(1)} %all-to-all-done) | copy-start | bytes 2359300
  46.7 14.2 %collective-permute-start.2 = (bf16[64,3072]{1,0:T(8,128)(2,1)}, bf16[64,3072]{1,0:T(8,128)(2,1)S(1)}, u32[]{:S(2)}, u32[]{:S(2)}) collective-permute-start(bf16[64,3072]{1,0:T(8,128)(2,1)} %get-tuple-element.18), channel_id=1, source_target_pairs={{1,0},{2,1},{3,2},{4,3},{5,4},{6,5},{7,6},{0,7},{9,8},{10,9},{11,1... | collective-permute-start | bytes 1179656 | tf_op jit(solution)/shard_map/ppermute | solution.py:47
  49.4 12.3 %collective-permute-start.3 = (bf16[64,3072]{1,0:T(8,128)(2,1)}, bf16[64,3072]{1,0:T(8,128)(2,1)}, u32[]{:S(2)}, u32[]{:S(2)}) collective-permute-start(bf16[64,3072]{1,0:T(8,128)(2,1)} %get-tuple-element.17), channel_id=1, source_target_pairs={{7,0},{0,1},{1,2},{2,3},{3,4},{4,5},{5,6},{6,7},{15,8},{8,9},{9,10... | collective-permute-start | bytes 1179656 | tf_op jit(solution)/shard_map/ppermute | solution.py:47
  56.2 10.1 %all-to-all-start.1 = ((bf16[8,16,1536]{2,1,0:T(8,128)(2,1)}), bf16[8,16,1536]{2,1,0:T(8,128)(2,1)S(1)}, u32[]{:S(2)}, u32[]{:S(2)}) async-start(bf16[8,16,1536]{2,1,0:T(8,128)(2,1)} %bitcast.1), calls=%async_computation.1 | async-start | bytes 786432 | tf_op jit(solution)/shard_map/all_to_all | solution.py:33
  61.0 0.8 copy-start.2
  66.4 11.1 %all-to-all-start.2 = ((bf16[8,16,1536]{2,1,0:T(8,128)(2,1)}), bf16[8,16,1536]{2,1,0:T(8,128)(2,1)S(1)}, u32[]{:S(2)}, u32[]{:S(2)}) async-start(bf16[8,16,1536]{2,1,0:T(8,128)(2,1)} %bitcast.4), calls=%async_computation.2 | async-start | bytes 786432 | tf_op jit(solution)/shard_map/all_to_all | solution.py:33
  77.6 6.9 %copy-start.1 = (bf16[16,8,3072]{2,1,0:T(8,128)(2,1)S(1)}, bf16[16,8,3072]{2,1,0:T(8,128)(2,1)}, u32[]{:S(2)}) copy-start(bf16[16,8,3072]{2,1,0:T(8,128)(2,1)} %copy-done) | copy-start | bytes 2359300
  78.6 13.4 %all-to-all-start.3 = ((bf16[8,32,1536]{2,1,0:T(8,128)(2,1)}), bf16[8,32,1536]{2,1,0:T(8,128)(2,1)S(1)}, u32[]{:S(2)}, u32[]{:S(2)}) async-start(bf16[8,32,1536]{2,1,0:T(8,128)(2,1)} %broadcast_in_dim.5), calls=%async_computation.3 | async-start | bytes 1572864 | tf_op jit(solution)/shard_map/all_to_all | solution.py:33
  84.7 21.9 %collective-permute-start.4 = (bf16[256,3072]{1,0:T(8,128)(2,1)S(1)}, bf16[256,3072]{1,0:T(8,128)(2,1)}, u32[]{:S(2)}, u32[]{:S(2)}) collective-permute-start(bf16[256,3072]{1,0:T(8,128)(2,1)S(1)} %bitcast.19), channel_id=1, source_target_pairs={{0,8},{8,0},{1,9},{9,1},{2,10},{10,2},{3,11},{11,3},{4,12},{12,4},... | collective-permute-start | bytes 4718600 | tf_op jit(solution)/shard_map/ppermute | solution.py:42
  95.5 27.5 %all-to-all-start.4 = ((bf16[32,8,1536]{2,1,0:T(8,128)(2,1)}), bf16[32,8,1536]{2,1,0:T(8,128)(2,1)S(1)}, u32[]{:S(2)}, u32[]{:S(2)}) async-start(bf16[32,8,1536]{2,1,0:T(8,128)(2,1)} %bitcast.6), calls=%async_computation.4 | async-start | bytes 1572864 | tf_op jit(solution)/shard_map/all_to_all | solution.py:33
  102.3 7.7 %collective-permute-start.5 = (bf16[256,384]{1,0:T(8,128)(2,1)S(1)}, bf16[256,384]{1,0:T(8,128)(2,1)S(1)}, u32[]{:S(2)}, u32[]{:S(2)}) collective-permute-start(bf16[256,384]{1,0:T(8,128)(2,1)S(1)} %get-tuple-element.15), channel_id=1, source_target_pairs={{0,8},{8,0},{1,9},{9,1},{2,10},{10,2},{3,11},{11,3},{4,12},{12,4},... | collective-permute-start | bytes 589832 | tf_op jit(solution)/shard_map/ppermute | solution.py:42
  104.2 3.9 %collective-permute-start.6 = (bf16[256,384]{1,0:T(8,128)(2,1)S(1)}, bf16[256,384]{1,0:T(8,128)(2,1)S(1)}, u32[]{:S(2)}, u32[]{:S(2)}) collective-permute-start(bf16[256,384]{1,0:T(8,128)(2,1)S(1)} %get-tuple-element.14), channel_id=1, source_target_pairs={{0,8},{8,0},{1,9},{9,1},{2,10},{10,2},{3,11},{11,3},{4,12},{12,4},... | collective-permute-start | bytes 589832 | tf_op jit(solution)/shard_map/ppermute | solution.py:42

commit v7 on v6

--- a/solution.py
+++ b/solution.py
@@ -138,22 +138,21 @@
 
 
 def input_kernel(pair, w_mine, w_other, out, grad_hidden, mine, other, total, arrived, sent):
-    width, hidden = mine.shape
-    cut = width // 3
-    pieces = [pl.ds(i * cut, cut) for i in range(3)]
-    places = [(pair.at[:, 2 * hidden :], grad_hidden)]
-    for piece in pieces:
-        places += [(w_mine.at[piece], mine.at[piece]), (w_other.at[piece], other.at[piece])]
-    copies = start_all(places, arrived)
+    hidden = mine.shape[1]
+    half = pair.shape[0] // 2
+    copies = start_all(
+        [(pair.at[:, 2 * hidden :], grad_hidden), (w_mine, mine), (w_other, other)], arrived
+    )
     copies[0].wait()
+    copies[1].wait()
+    value = dot(grad_hidden[:, :hidden], mine[...], (1, 1))
+    copies[2].wait()
     results = []
-    for i, piece in enumerate(pieces):
-        copies[1 + 2 * i].wait()
-        value = dot(grad_hidden[:, :hidden], mine[piece, :], (1, 1))
-        copies[2 + 2 * i].wait()
-        value = value + dot(grad_hidden[:, hidden:], other[piece, :], (1, 1))
-        total[:, piece] = value.astype(total.dtype)
-        results.append(pltpu.make_async_copy(total.at[:, piece], out.at[:, piece], sent.at[i]))
+    for i in range(2):
+        rows = pl.ds(i * half, half)
+        part = value[i * half : (i + 1) * half] + dot(grad_hidden[rows, hidden:], other[...], (1, 1))
+        total[rows, :] = part.astype(total.dtype)
+        results.append(pltpu.make_async_copy(total.at[rows], out.at[rows], sent.at[i]))
         results[i].start()
     for result in results:
         result.wait()
@@ -171,8 +170,8 @@
             pltpu.VMEM((width, hidden), pair.dtype),
             pltpu.VMEM((width, hidden), pair.dtype),
             pltpu.VMEM((rows, width), pair.dtype),
-            pltpu.SemaphoreType.DMA((7,)),
             pltpu.SemaphoreType.DMA((3,)),
+            pltpu.SemaphoreType.DMA((2,)),
         ],
         compiler_params=PARAMS,
         cost_estimate=pl.CostEstimate(

time: 125 us -> 125 us (level)
  no operation moved by 1% of the time
where the time goes in v7:
time: 125 us; the launch traced here: 124 us
  starting transfers between devices  55 us (44%)
  waiting for transfers between devices  44.1 us (35%)
  Pallas kernels  12.3 us (10%)
  local copies, waits for them, and re-layouts  4.59 us (4%)
  matrix products  3.84 us (3%)
  other arithmetic  3.07 us (2%)
    all_to_all x5, waiting for transfers between devices, exchange(): return lax.all_to_all(blocks, axes, 0, 0, tiled=True)  43.4 us
    all_to_all x5, starting transfers between devices, exchange(): return lax.all_to_all(blocks, axes, 0, 0, tiled=True)  38.6 us
    ppermute x5, starting transfers between devices, swap(): return lax.ppermute(block, 'core', [(0, 1), (1, 0)])  10.6 us
    pallas_call x2, Pallas kernels, products(): pl.pallas_call(functools.partial(products_kernel, count), out_shape=jax.S...  7.15 us
    ppermute x2, starting transfers between devices, fetch(): return lax.ppermute(block, RING, [((i + by) % n, i) for i in range(n)])  5.83 us
    dot_general x2, matrix products, dot(): lax.dot_general(a, b, ((dims[:1], dims[1:]), ((), ())), preferred_element...  3.84 us
    pallas_call x1, Pallas kernels, input_products(): pl.pallas_call(input_kernel, out_shape=jax.ShapeDtypeStruct((rows, width)...  3.46 us
  transfers between devices with their start and end apart: 12, of which 6 were waited for; matrix products, arithmetic and copies ran while one was open for 6% of the time, Pallas kernels for 10%

profile of v7, /device:TPU:6, one launch (start us, length us, event | category | flops | bytes accessed | tf_op | source)
XLA Modules:
  0.0 123.8 jit_solution(12393663081512135821)
XLA Ops:
  0.6 0.8 pad_maximum_fusion.4
  1.4 1.0 broadcast_in_dim.4
  2.3 15.7 %all-to-all-start = ((bf16[16,8,3072]{2,1,0:T(8,128)(2,1)}), bf16[16,8,3072]{2,1,0:T(8,128)(2,1)S(1)}, u32[]{:S(2)}, u32[]{:S(2)}) async-start(bf16[16,8,3072]{2,1,0:T(8,128)(2,1)} %broadcast_in_dim.4), calls=%async_computation | async-start | bytes 1572864 | tf_op jit(solution)/shard_map/all_to_all | solution.py:33
  18.0 1.9 %collective-permute-start = (bf16[1536,384]{1,0:T(8,128)(2,1)}, bf16[1536,384]{1,0:T(8,128)(2,1)}, u32[]{:S(2)}, u32[]{:S(2)}) collective-permute-start(bf16[1536,384]{1,0:T(8,128)(2,1)} %w_mine.1), channel_id=1, source_target_pairs={{0,8},{8,0},{1,9},{9,1},{2,10},{10,2},{3,11},{11,3},{4,12},{12,4},... | collective-permute-start | bytes 3538952 | tf_op jit(solution)/shard_map/ppermute | solution.py:42
  20.0 2.4 %collective-permute-start.1 = (bf16[384,1536]{1,0:T(8,128)(2,1)}, bf16[384,1536]{1,0:T(8,128)(2,1)}, u32[]{:S(2)}, u32[]{:S(2)}) collective-permute-start(bf16[384,1536]{1,0:T(8,128)(2,1)} %w_out.1), channel_id=1, source_target_pairs={{0,8},{8,0},{1,9},{9,1},{2,10},{10,2},{3,11},{11,3},{4,12},{12,4},... | collective-permute-start | bytes 3538952 | tf_op jit(solution)/shard_map/ppermute | solution.py:42
  22.4 1.6 %shard_map.67 = (bf16[1536,384]{1,0:T(8,128)(2,1)S(1)}, bf16[384,1536]{1,0:T(8,128)(2,1)S(1)}) custom-call(bf16[1536,384]{1,0:T(8,128)(2,1)} %w_mine.1, bf16[384,1536]{1,0:T(8,128)(2,1)} %w_out.1), custom_call_target="tpu_custom_call" | custom-call | bytes 4718592 | tf_op jit(solution)/shard_map/pallas_call | solution.py:78
  24.0 21.7 %all-to-all-done = bf16[16,8,3072]{2,1,0:T(8,128)(2,1)S(1)} async-done(((bf16[16,8,3072]{2,1,0:T(8,128)(2,1)}), bf16[16,8,3072]{2,1,0:T(8,128)(2,1)S(1)}, u32[]{:S(2)}, u32[]{:S(2)}) %all-to-all-start) | async-done | bytes 786464 | tf_op jit(solution)/shard_map/all_to_all | solution.py:33
  45.7 0.0 copy-start
  45.7 1.0 slice_bitcast_fusion
  46.7 2.7 %collective-permute-start.2 = (bf16[64,3072]{1,0:T(8,128)(2,1)}, bf16[64,3072]{1,0:T(8,128)(2,1)S(1)}, u32[]{:S(2)}, u32[]{:S(2)}) collective-permute-start(bf16[64,3072]{1,0:T(8,128)(2,1)} %get-tuple-element.18), channel_id=1, source_target_pairs={{1,0},{2,1},{3,2},{4,3},{5,4},{6,5},{7,6},{0,7},{9,8},{10,9},{11,1... | collective-permute-start | bytes 1179656 | tf_op jit(solution)/shard_map/ppermute | solution.py:47
  49.4 3.1 %collective-permute-start.3 = (bf16[64,3072]{1,0:T(8,128)(2,1)}, bf16[64,3072]{1,0:T(8,128)(2,1)}, u32[]{:S(2)}, u32[]{:S(2)}) collective-permute-start(bf16[64,3072]{1,0:T(8,128)(2,1)} %get-tuple-element.17), channel_id=1, source_target_pairs={{7,0},{0,1},{1,2},{2,3},{3,4},{4,5},{5,6},{6,7},{15,8},{8,9},{9,10... | collective-permute-start | bytes 1179656 | tf_op jit(solution)/shard_map/ppermute | solution.py:47
  52.6 0.0 collective-permute-done.refs_3_.refs_4_.w_other
  52.6 0.0 collective-permute-done.1.refs_4_.refs_5_
  52.6 0.0 copy-done
  52.6 3.6 %shard_map.68 = bf16[128,1536]{1,0:T(8,128)(2,1)} custom-call(bf16[128,3072]{1,0:T(8,128)(2,1)} %bitcast.17, bf16[1536,384]{1,0:T(8,128)(2,1)S(1)} %get-tuple-element.5.refs_1_.refs_2_, bf16[384,1536]{1,0:T(8,128)(2,1)S(1)} %get-tuple-element.6.refs_2_.refs_3_, bf16[1536,384]{1,0:T(8,128)(2,1)} %collective-permute-done.refs_3_.refs_4_.w_other, ...), custom_call_target="tpu_custom_call" | custom-call | flops 15099494400 | bytes 4718592 | tf_op jit(solution)/shard_map/pallas_call | solution.py:120
  56.2 4.8 %all-to-all-start.1 = ((bf16[8,16,1536]{2,1,0:T(8,128)(2,1)}), bf16[8,16,1536]{2,1,0:T(8,128)(2,1)S(1)}, u32[]{:S(2)}, u32[]{:S(2)}) async-start(bf16[8,16,1536]{2,1,0:T(8,128)(2,1)} %bitcast.1), calls=%async_computation.1 | async-start | bytes 786432 | tf_op jit(solution)/shard_map/all_to_all | solution.py:33
  61.0 0.0 collective-permute-done.2.refs_0_
  61.0 0.0 copy-start.2
  61.0 0.7 collective-permute-done.3.refs_1_
  61.7 0.0 copy-done.2
  61.7 3.6 %shard_map.69 = bf16[128,1536]{1,0:T(8,128)(2,1)} custom-call(bf16[64,3072]{1,0:T(8,128)(2,1)} %copy-done.2, bf16[64,3072]{1,0:T(8,128)(2,1)} %collective-permute-done.3.refs_1_, bf16[1536,384]{1,0:T(8,128)(2,1)S(1)} %get-tuple-element.5.refs_1_.refs_2_, bf16[384,1536]{1,0:T(8,128)(2,1)S(1)} %get-tuple-element.6.refs_2_.refs_3_, ...), custom_call_target="tpu_custom_call" | custom-call | flops 15099494400 | bytes 4718592 | tf_op jit(solution)/shard_map/pallas_call | solution.py:120
  65.3 1.0 all-to-all-done.1
  66.4 5.8 %all-to-all-start.2 = ((bf16[8,16,1536]{2,1,0:T(8,128)(2,1)}), bf16[8,16,1536]{2,1,0:T(8,128)(2,1)S(1)}, u32[]{:S(2)}, u32[]{:S(2)}) async-start(bf16[8,16,1536]{2,1,0:T(8,128)(2,1)} %bitcast.4), calls=%async_computation.2 | async-start | bytes 786432 | tf_op jit(solution)/shard_map/all_to_all | solution.py:33
  72.1 1.2 pad_maximum_fusion.1
  73.3 0.1 convert_reduce_fusion.1
  73.3 4.2 %all-to-all-done.2 = bf16[8,16,1536]{2,1,0:T(8,128)(2,1)S(1)} async-done(((bf16[8,16,1536]{2,1,0:T(8,128)(2,1)}), bf16[8,16,1536]{2,1,0:T(8,128)(2,1)S(1)}, u32[]{:S(2)}, u32[]{:S(2)}) %all-to-all-start.2) | async-done | bytes 393248 | tf_op jit(solution)/shard_map/all_to_all | solution.py:33
  77.5 0.1 convert_reduce_fusion
  77.6 0.0 copy-start.1
  77.6 0.1 multiply_convert_fusion
  77.7 0.9 broadcast_in_dim.5
  78.6 5.9 %all-to-all-start.3 = ((bf16[8,32,1536]{2,1,0:T(8,128)(2,1)}), bf16[8,32,1536]{2,1,0:T(8,128)(2,1)S(1)}, u32[]{:S(2)}, u32[]{:S(2)}) async-start(bf16[8,32,1536]{2,1,0:T(8,128)(2,1)} %broadcast_in_dim.5), calls=%async_computation.3 | async-start | bytes 1572864 | tf_op jit(solution)/shard_map/all_to_all | solution.py:33
  84.5 0.0 copy-done.1
  84.5 0.1 bitcast_select_fusion.1
  84.6 0.1 pad_maximum_fusion
  84.7 1.9 %collective-permute-start.4 = (bf16[256,3072]{1,0:T(8,128)(2,1)S(1)}, bf16[256,3072]{1,0:T(8,128)(2,1)}, u32[]{:S(2)}, u32[]{:S(2)}) collective-permute-start(bf16[256,3072]{1,0:T(8,128)(2,1)S(1)} %bitcast.19), channel_id=1, source_target_pairs={{0,8},{8,0},{1,9},{9,1},{2,10},{10,2},{3,11},{11,3},{4,12},{12,4},... | collective-permute-start | bytes 4718600 | tf_op jit(solution)/shard_map/ppermute | solution.py:42
  86.6 5.4 %all-to-all-done.3 = bf16[8,32,1536]{2,1,0:T(8,128)(2,1)S(1)} async-done(((bf16[8,32,1536]{2,1,0:T(8,128)(2,1)}), bf16[8,32,1536]{2,1,0:T(8,128)(2,1)S(1)}, u32[]{:S(2)}, u32[]{:S(2)}) %all-to-all-start.3) | async-done | bytes 786464 | tf_op jit(solution)/shard_map/all_to_all | solution.py:33
  92.1 3.5 %shard_map.70 = bf16[256,1536]{1,0:T(8,128)(2,1)} custom-call(bf16[256,1536]{1,0:T(8,128)(2,1)S(1)} %bitcast.15, bf16[1536,384]{1,0:T(8,128)(2,1)} %w_mine.1, bf16[1536,384]{1,0:T(8,128)(2,1)} %collective-permute-done.refs_3_.refs_4_.w_other), custom_call_target="tpu_custom_call" | custom-call | flops 603979776 | bytes 3538944 | tf_op jit(solution)/shard_map/pallas_call | solution.py:163
  95.5 6.5 %all-to-all-start.4 = ((bf16[32,8,1536]{2,1,0:T(8,128)(2,1)}), bf16[32,8,1536]{2,1,0:T(8,128)(2,1)S(1)}, u32[]{:S(2)}, u32[]{:S(2)}) async-start(bf16[32,8,1536]{2,1,0:T(8,128)(2,1)} %bitcast.6), calls=%async_computation.4 | async-start | bytes 1572864 | tf_op jit(solution)/shard_map/all_to_all | solution.py:33
  102.1 0.1 fusion.24
  102.2 0.1 fusion.26
  102.3 1.9 %collective-permute-start.5 = (bf16[256,384]{1,0:T(8,128)(2,1)S(1)}, bf16[256,384]{1,0:T(8,128)(2,1)S(1)}, u32[]{:S(2)}, u32[]{:S(2)}) collective-permute-start(bf16[256,384]{1,0:T(8,128)(2,1)S(1)} %get-tuple-element.15), channel_id=1, source_target_pairs={{0,8},{8,0},{1,9},{9,1},{2,10},{10,2},{3,11},{11,3},{4,12},{12,4},... | collective-permute-start | bytes 589832 | tf_op jit(solution)/shard_map/ppermute | solution.py:42
  104.2 2.4 %collective-permute-start.6 = (bf16[256,384]{1,0:T(8,128)(2,1)S(1)}, bf16[256,384]{1,0:T(8,128)(2,1)S(1)}, u32[]{:S(2)}, u32[]{:S(2)}) collective-permute-start(bf16[256,384]{1,0:T(8,128)(2,1)S(1)} %get-tuple-element.14), channel_id=1, source_target_pairs={{0,8},{8,0},{1,9},{9,1},{2,10},{10,2},{3,11},{11,3},{4,12},{12,4},... | collective-permute-start | bytes 589832 | tf_op jit(solution)/shard_map/ppermute | solution.py:42
  106.6 0.0 collective-permute-done.4
  106.6 1.5 %fusion.25 = (bf16[256,1536]{1,0:T(8,128)(2,1)S(1)}, bf16[256,1536]{1,0:T(8,128)(2,1)S(1)}) fusion(bf16[256,3072]{1,0:T(8,128)(2,1)} %collective-permute-done.4), kind=kLoop, calls=%fused_computation.45 | loop fusion | bytes 3145728 | tf_op jit(solution)/shard_map/slice | solution.py:211
  108.1 0.0 collective-permute-done.6
  108.1 1.8 %fusion.1 = bf16[384,1536]{1,0:T(8,128)(2,1)} fusion(bf16[256,1536]{1,0:T(8,128)(2,1)S(1)} %get-tuple-element.9, bf16[256,1536]{1,0:T(8,128)(2,1)S(1)} %get-tuple-element.7, bf16[256,384]{1,0:T(8,128)(2,1)S(1)} %collective-permute-done.6, bf16[256,384]{1,0:T(8,128)(2,1)S(1)} %get-tuple-element.13), kind=kOutput, calls=%fused_computation.3 | convolution fusion | flops 609091584 | bytes 3145728 | tf_op jit(solution)/shard_map/dot_general | solution.py:29
  109.9 0.0 collective-permute-done.5
  109.9 2.0 %fusion = bf16[1536,384]{1,0:T(8,128)(2,1)} fusion(bf16[256,1536]{1,0:T(8,128)(2,1)S(1)} %get-tuple-element.10, bf16[256,1536]{1,0:T(8,128)(2,1)S(1)} %get-tuple-element.8, bf16[256,384]{1,0:T(8,128)(2,1)S(1)} %collective-permute-done.5, bf16[256,384]{1,0:T(8,128)(2,1)S(1)} %get-tuple-element.16), kind=kOutput, calls=%fused_computation.2 | convolution fusion | flops 609091584 | bytes 3145728 | tf_op jit(solution)/shard_map/dot_general | solution.py:29
  112.0 11.1 %all-to-all-done.4 = bf16[32,8,1536]{2,1,0:T(8,128)(2,1)S(1)} async-done(((bf16[32,8,1536]{2,1,0:T(8,128)(2,1)}), bf16[32,8,1536]{2,1,0:T(8,128)(2,1)S(1)}, u32[]{:S(2)}, u32[]{:S(2)}) %all-to-all-start.4) | async-done | bytes 786464 | tf_op jit(solution)/shard_map/all_to_all | solution.py:33
  123.0 0.7 reduce_sum.32
  (2 shorter events, 0.0 us)
Async XLA Ops:
  2.3 43.4 %all-to-all-start = ((bf16[16,8,3072]{2,1,0:T(8,128)(2,1)}), bf16[16,8,3072]{2,1,0:T(8,128)(2,1)S(1)}, u32[]{:S(2)}, u32[]{:S(2)}) async-start(bf16[16,8,3072]{2,1,0:T(8,128)(2,1)} %broadcast_in_dim.4), calls=%async_computation | async-start | bytes 1572864 | tf_op jit(solution)/shard_map/all_to_all | solution.py:33
  18.0 34.6 %collective-permute-start = (bf16[1536,384]{1,0:T(8,128)(2,1)}, bf16[1536,384]{1,0:T(8,128)(2,1)}, u32[]{:S(2)}, u32[]{:S(2)}) collective-permute-start(bf16[1536,384]{1,0:T(8,128)(2,1)} %w_mine.1), channel_id=1, source_target_pairs={{0,8},{8,0},{1,9},{9,1},{2,10},{10,2},{3,11},{11,3},{4,12},{12,4},... | collective-permute-start | bytes 3538952 | tf_op jit(solution)/shard_map/ppermute | solution.py:42
  20.0 32.6 %collective-permute-start.1 = (bf16[384,1536]{1,0:T(8,128)(2,1)}, bf16[384,1536]{1,0:T(8,128)(2,1)}, u32[]{:S(2)}, u32[]{:S(2)}) collective-permute-start(bf16[384,1536]{1,0:T(8,128)(2,1)} %w_out.1), channel_id=1, source_target_pairs={{0,8},{8,0},{1,9},{9,1},{2,10},{10,2},{3,11},{11,3},{4,12},{12,4},... | collective-permute-start | bytes 3538952 | tf_op jit(solution)/shard_map/ppermute | solution.py:42
  45.7 6.9 %copy-start = (bf16[16,8,3072]{2,1,0:T(8,128)(2,1)}, bf16[16,8,3072]{2,1,0:T(8,128)(2,1)S(1)}, u32[]{:S(2)}) copy-start(bf16[16,8,3072]{2,1,0:T(8,128)(2,1)S(1)} %all-to-all-done) | copy-start | bytes 2359300
  46.7 14.2 %collective-permute-start.2 = (bf16[64,3072]{1,0:T(8,128)(2,1)}, bf16[64,3072]{1,0:T(8,128)(2,1)S(1)}, u32[]{:S(2)}, u32[]{:S(2)}) collective-permute-start(bf16[64,3072]{1,0:T(8,128)(2,1)} %get-tuple-element.18), channel_id=1, source_target_pairs={{1,0},{2,1},{3,2},{4,3},{5,4},{6,5},{7,6},{0,7},{9,8},{10,9},{11,1... | collective-permute-start | bytes 1179656 | tf_op jit(solution)/shard_map/ppermute | solution.py:47
  49.4 12.3 %collective-permute-start.3 = (bf16[64,3072]{1,0:T(8,128)(2,1)}, bf16[64,3072]{1,0:T(8,128)(2,1)}, u32[]{:S(2)}, u32[]{:S(2)}) collective-permute-start(bf16[64,3072]{1,0:T(8,128)(2,1)} %get-tuple-element.17), channel_id=1, source_target_pairs={{7,0},{0,1},{1,2},{2,3},{3,4},{4,5},{5,6},{6,7},{15,8},{8,9},{9,10... | collective-permute-start | bytes 1179656 | tf_op jit(solution)/shard_map/ppermute | solution.py:47
  56.2 10.1 %all-to-all-start.1 = ((bf16[8,16,1536]{2,1,0:T(8,128)(2,1)}), bf16[8,16,1536]{2,1,0:T(8,128)(2,1)S(1)}, u32[]{:S(2)}, u32[]{:S(2)}) async-start(bf16[8,16,1536]{2,1,0:T(8,128)(2,1)} %bitcast.1), calls=%async_computation.1 | async-start | bytes 786432 | tf_op jit(solution)/shard_map/all_to_all | solution.py:33
  61.0 0.8 copy-start.2
  66.4 11.1 %all-to-all-start.2 = ((bf16[8,16,1536]{2,1,0:T(8,128)(2,1)}), bf16[8,16,1536]{2,1,0:T(8,128)(2,1)S(1)}, u32[]{:S(2)}, u32[]{:S(2)}) async-start(bf16[8,16,1536]{2,1,0:T(8,128)(2,1)} %bitcast.4), calls=%async_computation.2 | async-start | bytes 786432 | tf_op jit(solution)/shard_map/all_to_all | solution.py:33
  77.6 6.9 %copy-start.1 = (bf16[16,8,3072]{2,1,0:T(8,128)(2,1)S(1)}, bf16[16,8,3072]{2,1,0:T(8,128)(2,1)}, u32[]{:S(2)}) copy-start(bf16[16,8,3072]{2,1,0:T(8,128)(2,1)} %copy-done) | copy-start | bytes 2359300
  78.6 13.4 %all-to-all-start.3 = ((bf16[8,32,1536]{2,1,0:T(8,128)(2,1)}), bf16[8,32,1536]{2,1,0:T(8,128)(2,1)S(1)}, u32[]{:S(2)}, u32[]{:S(2)}) async-start(bf16[8,32,1536]{2,1,0:T(8,128)(2,1)} %broadcast_in_dim.5), calls=%async_computation.3 | async-start | bytes 1572864 | tf_op jit(solution)/shard_map/all_to_all | solution.py:33
  84.7 21.9 %collective-permute-start.4 = (bf16[256,3072]{1,0:T(8,128)(2,1)S(1)}, bf16[256,3072]{1,0:T(8,128)(2,1)}, u32[]{:S(2)}, u32[]{:S(2)}) collective-permute-start(bf16[256,3072]{1,0:T(8,128)(2,1)S(1)} %bitcast.19), channel_id=1, source_target_pairs={{0,8},{8,0},{1,9},{9,1},{2,10},{10,2},{3,11},{11,3},{4,12},{12,4},... | collective-permute-start | bytes 4718600 | tf_op jit(solution)/shard_map/ppermute | solution.py:42
  95.5 27.5 %all-to-all-start.4 = ((bf16[32,8,1536]{2,1,0:T(8,128)(2,1)}), bf16[32,8,1536]{2,1,0:T(8,128)(2,1)S(1)}, u32[]{:S(2)}, u32[]{:S(2)}) async-start(bf16[32,8,1536]{2,1,0:T(8,128)(2,1)} %bitcast.6), calls=%async_computation.4 | async-start | bytes 1572864 | tf_op jit(solution)/shard_map/all_to_all | solution.py:33
  102.3 7.7 %collective-permute-start.5 = (bf16[256,384]{1,0:T(8,128)(2,1)S(1)}, bf16[256,384]{1,0:T(8,128)(2,1)S(1)}, u32[]{:S(2)}, u32[]{:S(2)}) collective-permute-start(bf16[256,384]{1,0:T(8,128)(2,1)S(1)} %get-tuple-element.15), channel_id=1, source_target_pairs={{0,8},{8,0},{1,9},{9,1},{2,10},{10,2},{3,11},{11,3},{4,12},{12,4},... | collective-permute-start | bytes 589832 | tf_op jit(solution)/shard_map/ppermute | solution.py:42
  104.2 3.9 %collective-permute-start.6 = (bf16[256,384]{1,0:T(8,128)(2,1)S(1)}, bf16[256,384]{1,0:T(8,128)(2,1)S(1)}, u32[]{:S(2)}, u32[]{:S(2)}) collective-permute-start(bf16[256,384]{1,0:T(8,128)(2,1)S(1)} %get-tuple-element.14), channel_id=1, source_target_pairs={{0,8},{8,0},{1,9},{9,1},{2,10},{10,2},{3,11},{11,3},{4,12},{12,4},... | collective-permute-start | bytes 589832 | tf_op jit(solution)/shard_map/ppermute | solution.py:42

commit v8 on v6

--- a/solution.py
+++ b/solution.py
@@ -11,7 +11,7 @@
 coef = 0.7978845608
 ROWS = ("y_lo", "x")
 EVEN = ("y_far", "y_near", "z_hi", "z_mid")
-CHIPS = ("y_far", "y_near", "z_hi", "z_lo", "z_mid")
+CHIPS = ("y_far", "y_near", "z_lo", "z_hi", "z_mid")
 RING = ("z_hi", "z_mid", "z_lo")
 
 
@@ -146,16 +146,13 @@
         places += [(w_mine.at[piece], mine.at[piece]), (w_other.at[piece], other.at[piece])]
     copies = start_all(places, arrived)
     copies[0].wait()
-    results = []
     for i, piece in enumerate(pieces):
         copies[1 + 2 * i].wait()
         value = dot(grad_hidden[:, :hidden], mine[piece, :], (1, 1))
         copies[2 + 2 * i].wait()
         value = value + dot(grad_hidden[:, hidden:], other[piece, :], (1, 1))
-        total[:, piece] = value.astype(total.dtype)
-        results.append(pltpu.make_async_copy(total.at[:, piece], out.at[:, piece], sent.at[i]))
-        results[i].start()
-    for result in results:
+        total[..., piece] = value.astype(total.dtype).reshape(total.shape[:-1] + (cut,))
+    for result in start_all([(total.at[:, i, j], out.at[:, j, i]) for i in range(2) for j in range(2)], sent):
         result.wait()
 
 
@@ -163,16 +160,16 @@
     rows, (width, hidden) = pair.shape[0], w_in[0].shape
     return pl.pallas_call(
         input_kernel,
-        out_shape=jax.ShapeDtypeStruct((rows, width), pair.dtype),
+        out_shape=jax.ShapeDtypeStruct((4, 2, 2, rows // 16, width), pair.dtype),
         in_specs=[pl.BlockSpec(memory_space=pl.ANY)] + [HBM] * 2,
         out_specs=HBM,
         scratch_shapes=[
             pltpu.VMEM((rows, 2 * hidden), pair.dtype),
             pltpu.VMEM((width, hidden), pair.dtype),
             pltpu.VMEM((width, hidden), pair.dtype),
-            pltpu.VMEM((rows, width), pair.dtype),
+            pltpu.VMEM((4, 2, 2, rows // 16, width), pair.dtype),
             pltpu.SemaphoreType.DMA((7,)),
-            pltpu.SemaphoreType.DMA((3,)),
+            pltpu.SemaphoreType.DMA((4,)),
         ],
         compiler_params=PARAMS,
         cost_estimate=pl.CostEstimate(

time: 125 us -> 125 us (level)
  no operation moved by 1% of the time
where the time goes in v8:
time: 125 us; the launch traced here: 123 us
  starting transfers between devices  55 us (44%)
  waiting for transfers between devices  43.6 us (35%)
  Pallas kernels  12.4 us (10%)
  local copies, waits for them, and re-layouts  4.59 us (4%)
  matrix products  3.84 us (3%)
  other arithmetic  3.07 us (2%)
    all_to_all x5, waiting for transfers between devices, exchange(): return lax.all_to_all(blocks, axes, 0, 0, tiled=True)  42.8 us
    all_to_all x5, starting transfers between devices, exchange(): return lax.all_to_all(blocks, axes, 0, 0, tiled=True)  38.6 us
    ppermute x5, starting transfers between devices, swap(): return lax.ppermute(block, 'core', [(0, 1), (1, 0)])  10.6 us
    pallas_call x2, Pallas kernels, products(): pl.pallas_call(functools.partial(products_kernel, count), out_shape=jax.S...  7.15 us
    ppermute x2, starting transfers between devices, fetch(): return lax.ppermute(block, RING, [((i + by) % n, i) for i in range(n)])  5.83 us
    dot_general x2, matrix products, dot(): lax.dot_general(a, b, ((dims[:1], dims[1:]), ((), ())), preferred_element...  3.84 us
    pallas_call x1, Pallas kernels, input_products(): pl.pallas_call(input_kernel, out_shape=jax.ShapeDtypeStruct((4, 2, 2, row...  3.63 us
  transfers between devices with their start and end apart: 12, of which 6 were waited for; matrix products, arithmetic and copies ran while one was open for 6% of the time, Pallas kernels for 10%

profile of v8, /device:TPU:6, one launch (start us, length us, event | category | flops | bytes accessed | tf_op | source)
XLA Modules:
  0.0 123.4 jit_solution(857046433043564660)
XLA Ops:
  0.6 0.8 pad_maximum_fusion.4
  1.4 1.0 broadcast_in_dim.4
  2.3 15.7 %all-to-all-start = ((bf16[16,8,3072]{2,1,0:T(8,128)(2,1)}), bf16[16,8,3072]{2,1,0:T(8,128)(2,1)S(1)}, u32[]{:S(2)}, u32[]{:S(2)}) async-start(bf16[16,8,3072]{2,1,0:T(8,128)(2,1)} %broadcast_in_dim.4), calls=%async_computation | async-start | bytes 1572864 | tf_op jit(solution)/shard_map/all_to_all | solution.py:33
  18.0 1.9 %collective-permute-start = (bf16[1536,384]{1,0:T(8,128)(2,1)}, bf16[1536,384]{1,0:T(8,128)(2,1)}, u32[]{:S(2)}, u32[]{:S(2)}) collective-permute-start(bf16[1536,384]{1,0:T(8,128)(2,1)} %w_mine.1), channel_id=1, source_target_pairs={{0,8},{8,0},{1,9},{9,1},{2,10},{10,2},{3,11},{11,3},{4,12},{12,4},... | collective-permute-start | bytes 3538952 | tf_op jit(solution)/shard_map/ppermute | solution.py:42
  20.0 2.4 %collective-permute-start.1 = (bf16[384,1536]{1,0:T(8,128)(2,1)}, bf16[384,1536]{1,0:T(8,128)(2,1)}, u32[]{:S(2)}, u32[]{:S(2)}) collective-permute-start(bf16[384,1536]{1,0:T(8,128)(2,1)} %w_out.1), channel_id=1, source_target_pairs={{0,8},{8,0},{1,9},{9,1},{2,10},{10,2},{3,11},{11,3},{4,12},{12,4},... | collective-permute-start | bytes 3538952 | tf_op jit(solution)/shard_map/ppermute | solution.py:42
  22.4 1.6 %shard_map.67 = (bf16[1536,384]{1,0:T(8,128)(2,1)S(1)}, bf16[384,1536]{1,0:T(8,128)(2,1)S(1)}) custom-call(bf16[1536,384]{1,0:T(8,128)(2,1)} %w_mine.1, bf16[384,1536]{1,0:T(8,128)(2,1)} %w_out.1), custom_call_target="tpu_custom_call" | custom-call | bytes 4718592 | tf_op jit(solution)/shard_map/pallas_call | solution.py:78
  24.0 21.7 %all-to-all-done = bf16[16,8,3072]{2,1,0:T(8,128)(2,1)S(1)} async-done(((bf16[16,8,3072]{2,1,0:T(8,128)(2,1)}), bf16[16,8,3072]{2,1,0:T(8,128)(2,1)S(1)}, u32[]{:S(2)}, u32[]{:S(2)}) %all-to-all-start) | async-done | bytes 786464 | tf_op jit(solution)/shard_map/all_to_all | solution.py:33
  45.7 0.0 copy-start
  45.7 1.0 slice_bitcast_fusion
  46.7 2.7 %collective-permute-start.2 = (bf16[64,3072]{1,0:T(8,128)(2,1)}, bf16[64,3072]{1,0:T(8,128)(2,1)S(1)}, u32[]{:S(2)}, u32[]{:S(2)}) collective-permute-start(bf16[64,3072]{1,0:T(8,128)(2,1)} %get-tuple-element.18), channel_id=1, source_target_pairs={{1,0},{2,1},{3,2},{4,3},{5,4},{6,5},{7,6},{0,7},{9,8},{10,9},{11,1... | collective-permute-start | bytes 1179656 | tf_op jit(solution)/shard_map/ppermute | solution.py:47
  49.4 3.1 %collective-permute-start.3 = (bf16[64,3072]{1,0:T(8,128)(2,1)}, bf16[64,3072]{1,0:T(8,128)(2,1)}, u32[]{:S(2)}, u32[]{:S(2)}) collective-permute-start(bf16[64,3072]{1,0:T(8,128)(2,1)} %get-tuple-element.17), channel_id=1, source_target_pairs={{7,0},{0,1},{1,2},{2,3},{3,4},{4,5},{5,6},{6,7},{15,8},{8,9},{9,10... | collective-permute-start | bytes 1179656 | tf_op jit(solution)/shard_map/ppermute | solution.py:47
  52.6 0.0 collective-permute-done.refs_3_.refs_4_.w_other
  52.6 0.0 collective-permute-done.1.refs_4_.refs_5_
  52.6 0.0 copy-done
  52.6 3.6 %shard_map.68 = bf16[128,1536]{1,0:T(8,128)(2,1)} custom-call(bf16[128,3072]{1,0:T(8,128)(2,1)} %bitcast.17, bf16[1536,384]{1,0:T(8,128)(2,1)S(1)} %get-tuple-element.5.refs_1_.refs_2_, bf16[384,1536]{1,0:T(8,128)(2,1)S(1)} %get-tuple-element.6.refs_2_.refs_3_, bf16[1536,384]{1,0:T(8,128)(2,1)} %collective-permute-done.refs_3_.refs_4_.w_other, ...), custom_call_target="tpu_custom_call" | custom-call | flops 15099494400 | bytes 4718592 | tf_op jit(solution)/shard_map/pallas_call | solution.py:120
  56.2 4.8 %all-to-all-start.1 = ((bf16[8,16,1536]{2,1,0:T(8,128)(2,1)}), bf16[8,16,1536]{2,1,0:T(8,128)(2,1)S(1)}, u32[]{:S(2)}, u32[]{:S(2)}) async-start(bf16[8,16,1536]{2,1,0:T(8,128)(2,1)} %bitcast.1), calls=%async_computation.1 | async-start | bytes 786432 | tf_op jit(solution)/shard_map/all_to_all | solution.py:33
  61.0 0.0 collective-permute-done.2.refs_0_
  61.0 0.0 copy-start.2
  61.0 0.7 collective-permute-done.3.refs_1_
  61.7 0.0 copy-done.2
  61.7 3.6 %shard_map.69 = bf16[128,1536]{1,0:T(8,128)(2,1)} custom-call(bf16[64,3072]{1,0:T(8,128)(2,1)} %copy-done.2, bf16[64,3072]{1,0:T(8,128)(2,1)} %collective-permute-done.3.refs_1_, bf16[1536,384]{1,0:T(8,128)(2,1)S(1)} %get-tuple-element.5.refs_1_.refs_2_, bf16[384,1536]{1,0:T(8,128)(2,1)S(1)} %get-tuple-element.6.refs_2_.refs_3_, ...), custom_call_target="tpu_custom_call" | custom-call | flops 15099494400 | bytes 4718592 | tf_op jit(solution)/shard_map/pallas_call | solution.py:120
  65.3 1.0 all-to-all-done.1
  66.4 5.8 %all-to-all-start.2 = ((bf16[8,16,1536]{2,1,0:T(8,128)(2,1)}), bf16[8,16,1536]{2,1,0:T(8,128)(2,1)S(1)}, u32[]{:S(2)}, u32[]{:S(2)}) async-start(bf16[8,16,1536]{2,1,0:T(8,128)(2,1)} %bitcast.4), calls=%async_computation.2 | async-start | bytes 786432 | tf_op jit(solution)/shard_map/all_to_all | solution.py:33
  72.1 1.2 pad_maximum_fusion.1
  73.3 0.1 convert_reduce_fusion.1
  73.3 4.2 %all-to-all-done.2 = bf16[8,16,1536]{2,1,0:T(8,128)(2,1)S(1)} async-done(((bf16[8,16,1536]{2,1,0:T(8,128)(2,1)}), bf16[8,16,1536]{2,1,0:T(8,128)(2,1)S(1)}, u32[]{:S(2)}, u32[]{:S(2)}) %all-to-all-start.2) | async-done | bytes 393248 | tf_op jit(solution)/shard_map/all_to_all | solution.py:33
  77.5 0.1 convert_reduce_fusion
  77.6 0.0 copy-start.1
  77.6 0.1 multiply_convert_fusion
  77.7 0.9 broadcast_in_dim.5
  78.6 5.9 %all-to-all-start.3 = ((bf16[8,32,1536]{2,1,0:T(8,128)(2,1)}), bf16[8,32,1536]{2,1,0:T(8,128)(2,1)S(1)}, u32[]{:S(2)}, u32[]{:S(2)}) async-start(bf16[8,32,1536]{2,1,0:T(8,128)(2,1)} %broadcast_in_dim.5), calls=%async_computation.3 | async-start | bytes 1572864 | tf_op jit(solution)/shard_map/all_to_all | solution.py:33
  84.5 0.0 copy-done.1
  84.5 0.1 bitcast_select_fusion.1
  84.6 0.1 pad_maximum_fusion
  84.7 1.9 %collective-permute-start.4 = (bf16[256,3072]{1,0:T(8,128)(2,1)S(1)}, bf16[256,3072]{1,0:T(8,128)(2,1)}, u32[]{:S(2)}, u32[]{:S(2)}) collective-permute-start(bf16[256,3072]{1,0:T(8,128)(2,1)S(1)} %bitcast.19), channel_id=1, source_target_pairs={{0,8},{8,0},{1,9},{9,1},{2,10},{10,2},{3,11},{11,3},{4,12},{12,4},... | collective-permute-start | bytes 4718600 | tf_op jit(solution)/shard_map/ppermute | solution.py:42
  86.6 5.4 %all-to-all-done.3 = bf16[8,32,1536]{2,1,0:T(8,128)(2,1)S(1)} async-done(((bf16[8,32,1536]{2,1,0:T(8,128)(2,1)}), bf16[8,32,1536]{2,1,0:T(8,128)(2,1)S(1)}, u32[]{:S(2)}, u32[]{:S(2)}) %all-to-all-start.3) | async-done | bytes 786464 | tf_op jit(solution)/shard_map/all_to_all | solution.py:33
  92.1 3.6 %shard_map.70 = bf16[4,2,2,16,1536]{4,3,2,1,0:T(8,128)(2,1)} custom-call(bf16[256,1536]{1,0:T(8,128)(2,1)S(1)} %bitcast.15, bf16[1536,384]{1,0:T(8,128)(2,1)} %w_mine.1, bf16[1536,384]{1,0:T(8,128)(2,1)} %collective-permute-done.refs_3_.refs_4_.w_other), custom_call_target="tpu_custom_call" | custom-call | flops 603979776 | bytes 3538944 | tf_op jit(solution)/shard_map/pallas_call | solution.py:161
  95.7 6.5 %all-to-all-start.4 = ((bf16[32,8,1536]{2,1,0:T(8,128)(2,1)}), bf16[32,8,1536]{2,1,0:T(8,128)(2,1)S(1)}, u32[]{:S(2)}, u32[]{:S(2)}) async-start(bf16[32,8,1536]{2,1,0:T(8,128)(2,1)} %bitcast.6), calls=%async_computation.4 | async-start | bytes 1572864 | tf_op jit(solution)/shard_map/all_to_all | solution.py:33
  102.2 0.1 fusion.24
  102.3 0.1 fusion.26
  102.4 1.9 %collective-permute-start.5 = (bf16[256,384]{1,0:T(8,128)(2,1)S(1)}, bf16[256,384]{1,0:T(8,128)(2,1)S(1)}, u32[]{:S(2)}, u32[]{:S(2)}) collective-permute-start(bf16[256,384]{1,0:T(8,128)(2,1)S(1)} %get-tuple-element.15), channel_id=1, source_target_pairs={{0,8},{8,0},{1,9},{9,1},{2,10},{10,2},{3,11},{11,3},{4,12},{12,4},... | collective-permute-start | bytes 589832 | tf_op jit(solution)/shard_map/ppermute | solution.py:42
  104.4 2.4 %collective-permute-start.6 = (bf16[256,384]{1,0:T(8,128)(2,1)S(1)}, bf16[256,384]{1,0:T(8,128)(2,1)S(1)}, u32[]{:S(2)}, u32[]{:S(2)}) collective-permute-start(bf16[256,384]{1,0:T(8,128)(2,1)S(1)} %get-tuple-element.14), channel_id=1, source_target_pairs={{0,8},{8,0},{1,9},{9,1},{2,10},{10,2},{3,11},{11,3},{4,12},{12,4},... | collective-permute-start | bytes 589832 | tf_op jit(solution)/shard_map/ppermute | solution.py:42
  106.8 0.0 collective-permute-done.4
  106.8 1.5 %fusion.25 = (bf16[256,1536]{1,0:T(8,128)(2,1)S(1)}, bf16[256,1536]{1,0:T(8,128)(2,1)S(1)}) fusion(bf16[256,3072]{1,0:T(8,128)(2,1)} %collective-permute-done.4), kind=kLoop, calls=%fused_computation.45 | loop fusion | bytes 3145728 | tf_op jit(solution)/shard_map/slice | solution.py:209
  108.3 0.0 collective-permute-done.6
  108.3 1.8 %fusion.1 = bf16[384,1536]{1,0:T(8,128)(2,1)} fusion(bf16[256,1536]{1,0:T(8,128)(2,1)S(1)} %get-tuple-element.9, bf16[256,1536]{1,0:T(8,128)(2,1)S(1)} %get-tuple-element.7, bf16[256,384]{1,0:T(8,128)(2,1)S(1)} %collective-permute-done.6, bf16[256,384]{1,0:T(8,128)(2,1)S(1)} %get-tuple-element.13), kind=kOutput, calls=%fused_computation.3 | convolution fusion | flops 609091584 | bytes 3145728 | tf_op jit(solution)/shard_map/dot_general | solution.py:29
  110.1 0.0 collective-permute-done.5
  110.1 2.0 %fusion = bf16[1536,384]{1,0:T(8,128)(2,1)} fusion(bf16[256,1536]{1,0:T(8,128)(2,1)S(1)} %get-tuple-element.10, bf16[256,1536]{1,0:T(8,128)(2,1)S(1)} %get-tuple-element.8, bf16[256,384]{1,0:T(8,128)(2,1)S(1)} %collective-permute-done.5, bf16[256,384]{1,0:T(8,128)(2,1)S(1)} %get-tuple-element.16), kind=kOutput, calls=%fused_computation.2 | convolution fusion | flops 609091584 | bytes 3145728 | tf_op jit(solution)/shard_map/dot_general | solution.py:29
  112.1 10.5 %all-to-all-done.4 = bf16[32,8,1536]{2,1,0:T(8,128)(2,1)S(1)} async-done(((bf16[32,8,1536]{2,1,0:T(8,128)(2,1)}), bf16[32,8,1536]{2,1,0:T(8,128)(2,1)S(1)}, u32[]{:S(2)}, u32[]{:S(2)}) %all-to-all-start.4) | async-done | bytes 786464 | tf_op jit(solution)/shard_map/all_to_all | solution.py:33
  122.7 0.7 reduce_sum.32
  (2 shorter events, 0.0 us)
Async XLA Ops:
  2.3 43.4 %all-to-all-start = ((bf16[16,8,3072]{2,1,0:T(8,128)(2,1)}), bf16[16,8,3072]{2,1,0:T(8,128)(2,1)S(1)}, u32[]{:S(2)}, u32[]{:S(2)}) async-start(bf16[16,8,3072]{2,1,0:T(8,128)(2,1)} %broadcast_in_dim.4), calls=%async_computation | async-start | bytes 1572864 | tf_op jit(solution)/shard_map/all_to_all | solution.py:33
  18.0 34.6 %collective-permute-start = (bf16[1536,384]{1,0:T(8,128)(2,1)}, bf16[1536,384]{1,0:T(8,128)(2,1)}, u32[]{:S(2)}, u32[]{:S(2)}) collective-permute-start(bf16[1536,384]{1,0:T(8,128)(2,1)} %w_mine.1), channel_id=1, source_target_pairs={{0,8},{8,0},{1,9},{9,1},{2,10},{10,2},{3,11},{11,3},{4,12},{12,4},... | collective-permute-start | bytes 3538952 | tf_op jit(solution)/shard_map/ppermute | solution.py:42
  20.0 32.6 %collective-permute-start.1 = (bf16[384,1536]{1,0:T(8,128)(2,1)}, bf16[384,1536]{1,0:T(8,128)(2,1)}, u32[]{:S(2)}, u32[]{:S(2)}) collective-permute-start(bf16[384,1536]{1,0:T(8,128)(2,1)} %w_out.1), channel_id=1, source_target_pairs={{0,8},{8,0},{1,9},{9,1},{2,10},{10,2},{3,11},{11,3},{4,12},{12,4},... | collective-permute-start | bytes 3538952 | tf_op jit(solution)/shard_map/ppermute | solution.py:42
  45.7 6.9 %copy-start = (bf16[16,8,3072]{2,1,0:T(8,128)(2,1)}, bf16[16,8,3072]{2,1,0:T(8,128)(2,1)S(1)}, u32[]{:S(2)}) copy-start(bf16[16,8,3072]{2,1,0:T(8,128)(2,1)S(1)} %all-to-all-done) | copy-start | bytes 2359300
  46.7 14.2 %collective-permute-start.2 = (bf16[64,3072]{1,0:T(8,128)(2,1)}, bf16[64,3072]{1,0:T(8,128)(2,1)S(1)}, u32[]{:S(2)}, u32[]{:S(2)}) collective-permute-start(bf16[64,3072]{1,0:T(8,128)(2,1)} %get-tuple-element.18), channel_id=1, source_target_pairs={{1,0},{2,1},{3,2},{4,3},{5,4},{6,5},{7,6},{0,7},{9,8},{10,9},{11,1... | collective-permute-start | bytes 1179656 | tf_op jit(solution)/shard_map/ppermute | solution.py:47
  49.4 12.3 %collective-permute-start.3 = (bf16[64,3072]{1,0:T(8,128)(2,1)}, bf16[64,3072]{1,0:T(8,128)(2,1)}, u32[]{:S(2)}, u32[]{:S(2)}) collective-permute-start(bf16[64,3072]{1,0:T(8,128)(2,1)} %get-tuple-element.17), channel_id=1, source_target_pairs={{7,0},{0,1},{1,2},{2,3},{3,4},{4,5},{5,6},{6,7},{15,8},{8,9},{9,10... | collective-permute-start | bytes 1179656 | tf_op jit(solution)/shard_map/ppermute | solution.py:47
  56.2 10.1 %all-to-all-start.1 = ((bf16[8,16,1536]{2,1,0:T(8,128)(2,1)}), bf16[8,16,1536]{2,1,0:T(8,128)(2,1)S(1)}, u32[]{:S(2)}, u32[]{:S(2)}) async-start(bf16[8,16,1536]{2,1,0:T(8,128)(2,1)} %bitcast.1), calls=%async_computation.1 | async-start | bytes 786432 | tf_op jit(solution)/shard_map/all_to_all | solution.py:33
  61.0 0.8 copy-start.2
  66.4 11.1 %all-to-all-start.2 = ((bf16[8,16,1536]{2,1,0:T(8,128)(2,1)}), bf16[8,16,1536]{2,1,0:T(8,128)(2,1)S(1)}, u32[]{:S(2)}, u32[]{:S(2)}) async-start(bf16[8,16,1536]{2,1,0:T(8,128)(2,1)} %bitcast.4), calls=%async_computation.2 | async-start | bytes 786432 | tf_op jit(solution)/shard_map/all_to_all | solution.py:33
  77.6 6.9 %copy-start.1 = (bf16[16,8,3072]{2,1,0:T(8,128)(2,1)S(1)}, bf16[16,8,3072]{2,1,0:T(8,128)(2,1)}, u32[]{:S(2)}) copy-start(bf16[16,8,3072]{2,1,0:T(8,128)(2,1)} %copy-done) | copy-start | bytes 2359300
  78.6 13.4 %all-to-all-start.3 = ((bf16[8,32,1536]{2,1,0:T(8,128)(2,1)}), bf16[8,32,1536]{2,1,0:T(8,128)(2,1)S(1)}, u32[]{:S(2)}, u32[]{:S(2)}) async-start(bf16[8,32,1536]{2,1,0:T(8,128)(2,1)} %broadcast_in_dim.5), calls=%async_computation.3 | async-start | bytes 1572864 | tf_op jit(solution)/shard_map/all_to_all | solution.py:33
  84.7 22.1 %collective-permute-start.4 = (bf16[256,3072]{1,0:T(8,128)(2,1)S(1)}, bf16[256,3072]{1,0:T(8,128)(2,1)}, u32[]{:S(2)}, u32[]{:S(2)}) collective-permute-start(bf16[256,3072]{1,0:T(8,128)(2,1)S(1)} %bitcast.19), channel_id=1, source_target_pairs={{0,8},{8,0},{1,9},{9,1},{2,10},{10,2},{3,11},{11,3},{4,12},{12,4},... | collective-permute-start | bytes 4718600 | tf_op jit(solution)/shard_map/ppermute | solution.py:42
  95.7 27.0 %all-to-all-start.4 = ((bf16[32,8,1536]{2,1,0:T(8,128)(2,1)}), bf16[32,8,1536]{2,1,0:T(8,128)(2,1)S(1)}, u32[]{:S(2)}, u32[]{:S(2)}) async-start(bf16[32,8,1536]{2,1,0:T(8,128)(2,1)} %bitcast.6), calls=%async_computation.4 | async-start | bytes 1572864 | tf_op jit(solution)/shard_map/all_to_all | solution.py:33
  102.4 7.7 %collective-permute-start.5 = (bf16[256,384]{1,0:T(8,128)(2,1)S(1)}, bf16[256,384]{1,0:T(8,128)(2,1)S(1)}, u32[]{:S(2)}, u32[]{:S(2)}) collective-permute-start(bf16[256,384]{1,0:T(8,128)(2,1)S(1)} %get-tuple-element.15), channel_id=1, source_target_pairs={{0,8},{8,0},{1,9},{9,1},{2,10},{10,2},{3,11},{11,3},{4,12},{12,4},... | collective-permute-start | bytes 589832 | tf_op jit(solution)/shard_map/ppermute | solution.py:42
  104.4 3.9 %collective-permute-start.6 = (bf16[256,384]{1,0:T(8,128)(2,1)S(1)}, bf16[256,384]{1,0:T(8,128)(2,1)S(1)}, u32[]{:S(2)}, u32[]{:S(2)}) collective-permute-start(bf16[256,384]{1,0:T(8,128)(2,1)S(1)} %get-tuple-element.14), channel_id=1, source_target_pairs={{0,8},{8,0},{1,9},{9,1},{2,10},{10,2},{3,11},{11,3},{4,12},{12,4},... | collective-permute-start | bytes 589832 | tf_op jit(solution)/shard_map/ppermute | solution.py:42
